TPU v7x, 32 devices: a whole 2x2x4 slice. The times are simulated.
32 devices in a mesh: seq: 4 (over z), fsdp: 8 (over y, x, core).
Axes of the slice: x: 2, y: 2, z: 4, core: 2. Of those that a mesh axis runs over, the one named last changes fastest.
Arguments:
- tokens: bfloat16 [8, 1536, 2048], P('fsdp', 'seq'), may hold values from -6 to 6
- cotangent: bfloat16 [8, 1536, 2048], P('fsdp', 'seq'), may hold values from -6 to 6
- doc_lengths: int32 [8, 3], P('fsdp'), may hold values from 1 to 1534, as said below
- routes: int32 [8, 1536, 8], P('fsdp', 'seq'), may hold values from 0 to 15, all different within a row; in each aligned block of 384 rows (0 to 383, 384 to 767, ..., all dimensions but the last counted through in order) at most 256 rows name the same one
- attn_weight: bfloat16 [2048, 8192], P(('seq', 'fsdp'))
- router_weight: bfloat16 [2048, 16], P(('seq', 'fsdp')), may hold values from -0.0625 to 0.0625
- gain_values: bfloat16 [4352], P(('seq', 'fsdp')), may hold values from 0.5 to 1.5
- expert_weight: bfloat16 [16, 2048, 3072], P('fsdp', 'seq')
- attn_first: float32 [2048, 8192], P(('seq', 'fsdp'))
- attn_second: float32 [2048, 8192], P(('seq', 'fsdp'))
- router_first: float32 [2048, 16], P(('seq', 'fsdp'))
- router_second: float32 [2048, 16], P(('seq', 'fsdp'))
- gain_first: float32 [4352], P(('seq', 'fsdp'))
- gain_second: float32 [4352], P(('seq', 'fsdp'))
- expert_first: float32 [16, 2048, 3072], P('fsdp', 'seq')
- expert_second: float32 [16, 2048, 3072], P('fsdp', 'seq')
Outputs:
- layer_out: bfloat16 [8, 1536, 2048], P('fsdp', 'seq')
- input_grad: float32 [8, 1536, 2048], P('fsdp', 'seq')
- attn_moment: float32 [2048, 8192], P(('seq', 'fsdp'))
- attn_square: float32 [2048, 8192], P(('seq', 'fsdp'))
- attn_master: float32 [2048, 8192], P(('seq', 'fsdp'))
- router_moment: float32 [2048, 16], P(('seq', 'fsdp'))
- router_square: float32 [2048, 16], P(('seq', 'fsdp'))
- router_master: float32 [2048, 16], P(('seq', 'fsdp'))
- gain_moment: float32 [4352], P(('seq', 'fsdp'))
- gain_square: float32 [4352], P(('seq', 'fsdp'))
- gain_master: float32 [4352], P(('seq', 'fsdp'))
- expert_moment: float32 [16, 2048, 3072], P('fsdp', 'seq')
- expert_square: float32 [16, 2048, 3072], P('fsdp', 'seq')
- expert_master: float32 [16, 2048, 3072], P('fsdp', 'seq')
Inputs may be any that keep to these rules, and one draw needn't show every extreme that they name: `routes`: each token names 8 different experts; among the 384 tokens of one device (aligned blocks of a sequence) no expert is named more than 256 times, a bound that some block reaches. `doc_lengths`: the three lengths sum to 1536; the first and the last are at most 192; in some sequence both are 1.
All inputs are finite; a program needn't handle non-finite values.
Results may differ from a plain program's by a relative error of at most 0.02.
Values may be sent and summed in bfloat16 or wider, within the bound.
No kernel may reach another device: no remote copies, remote signals or barrier semaphores. Data moves between devices by JAX's collectives and lax.ppermute only.
A program may use at most 512 MiB of HBM per device.

v0:
```python
import jax
import jax.numpy as jnp
from jax import lax
from jax.sharding import PartitionSpec as P

HEADS = 16
HDIM = 128
FFE = 1024
TOP = 8
EXP_DEV = 2
STEP = 10


NORM_EPS = 1e-06
ROPE_BASE = 10000.0
BETA_ONE = 0.9
BETA_TWO = 0.95
ADAM_EPS = 1e-08
WEIGHT_DECAY = 0.1
RATE_ATTN = 0.1
RATE_ROUTER = 0.03
RATE_GAIN = 0.5
RATE_EXPERT = 0.1


def norm_rows(values, gain_vector):
    return (
        values
        * lax.rsqrt(jnp.mean(values * values, axis=-1, keepdims=True) + NORM_EPS)
        * gain_vector
    )


def rotate(values, positions):
    half_width = values.shape[-1] // 2
    frequency = ROPE_BASE ** (-jnp.arange(half_width, dtype=jnp.float32) / half_width)
    angles = positions[:, None] * frequency[None, :]
    cosine = jnp.cos(angles)[:, None, :]
    sine_part = jnp.sin(angles)[:, None, :]
    first_half = values[..., :half_width]
    second_half = values[..., half_width:]
    return jnp.concatenate(
        [
            first_half * cosine - second_half * sine_part,
            first_half * sine_part + second_half * cosine,
        ],
        axis=-1,
    )


def adam_step(weight, gradient, first_state, second, step_rate):
    first_new = BETA_ONE * first_state + (1.0 - BETA_ONE) * gradient
    second_new = BETA_TWO * second + (1.0 - BETA_TWO) * gradient * gradient
    first_hat = first_new / (1.0 - BETA_ONE**STEP)
    second_hat = second_new / (1.0 - BETA_TWO**STEP)
    master = weight.astype(jnp.float32) * (
        1.0 - step_rate * WEIGHT_DECAY
    ) - step_rate * first_hat / (jnp.sqrt(second_hat) + ADAM_EPS)
    return (first_new, second_new, master)


def contract_rows(left_side, right_side):
    return lax.dot_general(
        left_side, right_side, (((0,), (0,)), ((), ())), preferred_element_type=jnp.float32
    )


def contract_cols(left_side, right_side):
    return lax.dot_general(
        left_side, right_side, (((1,), (1,)), ((), ())), preferred_element_type=jnp.float32
    )


def body(
    tokens,
    cotangent,
    doc_lengths,
    routes,
    attn_weight,
    router_weight,
    gain_values,
    expert_weight,
    attn_first,
    attn_second,
    router_first,
    router_second,
    gain_first,
    gain_second,
    expert_first,
    expert_second,
):
    fsdp_count = lax.axis_size("fsdp")
    seq_count = lax.axis_size("seq")
    rows_here = tokens.shape[1]
    model_width = tokens.shape[2]
    head_count = HEADS
    head_width = HDIM
    feed_width = FFE
    expert_count = EXP_DEV * fsdp_count
    capacity = (rows_here * TOP // expert_count * 4 // 3 + 7) // 8 * 8
    length = rows_here * seq_count
    score_scale = head_width ** (-0.5)
    zero_low = jnp.zeros((), jnp.bfloat16)
    full_attn, full_router, full_gains = (
        lax.all_gather(attn_weight, ("seq", "fsdp"), axis=0, tiled=True),
        lax.all_gather(router_weight, ("seq", "fsdp"), axis=0, tiled=True),
        lax.all_gather(gain_values, ("seq", "fsdp"), axis=0, tiled=True),
    )
    full_experts = lax.all_gather(expert_weight, "seq", axis=1, tiled=True)
    gains_float = full_gains.astype(jnp.float32)
    attn_gain = gains_float[:model_width]
    ffn_gain = gains_float[model_width : 2 * model_width]
    query_gain = gains_float[2 * model_width : 2 * model_width + head_width]
    key_gain = gains_float[2 * model_width + head_width :]
    token_place = lax.axis_index("seq") * rows_here + jnp.arange(rows_here, dtype=jnp.int32)
    positions = token_place.astype(jnp.float32)
    key_place = jnp.arange(length, dtype=jnp.int32)
    bounds = doc_lengths[0]
    query_doc = (token_place >= bounds[0]).astype(jnp.int32) + (
        token_place >= bounds[0] + bounds[1]
    ).astype(jnp.int32)
    key_doc = (key_place >= bounds[0]).astype(jnp.int32) + (
        key_place >= bounds[0] + bounds[1]
    ).astype(jnp.int32)
    same_doc = query_doc[:, None] == key_doc[None, :]
    inputs = tokens[0].astype(jnp.float32)
    first_norm, norm_pull = jax.vjp(norm_rows, inputs, attn_gain)
    normed_low = first_norm.astype(jnp.bfloat16)
    project = jnp.dot(
        normed_low, full_attn[:, : 3 * model_width], preferred_element_type=jnp.float32
    )
    query_pre = project[:, :model_width].reshape(rows_here, head_count, head_width)
    key_pre = project[:, model_width : 2 * model_width].reshape(rows_here, head_count, head_width)
    value_low = project[:, 2 * model_width :].astype(jnp.bfloat16)

    def rotate_pair(query_in, key_in, query_scale, key_scale):
        return (
            rotate(norm_rows(query_in, query_scale), positions),
            rotate(norm_rows(key_in, key_scale), positions),
        )

    (query_rot, key_rot), rotate_pull = jax.vjp(
        rotate_pair, query_pre, key_pre, query_gain, key_gain
    )
    query_low = query_rot.astype(jnp.bfloat16)
    key_low = key_rot.reshape(rows_here, model_width).astype(jnp.bfloat16)
    all_keys, all_values = (
        lax.all_gather(key_low, "seq", axis=0, tiled=True),
        lax.all_gather(value_low, "seq", axis=0, tiled=True),
    )
    key_heads = all_keys.reshape(length, head_count, head_width)
    value_heads = all_values.reshape(length, head_count, head_width)

    def score_rows(query_in):
        raw_scores = (
            jnp.einsum("ihd,jhd->hij", query_in, key_heads, preferred_element_type=jnp.float32)
            * score_scale
        )
        return jnp.where(same_doc[None, :, :], raw_scores, -1e30)

    scores = score_rows(query_low)
    row_top = jnp.max(scores, axis=2, keepdims=True)
    exponent = jnp.exp(scores - row_top)
    row_total = jnp.sum(exponent, axis=2, keepdims=True)
    log_total = row_top + jnp.log(row_total)
    attend_low = (exponent / row_total).astype(jnp.bfloat16)
    attended = jnp.einsum(
        "hij,jhd->ihd", attend_low, value_heads, preferred_element_type=jnp.float32
    )
    attended_low = attended.reshape(rows_here, model_width).astype(jnp.bfloat16)
    branch = jnp.dot(
        attended_low, full_attn[:, 3 * model_width :], preferred_element_type=jnp.float32
    )
    middle = inputs + branch
    second_norm, second_pull = jax.vjp(norm_rows, middle, ffn_gain)
    normed_two = second_norm.astype(jnp.bfloat16)
    logits = jnp.dot(normed_two, full_router, preferred_element_type=jnp.float32)
    routed = routes[0]
    chosen = routed[:, :, None] == jnp.arange(expert_count, dtype=jnp.int32)[None, None, :]
    chosen_float = chosen.astype(jnp.float32)
    picked = jnp.sum(chosen_float * logits[:, None, :], axis=2)
    gate_weights = jax.nn.softmax(picked, axis=1)
    pair_hot = chosen.reshape(rows_here * TOP, expert_count).astype(jnp.int32)
    before = jnp.cumsum(pair_hot, axis=0) - pair_hot
    slot_index = jnp.sum(before * pair_hot, axis=1)
    target = routed.reshape(rows_here * TOP) * capacity + slot_index
    matches = target[None, :] == jnp.arange(expert_count * capacity, dtype=jnp.int32)[:, None]
    pair_ids = jnp.arange(rows_here * TOP, dtype=jnp.int32)
    source = jnp.sum(jnp.where(matches, pair_ids[None, :] + 1, 0), axis=1) - 1
    filled = source >= 0
    safe_source = jnp.maximum(source, 0)
    outgoing = jnp.where(filled[:, None], normed_two[safe_source // TOP], zero_low)
    outgoing = outgoing.reshape(fsdp_count, EXP_DEV, capacity, model_width)
    arrived = lax.all_to_all(outgoing, "fsdp", split_axis=0, concat_axis=2, tiled=True)
    expert_rows = arrived[0]
    gate_up = jnp.einsum(
        "jrd,jdf->jrf",
        expert_rows,
        full_experts[:, :, : 2 * feed_width],
        preferred_element_type=jnp.float32,
    )
    gate_in = gate_up[:, :, :feed_width]
    up_in = gate_up[:, :, feed_width:]
    silu_value = jax.nn.silu(gate_in)
    hidden_low = (silu_value * up_in).astype(jnp.bfloat16)
    produced = jnp.einsum(
        "jrf,jdf->jrd",
        hidden_low,
        full_experts[:, :, 2 * feed_width :],
        preferred_element_type=jnp.float32,
    ).astype(jnp.bfloat16)
    returned = lax.all_to_all(produced[None], "fsdp", split_axis=2, concat_axis=0, tiled=True)
    returned = returned.reshape(expert_count * capacity, model_width)
    picked_rows = returned[target].reshape(rows_here, TOP, model_width).astype(jnp.float32)
    mixture = jnp.sum(gate_weights[:, :, None] * picked_rows, axis=1)
    layer_out = (middle + mixture).astype(jnp.bfloat16)
    back_attn, back_router = (
        lax.all_gather(attn_weight, ("seq", "fsdp"), axis=0, tiled=True),
        lax.all_gather(router_weight, ("seq", "fsdp"), axis=0, tiled=True),
    )
    back_experts = lax.all_gather(expert_weight, "seq", axis=1, tiled=True)
    grad_out = cotangent[0].astype(jnp.float32)
    gate_grad = jnp.sum(grad_out[:, None, :] * picked_rows, axis=2)
    pick_grad = gate_weights * (
        gate_grad - jnp.sum(gate_weights * gate_grad, axis=1, keepdims=True)
    )
    logit_grad = jnp.sum(chosen_float * pick_grad[:, :, None], axis=1).astype(jnp.bfloat16)
    row_grad = (
        (gate_weights[:, :, None] * grad_out[:, None, :])
        .astype(jnp.bfloat16)
        .reshape(rows_here * TOP, model_width)
    )
    back_rows = jnp.where(filled[:, None], row_grad[safe_source], zero_low)
    back_rows = back_rows.reshape(fsdp_count, EXP_DEV, capacity, model_width)
    grad_rows = lax.all_to_all(back_rows, "fsdp", split_axis=0, concat_axis=2, tiled=True)[0]
    sigmoid_gate = jax.nn.sigmoid(gate_in)
    mid_grad = jnp.einsum(
        "jrd,jdf->jrf",
        grad_rows,
        back_experts[:, :, 2 * feed_width :],
        preferred_element_type=jnp.float32,
    )
    gate_in_grad = mid_grad * up_in * sigmoid_gate * (1.0 + gate_in * (1.0 - sigmoid_gate))
    up_in_grad = mid_grad * silu_value
    both_grad = jnp.concatenate([gate_in_grad, up_in_grad], axis=2).astype(jnp.bfloat16)
    expert_grad = jnp.concatenate(
        [
            jnp.einsum("jrd,jrf->jdf", expert_rows, both_grad, preferred_element_type=jnp.float32),
            jnp.einsum("jrd,jrf->jdf", grad_rows, hidden_low, preferred_element_type=jnp.float32),
        ],
        axis=2,
    )
    expert_share = lax.psum_scatter(
        expert_grad.astype(jnp.bfloat16), "seq", scatter_dimension=1, tiled=True
    ).astype(jnp.float32)
    row_input_grad = jnp.einsum(
        "jrf,jdf->jrd",
        both_grad,
        back_experts[:, :, : 2 * feed_width],
        preferred_element_type=jnp.float32,
    ).astype(jnp.bfloat16)
    came_back = lax.all_to_all(
        row_input_grad[None], "fsdp", split_axis=2, concat_axis=0, tiled=True
    )
    came_back = came_back.reshape(expert_count * capacity, model_width)
    normed_grad = jnp.sum(
        came_back[target].reshape(rows_here, TOP, model_width).astype(jnp.float32), axis=1
    )
    normed_grad = normed_grad + contract_cols(logit_grad, back_router)
    router_grad = contract_rows(normed_two, logit_grad)
    middle_norm_grad, ffn_gain_grad = second_pull(normed_grad)
    middle_grad = grad_out + middle_norm_grad
    branch_grad = middle_grad.astype(jnp.bfloat16)
    out_proj_grad = contract_rows(attended_low, branch_grad)
    attended_grad = contract_cols(branch_grad, back_attn[:, 3 * model_width :]).astype(jnp.bfloat16)
    attended_grad = attended_grad.reshape(rows_here, head_count, head_width)
    recomputed = jnp.exp(score_rows(query_low) - log_total)
    prob_grad = jnp.einsum(
        "ihd,jhd->hij", attended_grad, value_heads, preferred_element_type=jnp.float32
    )
    row_dot = jnp.sum(recomputed * prob_grad, axis=2, keepdims=True)
    score_grad = (recomputed * (prob_grad - row_dot)).astype(jnp.bfloat16)
    query_grad = (
        jnp.einsum("hij,jhd->ihd", score_grad, key_heads, preferred_element_type=jnp.float32)
        * score_scale
    ).astype(jnp.bfloat16)
    key_part_grad = (
        jnp.einsum("hij,ihd->jhd", score_grad, query_low, preferred_element_type=jnp.float32)
        * score_scale
    )
    value_part_grad = jnp.einsum(
        "hij,ihd->jhd",
        recomputed.astype(jnp.bfloat16),
        attended_grad,
        preferred_element_type=jnp.float32,
    )
    key_sum, value_sum = (
        lax.psum_scatter(
            key_part_grad.reshape(length, model_width).astype(jnp.bfloat16),
            "seq",
            scatter_dimension=0,
            tiled=True,
        ).astype(jnp.float32),
        lax.psum_scatter(
            value_part_grad.reshape(length, model_width).astype(jnp.bfloat16),
            "seq",
            scatter_dimension=0,
            tiled=True,
        ).astype(jnp.float32),
    )
    key_grad = (
        lax.optimization_barrier(key_sum.astype(jnp.bfloat16))
        .astype(jnp.float32)
        .reshape(rows_here, head_count, head_width)
    )
    query_grad_float = lax.optimization_barrier(query_grad).astype(jnp.float32)
    value_grad = value_sum.astype(jnp.bfloat16)
    query_pre_grad, key_pre_grad, query_gain_grad, key_gain_grad = rotate_pull(
        (query_grad_float, key_grad)
    )
    project_grad = jnp.concatenate(
        [
            query_pre_grad.reshape(rows_here, model_width).astype(jnp.bfloat16),
            key_pre_grad.reshape(rows_here, model_width).astype(jnp.bfloat16),
            value_grad,
        ],
        axis=1,
    )
    in_proj_grad = contract_rows(normed_low, project_grad)
    normed_one_grad = contract_cols(project_grad, back_attn[:, : 3 * model_width])
    input_norm_grad, attn_gain_grad = norm_pull(normed_one_grad)
    input_grad = middle_grad + input_norm_grad
    attn_grad = jnp.concatenate([in_proj_grad, out_proj_grad], axis=1)
    gain_grad = jnp.concatenate([attn_gain_grad, ffn_gain_grad, query_gain_grad, key_gain_grad])
    attn_share, router_share, gain_share = (
        lax.psum_scatter(attn_grad, ("seq", "fsdp"), scatter_dimension=0, tiled=True),
        lax.psum_scatter(router_grad, ("seq", "fsdp"), scatter_dimension=0, tiled=True),
        lax.psum_scatter(gain_grad, ("seq", "fsdp"), scatter_dimension=0, tiled=True),
    )
    attn_moment, attn_square, attn_master = adam_step(
        attn_weight, attn_share, attn_first, attn_second, RATE_ATTN
    )
    router_moment, router_square, router_master = adam_step(
        router_weight, router_share, router_first, router_second, RATE_ROUTER
    )
    gain_moment, gain_square, gain_master = adam_step(
        gain_values, gain_share, gain_first, gain_second, RATE_GAIN
    )
    expert_moment, expert_square, expert_master = adam_step(
        expert_weight, expert_share, expert_first, expert_second, RATE_EXPERT
    )
    return (
        layer_out[None],
        input_grad[None],
        attn_moment,
        attn_square,
        attn_master,
        router_moment,
        router_square,
        router_master,
        gain_moment,
        gain_square,
        gain_master,
        expert_moment,
        expert_square,
        expert_master,
    )


def solution(mesh):
    return jax.shard_map(
        body,
        mesh=mesh,
        in_specs=(
            P("fsdp", "seq", None),
            P("fsdp", "seq", None),
            P("fsdp", None),
            P("fsdp", "seq", None),
            P(("seq", "fsdp"), None),
            P(("seq", "fsdp"), None),
            P(("seq", "fsdp")),
            P("fsdp", "seq", None),
            P(("seq", "fsdp"), None),
            P(("seq", "fsdp"), None),
            P(("seq", "fsdp"), None),
            P(("seq", "fsdp"), None),
            P(("seq", "fsdp")),
            P(("seq", "fsdp")),
            P("fsdp", "seq", None),
            P("fsdp", "seq", None),
        ),
        out_specs=(
            P("fsdp", "seq", None),
            P("fsdp", "seq", None),
            P(("seq", "fsdp"), None),
            P(("seq", "fsdp"), None),
            P(("seq", "fsdp"), None),
            P(("seq", "fsdp"), None),
            P(("seq", "fsdp"), None),
            P(("seq", "fsdp"), None),
            P(("seq", "fsdp")),
            P(("seq", "fsdp")),
            P(("seq", "fsdp")),
            P("fsdp", "seq", None),
            P("fsdp", "seq", None),
            P("fsdp", "seq", None),
        ),
        check_vma=False,
    )
```

profile of v0, /device:TPU:0, one launch (start us, length us, event | category | flops | bytes accessed | tf_op | source)
XLA Modules:
  0.0 3155.3 jit_solution(12099464295060647210)
XLA Ops:
  8.8 44.2 %all-reduce.4 = bf16[4352]{0:T(1024)(128)(2,1)S(1)} all-reduce(bf16[4352]{0:T(1024)(128)(2,1)S(1)} %dynamic-update-slice), channel_id=1, replica_groups=mesh['seq'=4,'fsdp'=8] {'seq','fsdp'}, use_global_device_ids=true, to_apply=%add.4 | all-reduce | flops 4352 | bytes 17408
  56.3 153.2 %all-gather.6.cloned.1.call-done = bf16[2048,8192]{1,0:T(8,128)(2,1)} async-done(((bf16[64,8192]{1,0:T(8,128)(2,1)}), bf16[2048,8192]{1,0:T(8,128)(2,1)}) %all-gather.6.cloned.1.call-update) | async-done | bytes 33554448 | tf_op jit(solution)/shard_map/all_gather | solution.py:105
  290.1 40.2 %all-gather = bf16[32,64,16]{1,2,0:T(8,128)(2,1)S(1)} all-gather(bf16[1,64,16]{1,2,0:T(8,128)(2,1)S(1)} %bitcast.204), channel_id=1, replica_groups=mesh['seq'=4,'fsdp'=8] {'seq','fsdp'}, dimensions={0}, use_global_device_ids=true | all-gather | bytes 67584 | tf_op jit(solution)/shard_map/all_gather | solution.py:106
  335.9 34.5 %all-gather.10.cloned.1.call-done = bf16[1536,2048]{0,1:T(8,128)(2,1)} async-done(((bf16[384,2048]{0,1:T(8,128)(2,1)}), bf16[1536,2048]{0,1:T(8,128)(2,1)}) %all-gather.10.cloned.1.call-update) | async-done | bytes 6291472 | tf_op jit(solution)/shard_map/all_gather | solution.py:148
  407.0 79.2 %all-gather.8.cloned.1.call-done = bf16[1536,2048]{1,0:T(8,128)(2,1)} async-done(((bf16[384,2048]{1,0:T(8,128)(2,1)}), bf16[1536,2048]{1,0:T(8,128)(2,1)}) %all-gather.8.cloned.1.call-update) | async-done | bytes 6291472 | tf_op jit(solution)/shard_map/all_gather | solution.py:149
  545.4 37.6 %gather_fusion.2 = bf16[4096,2048]{1,0:T(8,128)(2,1)} fusion(bf16[3072,2048]{1,0:T(8,128)(2,1)} %fusion.4, s32[4096]{0:T(1024)S(1)} %get-tuple-element.157), kind=kCustom, calls=%fused_computation.2 | custom fusion | bytes 33570816 | tf_op jit(solution)/shard_map/gather | solution.py:233
  600.9 187.7 %all_to_all.60 = bf16[8,2,256,2048]{3,2,1,0:T(8,128)(2,1)} all-to-all(bf16[8,2,256,2048]{3,2,1,0:T(8,128)(2,1)S(1)} %get-tuple-element.166), channel_id=1, replica_groups=mesh['seq'=4,'fsdp'=8] {'fsdp'}, dimensions={0} | all-to-all | bytes 33554432 | tf_op jit(solution)/shard_map/all_to_all | solution.py:194
  808.6 169.7 %all-to-all-done.2 = bf16[8,2,256,2048]{3,2,1,0:T(8,128)(2,1)} async-done(((bf16[8,2,256,2048]{3,2,1,0:T(8,128)(2,1)}), bf16[8,2,256,2048]{3,2,1,0:T(8,128)(2,1)}, u32[]{:S(2)}, u32[]{:S(2)}) %all-to-all-start.2) | async-done | bytes 16777248 | tf_op jit(solution)/shard_map/all_to_all | solution.py:235
  992.6 43.0 %fusion.16 = f32[2,2048,2048]{1,2,0:T(8,128)} fusion(bf16[2,2048,2048]{2,1,0:T(8,128)(2,1)} %bitcast.180, bf16[2,2048,3072]{1,2,0:T(8,128)(2,1)} %all-gather.12.cloned.1.call-done), kind=kOutput, calls=%fused_computation.44 | convolution fusion | flops 34359738368 | bytes 67108864 | tf_op jit(solution)/shard_map/jrd,jdf->jrf/dot_general | solution.py:196
  1035.6 36.5 %multiply_convert_fusion.2 = (bf16[2,2048,1024]{1,2,0:T(8,128)(2,1)}, bf16[2,2048,1024]{1,2,0:T(8,128)(2,1)}, bf16[2,2048,1024]{1,2,0:T(8,128)(2,1)}) fusion(f32[2,2048,2048]{1,2,0:T(8,128)} %fusion.16, bf16[2,2048,2048]{2,1,0:T(8,128)(2,1)} %bitcast.182, bf16[2,2048,3072]{1,2,0:T(8,128)(2,1)} %all-gather.12.cloned.1.call-done), kind=kOutput, calls=%fused_computation.34 | convolution fusion | flops 17242783744 | bytes 83886080 | tf_op jit(solution)/shard_map/jrd,jdf->jrf/dot_general | solution.py:237
  1096.4 31.0 copy.309
  1133.5 42.4 %convert_bitcast_fusion = bf16[1,2,2048,2048]{3,2,1,0:T(8,128)(2,1)} fusion(bf16[2,2048,3072]{1,2,0:T(8,128)(2,1)} %all-gather.12.cloned.1.call-done, bf16[2,2048,1024]{1,2,0:T(8,128)(2,1)} %get-tuple-element.135, bf16[2,2048,1024]{1,2,0:T(8,128)(2,1)} %get-tuple-element.134), kind=kOutput, calls=%fused_computation.32 | convolution fusion | flops 34401681408 | bytes 50331648 | tf_op jit(solution)/shard_map/jrf,jdf->jrd/dot_general | solution.py:256
  1206.9 110.5 %all-to-all-done.1 = bf16[1,2,2048,2048]{3,1,0,2:T(2,128)(2,1)} async-done(((bf16[1,2,2048,2048]{3,1,0,2:T(2,128)(2,1)}), bf16[1,2,2048,2048]{3,1,0,2:T(2,128)(2,1)}, u32[]{:S(2)}, u32[]{:S(2)}) %all-to-all-start.1) | async-done | bytes 16777248 | tf_op jit(solution)/shard_map/all_to_all | solution.py:212
  1341.2 31.9 %gather_fusion.1 = bf16[3072,2048]{1,0:T(8,128)(2,1)} fusion(bf16[4096,2048]{1,0:T(8,128)(2,1)} %bitcast.172, s32[3072]{0:T(1024)S(1)} %broadcast_clamp_fusion.1), kind=kCustom, calls=%fused_computation.1 | custom fusion | bytes 25178112 | tf_op jit(solution)/shard_map/gather | solution.py:214
  1387.5 119.7 %all-to-all-done.3 = bf16[1,2,2048,2048]{3,1,0,2:T(2,128)(2,1)} async-done(((bf16[1,2,2048,2048]{3,1,0,2:T(2,128)(2,1)}), bf16[1,2,2048,2048]{3,1,0,2:T(2,128)(2,1)}, u32[]{:S(2)}, u32[]{:S(2)}) %all-to-all-start.3) | async-done | bytes 16777248 | tf_op jit(solution)/shard_map/all_to_all | solution.py:262
  1524.5 31.7 %gather_fusion.3 = bf16[3072,2048]{1,0:T(8,128)(2,1)} fusion(bf16[4096,2048]{1,0:T(8,128)(2,1)} %bitcast.171, s32[3072]{0:T(1024)S(1)} %broadcast_clamp_fusion.1), kind=kCustom, calls=%fused_computation.3 | custom fusion | bytes 25178112 | tf_op jit(solution)/shard_map/gather | solution.py:267
  1609.5 31.8 %multiply_convert_fusion = bf16[16,384,1536]{2,1,0:T(8,128)(2,1)} fusion(f32[16,384,1536]{2,1,0:T(8,128)} %get-tuple-element.177, f32[16,384,1536]{2,1,0:T(8,128)} %get-tuple-element.172, f32[16,384]{1,0:T(8,128)S(1)} %get-tuple-element.176, f32[16,384]{1,0:T(8,128)S(1)} %log_add_fusion), kind=kLoop, calls=%fused_computation.7 | loop fusion | flops 37748736 | bytes 94420992 | tf_op jit(solution)/shard_map/convert_element_type | solution.py:282
  1715.8 45.2 %fusion.21 = bf16[2,2048,2048]{1,2,0:T(8,128)(2,1)} fusion(bf16[2,2048,2048]{2,1,0:T(8,128)(2,1)} %bitcast.181, bf16[2,2048,1024]{1,2,0:T(8,128)(2,1)} %get-tuple-element.135, bf16[2,2048,1024]{1,2,0:T(8,128)(2,1)} %get-tuple-element.134), kind=kOutput, calls=%fused_computation.51 | convolution fusion | flops 34401681408 | bytes 50331648 | tf_op jit(solution)/shard_map/jrd,jrf->jdf/dot_general | solution.py:248
  1845.1 38.9 %reduce-scatter.18.cloned.1.call-done = bf16[384,2048]{1,0:T(8,128)(2,1)} async-done(((bf16[1536,2048]{1,0:T(8,128)(2,1)}), bf16[384,2048]{1,0:T(8,128)(2,1)}) %reduce-scatter.18.cloned.1.call-update) | async-done | bytes 1572880
  1909.1 43.6 %pad_maximum_fusion = f32[2048,8192]{1,0:T(8,128)} fusion(f32[2048,2048]{1,0:T(8,128)} %fusion.66, f32[2048,6144]{1,0:T(8,128)} %fusion.60), kind=kLoop, calls=%fused_computation.4 | loop fusion | flops 16777216 | bytes 134217728 | tf_op jit(solution)/shard_map/concatenate | solution.py:333
  1978.0 44.1 %reduce-scatter.20.cloned.1.call-done = f32[64,16]{1,0:T(8,128)} async-done(((f32[2048,16]{1,0:T(8,128)}), f32[64,16]{1,0:T(8,128)}) %reduce-scatter.20.cloned.1.call-update) | async-done | bytes 4112
  2045.0 44.9 %all-reduce.5 = f32[4352]{0:T(1024)S(1)} all-reduce(f32[4352]{0:T(1024)S(1)} %pad_maximum_fusion.16), channel_id=6, replica_groups=mesh['seq'=4,'fsdp'=8] {'seq','fsdp'}, use_global_device_ids=true, to_apply=%region_31.32.clone | all-reduce | flops 4352 | bytes 34816
  2095.4 340.5 %reduce-scatter.14.cloned.1.call-done = bf16[2,512,3072]{1,2,0:T(8,128)(2,1)} async-done(((bf16[2,2048,3072]{1,2,0:T(8,128)(2,1)}), bf16[2,512,3072]{1,2,0:T(8,128)(2,1)}) %reduce-scatter.14.cloned.1.call-update) | async-done | bytes 6291472 | tf_op jit(solution)/shard_map/reduce_scatter | solution.py:253
  2503.0 639.7 %reduce-scatter.12.cloned.1.call-done = f32[64,8192]{1,0:T(8,128)} async-done(((f32[2048,8192]{1,0:T(8,128)}), f32[64,8192]{1,0:T(8,128)}) %reduce-scatter.12.cloned.1.call-update) | async-done | bytes 2097168 | tf_op jit(solution)/shard_map/reduce_scatter | solution.py:336
  (311 shorter events, 717.0 us)
Async XLA Ops:
  7.2 202.3 %all-gather.6.cloned.1.call-start = ((), (), s32[]{:S(2)}) async-start(), calls=%async_computation.9 | async-start | bytes 34603008 | tf_op jit(solution)/shard_map/all_gather | solution.py:105
  7.9 362.5 %all-gather.10.cloned.1.call-start = ((), (), s32[]{:S(2)}) async-start(), calls=%async_computation.11 | async-start | bytes 7864320 | tf_op jit(solution)/shard_map/all_gather | solution.py:148
  54.9 190.8 %copy-start.69 = (f32[128]{0:T(128)}, f32[128]{0:T(128)S(1)}, u32[]{:S(2)}) copy-start(f32[128]{0:T(128)S(1)} %get-tuple-element.164) | copy-start | bytes 1540
  54.9 193.3 %copy-start.67 = (f32[128]{0:T(128)}, f32[128]{0:T(128)S(1)}, u32[]{:S(2)}) copy-start(f32[128]{0:T(128)S(1)} %get-tuple-element.163) | copy-start | bytes 1540
  54.9 154.6 %copy-start.31 = (f32[384]{0:T(512)}, f32[384]{0:T(512)S(1)}, u32[]{:S(2)}) copy-start(f32[384]{0:T(512)S(1)} %fusion.89) | copy-start | bytes 4612
  55.5 153.9 %copy-start.29 = (f32[2048]{0:T(1024)}, f32[2048]{0:T(1024)S(1)}, u32[]{:S(2)}) copy-start(f32[2048]{0:T(1024)S(1)} %get-tuple-element.162) | copy-start | bytes 24580
  56.3 192.8 %copy-start.21 = (f32[384,64]{1,0:T(8,128)}, f32[384,64]{1,0:T(8,128)S(1)}, u32[]{:S(2)}) copy-start(f32[384,64]{1,0:T(8,128)S(1)} %get-tuple-element.167) | copy-start | bytes 294916
  56.3 192.8 %copy-start.23 = (f32[384,64]{1,0:T(8,128)}, f32[384,64]{1,0:T(8,128)S(1)}, u32[]{:S(2)}) copy-start(f32[384,64]{1,0:T(8,128)S(1)} %get-tuple-element.168) | copy-start | bytes 294916
  251.4 119.0 %copy-start.11 = (bf16[384,16,64]{2,0,1:T(8,128)(2,1)}, bf16[384,16,64]{2,0,1:T(8,128)(2,1)S(1)}, u32[]{:S(2)}) copy-start(bf16[384,16,64]{2,0,1:T(8,128)(2,1)S(1)} %get-tuple-element.145) | copy-start | bytes 2359300
  251.4 119.0 %copy-start.13 = (bf16[384,16,64]{2,0,1:T(8,128)(2,1)}, bf16[384,16,64]{2,0,1:T(8,128)(2,1)S(1)}, u32[]{:S(2)}) copy-start(bf16[384,16,64]{2,0,1:T(8,128)(2,1)S(1)} %get-tuple-element.146) | copy-start | bytes 2359300
  256.2 230.1 %all-gather.8.cloned.1.call-start = ((), (), s32[]{:S(2)}) async-start(), calls=%async_computation.10 | async-start | bytes 7864320 | tf_op jit(solution)/shard_map/all_gather | solution.py:149
  259.5 733.1 %all-gather.12.cloned.1.call-start = ((), (), s32[]{:S(2)}) async-start(), calls=%async_computation.12 | async-start | bytes 31457280 | tf_op jit(solution)/shard_map/all_gather | solution.py:109
  330.5 184.5 %copy-start.33 = (bf16[2048,16]{0,1:T(8,128)(2,1)}, bf16[2048,16]{0,1:T(8,128)(2,1)S(1)}, u32[]{:S(2)}) copy-start(bf16[2048,16]{0,1:T(8,128)(2,1)S(1)} %reshape.583) | copy-start | bytes 196612
  788.6 189.7 %all-to-all-start.2 = ((bf16[8,2,256,2048]{3,2,1,0:T(8,128)(2,1)}), bf16[8,2,256,2048]{3,2,1,0:T(8,128)(2,1)}, u32[]{:S(2)}, u32[]{:S(2)}) async-start(bf16[8,2,256,2048]{3,2,1,0:T(8,128)(2,1)} %get-tuple-element.165), calls=%async_computation.2 | async-start | bytes 33554432 | tf_op jit(solution)/shard_map/all_to_all | solution.py:235
  1127.4 190.1 %all-to-all-start.1 = ((bf16[1,2,2048,2048]{3,1,0,2:T(2,128)(2,1)}), bf16[1,2,2048,2048]{3,1,0,2:T(2,128)(2,1)}, u32[]{:S(2)}, u32[]{:S(2)}) async-start(bf16[1,2,2048,2048]{3,1,0,2:T(2,128)(2,1)} %copy.309), calls=%async_computation.1 | async-start | bytes 33554432 | tf_op jit(solution)/shard_map/all_to_all | solution.py:212
  1317.5 189.7 %all-to-all-start.3 = ((bf16[1,2,2048,2048]{3,1,0,2:T(2,128)(2,1)}), bf16[1,2,2048,2048]{3,1,0,2:T(2,128)(2,1)}, u32[]{:S(2)}, u32[]{:S(2)}) async-start(bf16[1,2,2048,2048]{3,1,0,2:T(2,128)(2,1)} %copy.316), calls=%async_computation.3 | async-start | bytes 33554432 | tf_op jit(solution)/shard_map/all_to_all | solution.py:262
  1323.2 488.6 %reduce-scatter.16.cloned.1.call-start = ((), (), s32[]{:S(2)}) async-start(), calls=%async_computation.15 | async-start | bytes 7864320
  1387.4 179.7 %copy-start.48 = (bf16[384,16]{0,1:T(8,128)(2,1)}, bf16[384,16]{0,1:T(8,128)(2,1)S(1)}, u32[]{:S(2)}) copy-start(bf16[384,16]{0,1:T(8,128)(2,1)S(1)} %select_reduce_fusion.1) | copy-start | bytes 36868
  1663.2 220.7 %reduce-scatter.18.cloned.1.call-start = ((), (), s32[]{:S(2)}) async-start(), calls=%async_computation.16 | async-start | bytes 7864320
  1691.6 330.5 %reduce-scatter.20.cloned.1.call-start = ((), (), s32[]{:S(2)}) async-start(), calls=%async_computation.17 | async-start | bytes 1081344
  1762.8 673.2 %reduce-scatter.14.cloned.1.call-start = ((), (), s32[]{:S(2)}) async-start(), calls=%async_computation.14 | async-start | bytes 31457280 | tf_op jit(solution)/shard_map/reduce_scatter | solution.py:253
  1790.0 1352.7 %reduce-scatter.12.cloned.1.call-start = ((), (), s32[]{:S(2)}) async-start(), calls=%async_computation.13 | async-start | bytes 69206016 | tf_op jit(solution)/shard_map/reduce_scatter | solution.py:336
  2490.1 652.6 %copy-start.19 = (bf16[64,8192]{1,0:T(8,128)(2,1)S(1)}, bf16[64,8192]{1,0:T(8,128)(2,1)}, u32[]{:S(2)}) copy-start(bf16[64,8192]{1,0:T(8,128)(2,1)} %param.20) | copy-start | bytes 3145732
  2490.1 652.6 %copy-start.20 = (f32[64,8192]{1,0:T(8,128)S(1)}, f32[64,8192]{1,0:T(8,128)}, u32[]{:S(2)}) copy-start(f32[64,8192]{1,0:T(8,128)} %param.25) | copy-start | bytes 6291460
  (68 other events, 2127.7 us)
Sparse Core Ops, SparseCore 0:
  10.9 198.5 all-gather.5
  256.3 114.0 all-gather.9
  372.5 113.7 all-gather.7
  487.7 423.3 all-gather.11
  1663.3 107.0 reduce-scatter.15
  1772.6 111.2 reduce-scatter.17
  1886.7 135.2 reduce-scatter.19
  2024.6 411.3 reduce-scatter.13
  2438.3 704.3 reduce-scatter.11
where the time goes:
time: 3170 us; the launch traced here: 3160 us
  waiting for transfers between devices  1730 us (55%)
  matrix products  416 us (13%)
  local copies, waits for them, and re-layouts  390 us (12%)
  blocking collectives  317 us (10%)
  other arithmetic  267 us (8%)
    reduce_scatter x1, waiting for transfers between devices, body(): lax.psum_scatter(attn_grad, ('seq', 'fsdp'), scatter_dimension=0, tiled=T...  640 us
    reduce_scatter x1, waiting for transfers between devices, body(): lax.psum_scatter(expert_grad.astype(jnp.bfloat16), 'seq', scatter_dimensi...  341 us
    all_to_all x1, blocking collectives, body(): lax.all_to_all(outgoing, 'fsdp', split_axis=0, concat_axis=2, tiled=True)  188 us
    all_to_all x1, waiting for transfers between devices, body(): lax.all_to_all(back_rows, 'fsdp', split_axis=0, concat_axis=2, tiled=True)  170 us
    all_gather x1, waiting for transfers between devices, body(): lax.all_gather(attn_weight, ('seq', 'fsdp'), axis=0, tiled=True)  153 us
    unnamed x180, local copies, waits for them, and re-layouts  120 us
    all_to_all x1, waiting for transfers between devices, body(): lax.all_to_all(row_input_grad[None], 'fsdp', split_axis=2, concat_axis=0,...  120 us
    all_to_all x1, waiting for transfers between devices, body(): lax.all_to_all(produced[None], 'fsdp', split_axis=2, concat_axis=0, tiled...  111 us
  transfers between devices with their start and end apart: 12, of which 10 were waited for; matrix products, arithmetic and copies ran while one was open for 23% of the time, Pallas kernels for 0%

commit v1 on v0

v1 whole, which is shorter than its diff:
```python
import functools
import math

import jax
import jax.numpy as jnp
from jax import lax
from jax.experimental import pallas as pl
from jax.experimental.pallas import tpu as pltpu
from jax.sharding import PartitionSpec as P

HEADS = 16
HDIM = 128
FFE = 1024
TOP = 8
EXP_DEV = 2
STEP = 10

NORM_EPS = 1e-06
ROPE_BASE = 10000.0
BETA_ONE = 0.9
BETA_TWO = 0.95
ADAM_EPS = 1e-08
WEIGHT_DECAY = 0.1
RATE_ATTN = 0.1
RATE_ROUTER = 0.03
RATE_GAIN = 0.5
RATE_EXPERT = 0.1
VMEM_LIMIT = 56 * 1024 * 1024

BRIEF = pl.CostEstimate(flops=1000, bytes_accessed=1000, transcendentals=0)

F32 = jnp.float32
BF16 = jnp.bfloat16


def dot(a, b, ca, cb):
    return lax.dot_general(a, b, (((ca,), (cb,)), ((), ())), preferred_element_type=F32)


def adam_step(weight, gradient, first_state, second, step_rate):
    gradient = gradient.astype(F32)
    first_new = BETA_ONE * first_state + (1.0 - BETA_ONE) * gradient
    second_new = BETA_TWO * second + (1.0 - BETA_TWO) * gradient * gradient
    first_hat = first_new / (1.0 - BETA_ONE**STEP)
    second_hat = second_new / (1.0 - BETA_TWO**STEP)
    master = weight.astype(F32) * (1.0 - step_rate * WEIGHT_DECAY) - step_rate * first_hat / (
        jnp.sqrt(second_hat) + ADAM_EPS
    )
    return first_new, second_new, master


def swap(value, step, axis, count):
    return lax.ppermute(value, axis, [(i, i ^ step) for i in range(count)])


def gather_direct(value, axis, count):
    return jnp.stack([value] + [swap(value, k, axis, count) for k in range(1, count)])


def exchange(parts, axis, count):
    return [parts[0]] + [swap(parts[k], k, axis, count) for k in range(1, count)]


def reorder(stacked, index, axis=0):
    return jnp.take(stacked, index, axis=axis, mode="clip")


def plane_gather(count, value):
    if count != 8:
        whole = lax.all_gather(value, "fsdp")
        mine = lax.axis_index("fsdp")
        return [lax.dynamic_index_in_dim(whole, mine ^ k, 0, False) for k in range(count)]
    go = functools.partial(swap, axis="fsdp", count=count)
    half = value.shape[0] // 2
    by_x, by_y = go(value, 2), go(value, 4)
    far = jnp.concatenate([go(by_x[:half], 4), go(by_y[half:], 2)], axis=0)
    return [value, go(value, 1), by_x, go(by_x, 1), by_y, go(by_y, 1), far, go(far, 1)]


def scatter_first(count, value):
    return swap(value[1], 1, "fsdp", count) if count == 8 else None


def scatter_rest(count, value, got):
    if count != 8:
        mine = lax.axis_index("fsdp")
        stacked = value.transpose(1, 0, 2, 3).reshape(count, *value.shape[2:])
        stacked = reorder(stacked, mine ^ jnp.arange(count))
        return lax.psum_scatter(stacked, "fsdp", scatter_dimension=0).astype(F32)
    go = functools.partial(swap, axis="fsdp", count=count)
    total = value[0].astype(F32) + got.astype(F32)
    half = total.shape[1] // 2
    top, low = total[:, :half], total[:, half:]
    by_x = go(jnp.stack([top[3], top[1]]).astype(BF16), 2).astype(F32)
    by_y = go(jnp.stack([low[3], low[2]]).astype(BF16), 4).astype(F32)
    y_last = go((top[2] + by_x[0]).astype(BF16), 4).astype(F32)
    x_last = go((low[1] + by_y[0]).astype(BF16), 2).astype(F32)
    return jnp.concatenate([top[0] + by_x[1] + y_last, low[0] + by_y[1] + x_last], axis=0)


def plane_scatter(count, value):
    return scatter_rest(count, value, scatter_first(count, value))


def small_sum(value, shares, planes, seq_count, fsdp_count):
    step = 1
    while step < fsdp_count:
        value = value + swap(value, step, "fsdp", fsdp_count)
        step *= 2
    return sum(exchange([shares(value, planes[m]) for m in range(seq_count)], "seq", seq_count))


def to_plane(value, seq_count, fsdp_count):
    rows, width = value.shape
    members, chunk = fsdp_count // seq_count, rows // fsdp_count
    value = value.reshape(fsdp_count, chunk, width)
    value = lax.all_to_all(value, "fsdp", split_axis=0, concat_axis=0, tiled=True)
    value = value.reshape(seq_count, members * chunk, width)
    value = lax.all_to_all(value, "seq", split_axis=0, concat_axis=0, tiled=True)
    value = value.reshape(seq_count, members, chunk, width).transpose(1, 0, 2, 3)
    return value.reshape(rows, width)


def from_plane(value, here, plane, seq_count, fsdp_count):
    rows, width = value.shape
    members, chunk = fsdp_count // seq_count, rows // fsdp_count
    around, planes = here ^ jnp.arange(fsdp_count), plane ^ jnp.arange(seq_count)
    value = value.reshape(members, seq_count, chunk, width).transpose(1, 0, 2, 3)
    value = reorder(value.reshape(seq_count, members * chunk, width), planes)
    value = jnp.stack(exchange(list(value), "seq", seq_count))
    value = value.reshape(seq_count, members, chunk, width)
    value = reorder(value, planes).reshape(fsdp_count, chunk, width)
    value = jnp.stack(exchange(list(reorder(value, around)), "fsdp", fsdp_count))
    return reorder(value, around).reshape(rows, width)


def from_plane_whole(value, seq_count, fsdp_count):
    rows, width = value.shape
    members, chunk = fsdp_count // seq_count, rows // fsdp_count
    value = value.reshape(members, seq_count, chunk, width).transpose(1, 0, 2, 3)
    value = value.reshape(seq_count, members * chunk, width)
    value = lax.all_to_all(value, "seq", split_axis=0, concat_axis=0, tiled=True)
    value = value.reshape(fsdp_count, chunk, width)
    value = lax.all_to_all(value, "fsdp", split_axis=0, concat_axis=0, tiled=True)
    return value.reshape(rows, width)


def head_norm(value):
    return lax.rsqrt(jnp.mean(value * value, axis=-1, keepdims=True) + NORM_EPS)


def turn(value, cosine, sine):
    return value * cosine + pltpu.roll(value, HDIM // 2, 1) * sine


def project_kernel(
    heads, x_ref, gain_ref, w_ref, cos_ref, sin_ref, gq_ref, gk_ref, a_ref, q_ref, k_ref, v_ref, qp_ref, kp_ref
):
    x = x_ref[...].astype(F32)
    a = (x * head_norm(x) * gain_ref[...]).astype(BF16)
    a_ref[...] = a
    width = heads * HDIM
    cosine, sine = cos_ref[...], sin_ref[...]
    for n, (low_ref, pre_ref, g_ref) in enumerate(((q_ref, qp_ref, gq_ref), (k_ref, kp_ref, gk_ref))):
        part = dot(a, w_ref[:, n * width : (n + 1) * width], 1, 0)
        pre_ref[...] = part
        for h in range(heads):
            cols = slice(h * HDIM, (h + 1) * HDIM)
            one = part[:, cols]
            low_ref[:, cols] = turn(one * head_norm(one) * g_ref[...], cosine, sine).astype(BF16)
    v_ref[...] = dot(a, w_ref[:, 2 * width :], 1, 0).astype(BF16)


def project(x, gain, w, cosine, sine, gain_q, gain_k, block):
    rows, model = x.shape
    width = w.shape[1] // 3
    heads = width // HDIM

    def row(cols):
        return pl.BlockSpec((block, cols), lambda i: (i, 0))

    def whole(shape):
        return pl.BlockSpec(shape, lambda i: (0, 0))

    shape = jax.ShapeDtypeStruct
    return pl.pallas_call(
        functools.partial(project_kernel, heads),
        grid=(rows // block,),
        in_specs=[
            row(model),
            whole((1, model)),
            whole(w.shape),
            row(HDIM),
            row(HDIM),
            whole((1, HDIM)),
            whole((1, HDIM)),
        ],
        out_specs=[row(model), row(width), row(width), row(width), row(width), row(width)],
        out_shape=[
            shape((rows, model), BF16),
            shape((rows, width), BF16),
            shape((rows, width), BF16),
            shape((rows, width), BF16),
            shape((rows, width), F32),
            shape((rows, width), F32),
        ],
        compiler_params=pltpu.CompilerParams(vmem_limit_bytes=VMEM_LIMIT),
        cost_estimate=BRIEF,
        name="project",
    )(x, gain, w, cosine, sine, gain_q, gain_k)


SCORE = HDIM**-0.5


def probabilities(q, k, row_doc, col_doc):
    scores = dot(q, k, 1, 1) * (SCORE * math.log2(math.e))
    weight = jnp.where(row_doc == col_doc, jnp.exp2(scores), 0.0)
    return weight * (1.0 / jnp.sum(weight, axis=1, keepdims=True))


def attend_kernel(block, q_ref, k_ref, v_ref, rd_ref, cd_ref, o_ref):
    k, v = k_ref[0], v_ref[0]

    def step(i, _):
        rows = pl.ds(i * block, block)
        p = probabilities(q_ref[0, rows, :], k, rd_ref[0, rows, :], cd_ref[0])
        o_ref[0, rows, :] = dot(p.astype(BF16), v, 1, 0).astype(BF16)
        return 0

    lax.fori_loop(0, q_ref.shape[1] // block, step, 0)


def attend_back_kernel(block, q_ref, k_ref, v_ref, do_ref, rd_ref, cd_ref, dq_ref, dk_ref, dv_ref, sk_ref, sv_ref):
    k, v = k_ref[0], v_ref[0]
    sk_ref[...] = jnp.zeros_like(sk_ref)
    sv_ref[...] = jnp.zeros_like(sv_ref)

    def step(i, _):
        rows = pl.ds(i * block, block)
        q, do = q_ref[0, rows, :], do_ref[0, rows, :]
        p = probabilities(q, k, rd_ref[0, rows, :], cd_ref[0])
        dp = dot(do, v, 1, 1)
        ds = (p * (dp - jnp.sum(p * dp, axis=1, keepdims=True))).astype(BF16)
        dq_ref[0, rows, :] = (dot(ds, k, 1, 0) * SCORE).astype(BF16)
        sk_ref[...] += dot(ds, q, 0, 0)
        sv_ref[...] += dot(p.astype(BF16), do, 0, 0)
        return 0

    lax.fori_loop(0, q_ref.shape[1] // block, step, 0)
    dk_ref[0] = (sk_ref[...] * SCORE).astype(BF16)
    dv_ref[0] = sv_ref[...].astype(BF16)


def attention_specs(length, width):
    head = pl.BlockSpec((1, length, HDIM), lambda s, h: (s, 0, h))
    row_doc = pl.BlockSpec((1, length, 1), lambda s, h: (s, 0, 0))
    col_doc = pl.BlockSpec((1, 1, length), lambda s, h: (s, 0, 0))
    return head, row_doc, col_doc


def attend(q, k, v, row_doc, col_doc):
    seqs, length, width = q.shape
    head, rd, cd = attention_specs(length, width)
    pairs = seqs * (width // HDIM) * length * length
    return pl.pallas_call(
        functools.partial(attend_kernel, 256),
        grid=(seqs, width // HDIM),
        in_specs=[head, head, head, rd, cd],
        out_specs=head,
        out_shape=jax.ShapeDtypeStruct(q.shape, BF16),
        compiler_params=pltpu.CompilerParams(vmem_limit_bytes=VMEM_LIMIT),
        cost_estimate=BRIEF,
        name="attend",
    )(q, k, v, row_doc, col_doc)


def attend_back(q, k, v, do, row_doc, col_doc):
    seqs, length, width = q.shape
    head, rd, cd = attention_specs(length, width)
    pairs = seqs * (width // HDIM) * length * length
    out = jax.ShapeDtypeStruct(q.shape, BF16)
    return pl.pallas_call(
        functools.partial(attend_back_kernel, 256),
        grid=(seqs, width // HDIM),
        in_specs=[head, head, head, head, rd, cd],
        out_specs=[head, head, head],
        out_shape=[out, out, out],
        scratch_shapes=[pltpu.VMEM((length, HDIM), F32), pltpu.VMEM((length, HDIM), F32)],
        compiler_params=pltpu.CompilerParams(vmem_limit_bytes=VMEM_LIMIT),
        cost_estimate=BRIEF,
        name="attend_back",
    )(q, k, v, do, row_doc, col_doc)


def project_back_kernel(
    heads, dq_ref, dk_ref, dv_ref, qp_ref, kp_ref, cos_ref, sin_ref, gq_ref, gk_ref, w_ref, dp_ref, da_ref, dg_ref
):
    cosine, sine = cos_ref[...], -sin_ref[...]
    width = heads * HDIM

    @pl.when(pl.program_id(0) == 0)
    def _():
        dg_ref[...] = jnp.zeros_like(dg_ref)

    for n, (d_ref, pre_ref, g_ref) in enumerate(((dq_ref, qp_ref, gq_ref), (dk_ref, kp_ref, gk_ref))):
        gain = g_ref[...]
        total = jnp.zeros((1, HDIM), F32)
        for h in range(heads):
            cols = slice(h * HDIM, (h + 1) * HDIM)
            dn = turn(d_ref[:, cols].astype(F32), cosine, sine)
            pre = pre_ref[:, cols]
            scale = head_norm(pre)
            hat = pre * scale
            total += jnp.sum(dn * hat, axis=0, keepdims=True)
            inner = dn * gain
            back = scale * (inner - hat * jnp.mean(inner * hat, axis=1, keepdims=True))
            dp_ref[:, n * width + h * HDIM : n * width + (h + 1) * HDIM] = back.astype(BF16)
        dg_ref[n : n + 1, :] += total
    dp_ref[:, 2 * width :] = dv_ref[...]
    split_chunks(da_ref, slice(None), dot(dp_ref[...], w_ref[...], 1, 1))


def project_back(dq, dk, dv, q_pre, k_pre, cosine, sine, gain_q, gain_k, w, block):
    rows, width = dq.shape
    model = w.shape[0]
    form, result = chunk_form(rows // block, block, model)
    heads = width // HDIM

    def row(cols):
        return pl.BlockSpec((block, cols), lambda i: (i, 0))

    def whole(shape):
        return pl.BlockSpec(shape, lambda i: (0, 0))

    shape = jax.ShapeDtypeStruct
    return pl.pallas_call(
        functools.partial(project_back_kernel, heads),
        grid=(rows // block,),
        in_specs=[row(width)] * 5
        + [row(HDIM), row(HDIM), whole((1, HDIM)), whole((1, HDIM)), whole(w.shape)],
        out_specs=[row(3 * width), form, whole((8, HDIM))],
        out_shape=[shape((rows, 3 * width), BF16), result, shape((8, HDIM), F32)],
        compiler_params=pltpu.CompilerParams(vmem_limit_bytes=VMEM_LIMIT),
        cost_estimate=BRIEF,
        name="project_back",
    )(dq, dk, dv, q_pre, k_pre, cosine, sine, gain_q, gain_k, w)


def join_chunks(ref, cols):
    if len(ref.shape) == 2:
        return ref[:, cols]
    two, half, _, chunk, _ = ref.shape
    return jnp.concatenate([ref[k % 2, k // 2, 0, :, cols] for k in range(two * half)], axis=0)


def split_chunks(ref, cols, value):
    if len(ref.shape) == 2:
        ref[:, cols] = value.astype(BF16)
        return
    two, half, _, chunk, _ = ref.shape
    for k in range(two * half):
        ref[k % 2, k // 2, 0, :, cols] = value[k * chunk : (k + 1) * chunk].astype(BF16)


def chunk_form(blocks, rows, model):
    chunk = rows // blocks
    if chunk % 16:
        return pl.BlockSpec((rows, model), lambda i: (i, 0)), jax.ShapeDtypeStruct((blocks * rows, model), BF16)
    shape = (2, blocks // 2, blocks, chunk, model)
    spec = pl.BlockSpec((2, blocks // 2, 1, chunk, model), lambda i: (0, 0, i, 0, 0))
    return spec, jax.ShapeDtypeStruct(shape, BF16)


def by_owner(value, blocks):
    if value.ndim == 2:
        rows, model = value.shape[0] // blocks, value.shape[1]
        value = value.reshape(blocks, blocks // 2, 2, rows // blocks, model).transpose(2, 1, 0, 3, 4)
    return value.reshape(2, blocks // 2, -1, value.shape[-1])


def expert_kernel(wide, narrow, more, rank_ref, rank_col_ref, gate_ref, x_ref, dz_ref, w_ref, *refs):
    if more:
        old_out_ref, old_dx_ref, *refs = refs
    xg_ref, dy_ref, hm_ref, dgu_ref, out_ref, dx_ref, dgate_ref, dzg_ref, yg_ref, dxe_ref, sum_ref = refs
    rows, model = x_ref.shape
    capacity, feed = hm_ref.shape
    hit = rank_ref[0] == lax.broadcasted_iota(jnp.int32, (capacity, rows), 0)
    sel = hit.astype(F32).astype(BF16)
    sel_back = (rank_col_ref[0] == lax.broadcasted_iota(jnp.int32, (rows, capacity), 1)).astype(F32).astype(BF16)
    gate = jnp.sum(jnp.where(hit, gate_ref[0], 0.0), axis=1, keepdims=True)

    def dispatch(i, _):
        cols = pl.ds(pl.multiple_of(i * wide, wide), wide)
        xg_ref[:, cols] = dot(sel, x_ref[:, cols], 1, 0).astype(BF16)
        dz = dot(sel, dz_ref[:, cols], 1, 0)
        dzg_ref[:, cols] = dz.astype(BF16)
        dy_ref[:, cols] = (gate * dz).astype(BF16)
        return 0

    lax.fori_loop(0, model // wide, dispatch, 0)

    def inner(i, _):
        cols = pl.ds(pl.multiple_of(i * narrow, narrow), narrow)
        ups = pl.ds(pl.multiple_of(feed + i * narrow, narrow), narrow)
        downs = pl.ds(pl.multiple_of(2 * feed + i * narrow, narrow), narrow)
        g = dot(xg_ref[...], w_ref[:, cols], 1, 0)
        u = dot(xg_ref[...], w_ref[:, ups], 1, 0)
        dh = dot(dy_ref[...], w_ref[:, downs], 1, 0)
        sig = 1.0 / (1.0 + jnp.exp(-g))
        silu = g * sig
        hm_ref[:, cols] = (silu * u).astype(BF16)
        dgu_ref[:, cols] = (dh * u * (sig + silu * (1.0 - sig))).astype(BF16)
        dgu_ref[:, ups] = (dh * silu).astype(BF16)
        return 0

    lax.fori_loop(0, feed // narrow, inner, 0)
    sum_ref[...] = jnp.zeros_like(sum_ref)

    def outer(i, _):
        cols = pl.ds(pl.multiple_of(i * narrow, narrow), narrow)
        y = dot(hm_ref[...], w_ref[cols, 2 * feed :], 1, 1).astype(BF16).astype(F32)
        part = y * dzg_ref[:, cols].astype(F32)
        total = part[:, :128]
        for j in range(1, narrow // 128):
            total += part[:, j * 128 : (j + 1) * 128]
        sum_ref[...] += total
        yg_ref[:, cols] = (gate * y).astype(BF16)
        dxe_ref[:, cols] = dot(dgu_ref[...], w_ref[cols, : 2 * feed], 1, 1).astype(BF16)
        return 0

    lax.fori_loop(0, model // narrow, outer, 0)
    dgate_ref[0] = jnp.sum(jnp.where(hit, jnp.sum(sum_ref[...], axis=1, keepdims=True), 0.0), axis=0, keepdims=True)

    def combine(i, _):
        cols = pl.ds(pl.multiple_of(i * wide, wide), wide)
        out = dot(sel_back, yg_ref[:, cols], 1, 0)
        dx = dot(sel_back, dxe_ref[:, cols], 1, 0)
        if more:
            out += join_chunks(old_out_ref, cols).astype(F32)
            dx += join_chunks(old_dx_ref, cols).astype(F32)
        split_chunks(out_ref, cols, out)
        split_chunks(dx_ref, cols, dx)
        return 0

    lax.fori_loop(0, model // wide, combine, 0)


def run_expert(rank, gate, x, dz, w, old, capacity, wide=2048, narrow=1024):
    blocks, rows = rank.shape
    model, feed = x.shape[1], w.shape[1] // 3
    def per_block(r, c): return pl.BlockSpec((r, c), lambda i: (i, 0))
    line = pl.BlockSpec((1, 1, rows), lambda i: (i, 0, 0))
    shape = jax.ShapeDtypeStruct
    slots = blocks * capacity
    more = old is not None
    form, result = chunk_form(blocks, rows, model)
    return pl.pallas_call(
        functools.partial(expert_kernel, wide, narrow, more),
        grid=(blocks,),
        in_specs=[line, pl.BlockSpec((1, rows, 1), lambda i: (i, 0, 0)), line, per_block(rows, model), per_block(rows, model),
            pl.BlockSpec(w.shape, lambda i: (0, 0), pipeline_mode=pl.Buffered(1))] + [form] * (2 if more else 0),
        out_specs=[per_block(capacity, model), per_block(capacity, model), per_block(capacity, feed), per_block(capacity, 2 * feed), form, form, line],
        out_shape=[shape((slots, model), BF16), shape((slots, model), BF16), shape((slots, feed), BF16), shape((slots, 2 * feed), BF16),
            result, result, shape((blocks, 1, rows), F32)],
        scratch_shapes=[pltpu.VMEM((capacity, model), BF16)] * 3 + [pltpu.VMEM((capacity, 128), F32)],
        compiler_params=pltpu.CompilerParams(vmem_limit_bytes=VMEM_LIMIT),
        cost_estimate=BRIEF,
        name="expert",
    )(rank[:, None, :], rank[:, :, None], gate[:, None, :], x, dz, w, *(old or ()))


def weight_kernel(narrow, xg_ref, dy_ref, dgu_ref, hm_ref, out_ref, flip_ref):
    feed = hm_ref.shape[1]
    for src, other, base, width in ((xg_ref, dgu_ref, 0, 2 * feed), (dy_ref, hm_ref, 2 * feed, feed)):
        flip_ref[...] = src[...].T
        def step(i, _):
            cols = pl.ds(pl.multiple_of(i * narrow, narrow), narrow)
            to = pl.ds(pl.multiple_of(base + i * narrow, narrow), narrow)
            out_ref[:, to] = dot(flip_ref[...], other[:, cols], 1, 0).astype(BF16)
            return 0
        lax.fori_loop(0, width // narrow, step, 0)


def expert_weight_grad(xg, dy, dgu, hm, block=512, narrow=1024):
    slots, model = xg.shape
    feed = hm.shape[1]
    cut = pl.BlockSpec((slots, block), lambda i: (0, i))
    def whole(c): return pl.BlockSpec((slots, c), lambda i: (0, 0), pipeline_mode=pl.Buffered(1))
    return pl.pallas_call(
        functools.partial(weight_kernel, narrow),
        grid=(model // block,),
        in_specs=[cut, cut, whole(2 * feed), whole(feed)],
        out_specs=pl.BlockSpec((block, 3 * feed), lambda i: (i, 0)),
        out_shape=jax.ShapeDtypeStruct((model, 3 * feed), BF16),
        scratch_shapes=[pltpu.VMEM((block, slots), BF16)],
        compiler_params=pltpu.CompilerParams(vmem_limit_bytes=VMEM_LIMIT),
        cost_estimate=BRIEF,
        name="expert_weight_grad",
    )(xg, dy, dgu, hm)

def adam_kernel(rate, w_ref, g_ref, m_ref, v_ref, *refs):
    m_out, v_out, w_out = refs[-3:]
    new = adam_step(w_ref[0], g_ref[...], m_ref[0], v_ref[0], rate)
    m_out[0], v_out[0], w_out[0] = new

def adam_expert(e, weight, grad, first, second, old, rate, block=64):
    _, rows, cols = weight.shape
    one = pl.BlockSpec((1, block, cols), lambda i: (e, i, 0))
    out = jax.ShapeDtypeStruct(weight.shape, F32)
    old = tuple(old or ())
    return pl.pallas_call(
        functools.partial(adam_kernel, rate),
        grid=(rows // block,),
        in_specs=[one, pl.BlockSpec((block, cols), lambda i: (i, 0)), one, one] + [pl.BlockSpec(memory_space=pl.ANY)] * len(old),
        out_specs=[one] * 3,
        out_shape=[out] * 3,
        input_output_aliases={4 + i: i for i in range(len(old))},
        compiler_params=pltpu.CompilerParams(vmem_limit_bytes=VMEM_LIMIT),
        cost_estimate=BRIEF,
        name="adam_expert",
    )(weight, grad, first, second, *old)


def norm_back(dn, value, gain):
    scale = lax.rsqrt(jnp.mean(value * value, axis=-1, keepdims=True) + NORM_EPS)
    hat = value * scale
    inner = dn * gain
    back = scale * (inner - hat * jnp.mean(inner * hat, axis=-1, keepdims=True))
    return back, jnp.sum(dn * hat, axis=0)


def after(value, *others):
    return lax.optimization_barrier((value, *others))[0]


def body(
    tokens,
    cotangent,
    doc_lengths,
    routes,
    attn_weight,
    router_weight,
    gain_values,
    expert_weight,
    attn_first,
    attn_second,
    router_first,
    router_second,
    gain_first,
    gain_second,
    expert_first,
    expert_second,
):
    fsdp_count, seq_count = lax.axis_size("fsdp"), lax.axis_size("seq")
    everywhere = ("seq", "fsdp")
    here, plane = lax.axis_index("fsdp"), lax.axis_index("seq")
    around = here ^ jnp.arange(fsdp_count, dtype=jnp.int32)
    planes = plane ^ jnp.arange(seq_count, dtype=jnp.int32)
    rows, model = tokens.shape[1:]
    length = rows * seq_count
    experts = EXP_DEV * fsdp_count
    capacity = (rows * TOP // experts * 4 // 3 + 7) // 8 * 8
    width = model // fsdp_count
    shard = attn_weight.shape[0]
    members, chunk = fsdp_count // seq_count, rows // fsdp_count
    blocks = fsdp_count

    def blocked(parts):
        stacked = jnp.stack([part.reshape(blocks, chunk, -1) for part in parts], axis=1)
        return stacked.reshape(blocks * rows, -1)

    def pieces(value):
        cut = value.reshape(blocks, fsdp_count, chunk, -1)
        return [cut[:, k].reshape(rows, -1) for k in range(fsdp_count)]

    with jax.named_scope("gather_wo"):
        out_part = gather_direct(attn_weight[:, 3 * model :], "seq", seq_count)
    with jax.named_scope("remap_x"):
        x_low = to_plane(tokens[0], seq_count, fsdp_count)
    with jax.named_scope("gather_wqkv"):
        first_part = attn_weight[:, : 3 * model].reshape(shard, 3, fsdp_count, width).transpose(2, 0, 1, 3)
        first_part = reorder(first_part.reshape(fsdp_count, shard, 3 * width), around)
        first_part = reorder(jnp.stack(exchange(list(first_part), "fsdp", fsdp_count)), around)
        in_proj = lax.all_gather(first_part.reshape(fsdp_count * shard, 3 * width), "seq", axis=0, tiled=True)
    with jax.named_scope("gather_small"):
        flat = [router_weight.reshape(-1), gain_values, routes.reshape(-1), doc_lengths.reshape(-1)]
        sizes = [v.shape[0] for v in flat]
        starts = [sum(sizes[:i]) for i in range(len(sizes))]
        flat = after(jnp.concatenate([v.astype(F32) for v in flat]), x_low)
        flat = jnp.pad(flat, (0, -flat.shape[0] % 1024)).reshape(-1, 128)
        lines = flat.shape[0]
        small_all = lax.all_gather(flat, "seq", axis=0, tiled=True)
        small_all = lax.all_gather(small_all, "fsdp", axis=0, tiled=True)
        every = small_all.reshape(fsdp_count, seq_count, lines * 128)
        per_device = every.transpose(1, 0, 2).reshape(seq_count * fsdp_count, lines * 128)
        full_router = per_device[:, : sizes[0]].reshape(model, experts).astype(BF16)
        gains = per_device[:, starts[1] : starts[2]].reshape(-1)
        attn_gain, ffn_gain = gains[:model], gains[model : 2 * model]
        gain_q = gains[2 * model : 2 * model + HDIM][None]
        gain_k = gains[2 * model + HDIM : 2 * model + 2 * HDIM][None]
        meta = lax.dynamic_slice_in_dim(every, plane * members, members, 0)[:, :, starts[2] : starts[3] + 3]
        meta = meta.astype(jnp.int32)
    docs = meta[:, 0, rows * TOP : rows * TOP + 3]
    routes_all = meta[:, :, : rows * TOP].reshape(blocks, fsdp_count, chunk, TOP)
    routes_all = reorder(routes_all, around, 1).reshape(blocks, rows, TOP)
    positions = (
        jnp.arange(seq_count, dtype=jnp.int32)[:, None, None] * rows
        + around[None, :, None] * chunk
        + jnp.arange(chunk, dtype=jnp.int32)[None, None, :]
    ).reshape(1, length)
    doc_index = (positions >= docs[:, :1]).astype(jnp.int32) + (
        positions >= docs[:, :1] + docs[:, 1:2]
    ).astype(jnp.int32)
    row_doc, col_doc = doc_index[:, :, None], doc_index[:, None, :]
    frequency = ROPE_BASE ** (-jnp.arange(HDIM // 2, dtype=F32) / (HDIM // 2))
    angles = positions[0].astype(F32)[:, None] * frequency[None, :]
    cosine, sine = jnp.cos(angles), jnp.sin(angles)
    cosine = jnp.concatenate([cosine, cosine], axis=1)
    sine = jnp.concatenate([-sine, sine], axis=1)

    with jax.named_scope("gather_experts"):
        expert_later = after(expert_weight, first_part)
        expert_full = [lax.all_gather(expert_later[e], "seq", axis=0, tiled=True) for e in range(EXP_DEV)]
    with jax.named_scope("gather_wo"):
        out_part = jnp.stack(plane_gather(fsdp_count, out_part.reshape(seq_count * shard, model)))
        out_part = out_part.reshape(fsdp_count * seq_count, shard, model)
        place = jnp.arange(seq_count * fsdp_count, dtype=jnp.int32)
        place = (here ^ (place % fsdp_count)) * seq_count + (plane ^ (place // fsdp_count))
        out_proj = reorder(out_part, place).reshape(model, model)
    with jax.named_scope("gather_x"):
        x_all = blocked(plane_gather(fsdp_count, x_low))
    with jax.named_scope("remap_dz"):
        dz_low = to_plane(after(cotangent[0], x_all), seq_count, fsdp_count)

    own = here * EXP_DEV + jnp.arange(EXP_DEV, dtype=jnp.int32)
    named = jnp.any(routes_all[:, None, :, :] == own[None, :, None, None], axis=3)
    before = jnp.cumsum(named.astype(jnp.int32), axis=2) - named.astype(jnp.int32)
    rank = jnp.where(named, before, -1)
    chosen = jnp.any(
        routes_all[:, :, :, None] == jnp.arange(experts, dtype=jnp.int32)[None, None, None, :], axis=2
    )

    cosine_all, sine_all = jnp.tile(cosine, (members, 1)), jnp.tile(sine, (members, 1))
    a_all, q_low, k_low, v_low, q_pre, k_pre = project(
        x_all, attn_gain[None], in_proj, cosine_all, sine_all, gain_q, gain_k, rows
    )
    with jax.named_scope("gather_dz"):
        dz_all = blocked(plane_gather(fsdp_count, dz_low))
    seq_shape = (members, length, width)
    q_seq, k_seq, v_seq = (t.reshape(seq_shape) for t in (q_low, k_low, v_low))
    o_all = attend(q_seq, k_seq, v_seq, row_doc, col_doc)
    with jax.named_scope("o_exchange"):
        o_own = reorder(o_all.reshape(blocks, fsdp_count, chunk, width), around, 1)
        o_own = o_own.transpose(1, 0, 2, 3).reshape(fsdp_count, rows, width)
        o_own = lax.all_to_all(o_own, "fsdp", split_axis=0, concat_axis=0, tiled=True)
        o_own = o_own.transpose(1, 0, 2).reshape(rows, model)
    inputs = x_low.astype(F32)
    middle = inputs + dot(o_own, out_proj, 1, 0)
    middle_scale = lax.rsqrt(jnp.mean(middle * middle, axis=-1, keepdims=True) + NORM_EPS)
    normed = (middle * middle_scale * ffn_gain).astype(BF16)

    with jax.named_scope("gather_xn"):
        xn_all = blocked(plane_gather(fsdp_count, normed))
    with jax.named_scope("gates"):
        logits = dot(xn_all, full_router, 1, 0).reshape(blocks, rows, experts)
        top = jnp.max(jnp.where(chosen, logits, -jnp.inf), axis=2, keepdims=True)
        raised = jnp.where(chosen, jnp.exp(logits - top), 0.0)
        gates = raised / jnp.sum(raised, axis=2, keepdims=True)
        gates_mine = lax.dynamic_slice_in_dim(gates, here * EXP_DEV, EXP_DEV, axis=2)
    sums, gate_back, expert_share, held = None, [], [], None
    for e in range(EXP_DEV):
        with jax.named_scope(f"expert{e}"):
            w = expert_full[e] if held is None else after(expert_full[e], held)
            xg, dy, hm, dgu, mixed, dxn, dgate = run_expert(
                rank[:, e], gates_mine[:, :, e], xn_all, dz_all, w, sums, capacity
            )
            sums = (mixed, dxn)
            gate_back.append(dgate[:, 0])
            if e == EXP_DEV - 1:
                dxn = by_owner(dxn, blocks)
                dxn_first = scatter_first(fsdp_count, dxn)
                if dxn_first is not None:
                    xg = after(xg, dxn_first)
            held = expert_weight_grad(xg, dy, dgu, hm)
            expert_share.append(lax.psum_scatter(held, "seq", scatter_dimension=0, tiled=True))

    with jax.named_scope("router_back"):
        parts = exchange(pieces(jnp.stack(gate_back, axis=2)), "fsdp", fsdp_count)
        gate_grad = reorder(jnp.stack(parts, axis=1), around, 1).reshape(rows, experts)
        gates_own, chosen_own = pieces(gates)[0], pieces(chosen)[0]
        gate_grad = jnp.where(chosen_own, gate_grad, 0.0)
        dlog = (gates_own * (gate_grad - jnp.sum(gates_own * gate_grad, axis=1, keepdims=True))).astype(BF16)
    with jax.named_scope("scatter_dxn"):
        dxn_own = scatter_rest(fsdp_count, dxn, dxn_first)
    dxn_own = dxn_own + dot(dlog, full_router, 1, 1)
    middle_back, ffn_gain_grad = norm_back(dxn_own, middle, ffn_gain)
    middle_grad = dz_low.astype(F32) + middle_back
    db = middle_grad.astype(BF16)
    with jax.named_scope("do_exchange"):
        do_own = dot(db, out_proj, 1, 1).astype(BF16).reshape(rows, fsdp_count, width).transpose(1, 0, 2)
        do_own = lax.all_to_all(do_own, "fsdp", split_axis=0, concat_axis=0, tiled=True)
        do_all = reorder(do_own, around).reshape(fsdp_count, blocks, chunk, width).transpose(1, 0, 2, 3)
        do_all = do_all.reshape(seq_shape)
    do_all = after(do_all, held, expert_share[0])
    dq, dk, dv = (
        t.reshape(-1, width) for t in attend_back(q_seq, k_seq, v_seq, do_all, row_doc, col_doc)
    )
    with jax.named_scope("scatter_out"):
        mixture = plane_scatter(fsdp_count, by_owner(after(mixed, dq), blocks))
        layer_low = (middle + mixture).astype(BF16)
    d_proj, da_part, gain_qk = project_back(
        dq, dk, dv, q_pre, k_pre, cosine_all, sine_all, gain_q, gain_k, in_proj, rows
    )
    with jax.named_scope("remap_out"):
        layer_out = from_plane(layer_low, here, plane, seq_count, fsdp_count)
    with jax.named_scope("scatter_da"):
        da = plane_scatter(fsdp_count, by_owner(da_part, blocks))
    input_back, attn_gain_grad = norm_back(da, inputs, attn_gain)
    input_low = (middle_grad + input_back).astype(BF16)
    with jax.named_scope("scatter_wqkv"):
        in_grad = after(dot(a_all, d_proj, 0, 0).astype(BF16), expert_share[1], input_low)
        in_share = lax.psum_scatter(in_grad, "seq", scatter_dimension=0, tiled=True)
        in_share = reorder(in_share.reshape(fsdp_count, shard, 3 * width), around)
        in_share = reorder(jnp.stack(exchange(list(in_share), "fsdp", fsdp_count)), around)
        in_share = in_share.reshape(fsdp_count, shard, 3, width).transpose(1, 2, 0, 3).reshape(shard, 3 * model)
    with jax.named_scope("remap_grad"):
        input_grad = from_plane_whole(input_low, seq_count, fsdp_count).astype(F32)
    with jax.named_scope("scatter_wo"):
        out_grad = dot(o_own, db, 0, 0).astype(BF16).reshape(seq_count, fsdp_count, shard, model)
        pairs = reorder(around, jnp.arange(fsdp_count).reshape(-1, 2).T.reshape(-1))
        out_grad = reorder(out_grad, pairs, 1).transpose(1, 0, 2, 3)
        out_grad = out_grad.reshape(2, fsdp_count // 2, seq_count * shard, model)
        out_share = plane_scatter(fsdp_count, after(out_grad, da)).astype(BF16)
        out_share = reorder(out_share.reshape(seq_count, shard, model), planes)
        out_share = sum(p.astype(F32) for p in exchange(list(out_share), "seq", seq_count))
    with jax.named_scope("small_sum"):
        router_grad = dot(normed, dlog, 0, 0)
        small = jnp.concatenate(
            [router_grad.reshape(-1), attn_gain_grad, ffn_gain_grad, gain_qk[0], gain_qk[1]]
        )
        own_router, own_gain = shard * experts, gain_values.shape[0]

        def shares(value, p):
            device = p * fsdp_count + here
            return jnp.concatenate(
                [
                    lax.dynamic_slice_in_dim(value, device * own_router, own_router),
                    lax.dynamic_slice_in_dim(value, model * experts + device * own_gain, own_gain),
                ]
            )

        small = small_sum(small, shares, planes, seq_count, fsdp_count)
        router_share, gain_share = small[:own_router].reshape(shard, experts), small[own_router:]

    attn_share = jnp.concatenate([in_share.astype(F32), out_share], axis=1)
    attn_new = adam_step(attn_weight, attn_share, attn_first, attn_second, RATE_ATTN)
    router_new = adam_step(router_weight, router_share, router_first, router_second, RATE_ROUTER)
    gain_new = adam_step(gain_values, gain_share, gain_first, gain_second, RATE_GAIN)
    expert_new = None
    for e in range(EXP_DEV):
        expert_new = adam_expert(
            e, expert_weight, expert_share[e], expert_first, expert_second, expert_new, RATE_EXPERT
        )
    return (layer_out[None], input_grad[None], *attn_new, *router_new, *gain_new, *expert_new)


def solution(mesh):
    tokens = P("fsdp", "seq", None)
    matrix, vector = P(("seq", "fsdp"), None), P(("seq", "fsdp"))
    return jax.shard_map(
        body,
        mesh=mesh,
        in_specs=(
            tokens,
            tokens,
            P("fsdp", None),
            tokens,
            matrix,
            matrix,
            vector,
            tokens,
            matrix,
            matrix,
            matrix,
            matrix,
            vector,
            vector,
            tokens,
            tokens,
        ),
        out_specs=(
            tokens,
            tokens,
            matrix,
            matrix,
            matrix,
            matrix,
            matrix,
            matrix,
            vector,
            vector,
            vector,
            tokens,
            tokens,
            tokens,
        ),
        check_vma=False,
    )
```

time: 3170 us -> 1420 us (0.45)
  waiting for transfers between devices: 1730 us -> 354 us
  Pallas kernels: 0 us -> 395 us
  matrix products: 416 us -> 47.3 us
  blocking collectives: 317 us -> 64.7 us
  local copies, waits for them, and re-layouts: 390 us -> 231 us
  starting transfers between devices: 17.9 us -> 152 us
  other arithmetic: 267 us -> 144 us
    reduce_scatter x2 -> x3, waiting for transfers between devices: 980 us -> 0.01 us  [the longest x2 0.01 us: body(): lax.psum_scatter(held, 'seq', scatter_dimension=0, tiled=True)]
    pallas_call x0 -> x10, Pallas kernels: none -> 395 us  [the longest x2 173 us: run_expert(): pl.pallas_call(functools.partial(expert_kernel, wide, narrow, more), grid...]
    dot_general x20 -> x7, matrix products: 414 us -> 47.3 us  [dot(): lax.dot_general(a, b, (((ca,), (cb,)), ((), ())), preferred_element_type=...]
    all_to_all x3 -> x7, waiting for transfers between devices: 400 us -> 54.7 us  [the longest x2 33 us: to_plane(): lax.all_to_all(value, 'seq', split_axis=0, concat_axis=0, tiled=True)]
    ppermute x0 -> x95, waiting for transfers between devices: none -> 280 us  [swap(): return lax.ppermute(value, axis, [(i, i ^ step) for i in range(count)])]
    all_gather x4 -> x3, waiting for transfers between devices: 267 us -> 18.9 us  [the longest x2 18.9 us: body(): lax.all_gather(expert_later[e], 'seq', axis=0, tiled=True)]
    all_to_all x1, blocking collectives: 188 us -> 24.3 us  [body(): lax.all_to_all(do_own, 'fsdp', split_axis=0, concat_axis=0, tiled=True)]
    ppermute x0 -> x95, starting transfers between devices: none -> 105 us  [swap(): return lax.ppermute(value, axis, [(i, i ^ step) for i in range(count)])]
  transfers between devices with their start and end apart: 12 -> 108, of which waited for: 10 -> 35; matrix products, arithmetic and copies ran while one was open for 23% -> 28% of each run, Pallas kernels for 0% -> 28%
where the time goes in v1:
time: 1420 us; the launch traced here: 1410 us
  Pallas kernels  395 us (28%)
  waiting for transfers between devices  354 us (25%)
  local copies, waits for them, and re-layouts  231 us (16%)
  starting transfers between devices  152 us (11%)
  other arithmetic  144 us (10%)
  blocking collectives  64.7 us (5%)
  matrix products  47.3 us (3%)
  between operations  19.1 us (1%)
    ppermute x95, waiting for transfers between devices, swap(): return lax.ppermute(value, axis, [(i, i ^ step) for i in range(count)])  280 us
    pallas_call x2, Pallas kernels, run_expert(): pl.pallas_call(functools.partial(expert_kernel, wide, narrow, more), grid...  173 us
    ppermute x95, starting transfers between devices, swap(): return lax.ppermute(value, axis, [(i, i ^ step) for i in range(count)])  105 us
    pallas_call x2, Pallas kernels, expert_weight_grad(): pl.pallas_call(functools.partial(weight_kernel, narrow), grid=(model // b...  77.1 us
    unnamed x200, local copies, waits for them, and re-layouts  73.9 us
    add x4, other arithmetic, scatter_rest(): total = value[0].astype(F32) + got.astype(F32)  54.3 us
    dot_general x7, matrix products, dot(): lax.dot_general(a, b, (((ca,), (cb,)), ((), ())), preferred_element_type=...  47.3 us
    gather x17, local copies, waits for them, and re-layouts, reorder(): return jnp.take(stacked, index, axis=axis, mode='clip')  42.9 us
  transfers between devices with their start and end apart: 108, of which 35 were waited for; matrix products, arithmetic and copies ran while one was open for 28% of the time, Pallas kernels for 28%

profile of v1, /device:TPU:0, one launch (start us, length us, event | category | flops | bytes accessed | tf_op | source)
XLA Modules:
  0.0 1407.1 jit_solution(17512715618758937766)
XLA Ops:
  80.5 20.9 %all-to-all-start.1 = ((bf16[4,96,2048]{2,1,0:T(8,128)(2,1)}), bf16[4,96,2048]{2,1,0:T(8,128)(2,1)S(1)}, u32[]{:S(2)}, u32[]{:S(2)}) async-start(bf16[4,96,2048]{2,1,0:T(8,128)(2,1)} %bitcast.1), calls=%async_computation.1 | async-start | bytes 3145728 | tf_op jit(solution)/shard_map/remap_x/all_to_all | solution.py:119
  122.8 24.6 %all-to-all-done.1 = bf16[4,96,2048]{2,1,0:T(8,128)(2,1)S(1)} async-done(((bf16[4,96,2048]{2,1,0:T(8,128)(2,1)}), bf16[4,96,2048]{2,1,0:T(8,128)(2,1)S(1)}, u32[]{:S(2)}, u32[]{:S(2)}) %all-to-all-start.1) | async-done | bytes 1572896 | tf_op jit(solution)/shard_map/remap_x/all_to_all | solution.py:119
  152.1 23.2 %all_gather.15 = f32[160,128]{1,0:T(8,128)S(1)} all-gather(f32[40,128]{1,0:T(8,128)S(1)} %pad_bitcast_fusion), channel_id=1, replica_groups=mesh['seq'=4,'fsdp'=8] {'seq'}, dimensions={0}, use_global_device_ids=true | all-gather | bytes 102400 | tf_op jit(solution)/shard_map/gather_small/all_gather | solution.py:593
  175.2 17.2 %all_gather.16 = f32[1280,128]{1,0:T(8,128)S(1)} all-gather(f32[160,128]{1,0:T(8,128)S(1)} %all_gather.15), channel_id=1, replica_groups=mesh['seq'=4,'fsdp'=8] {'fsdp'}, dimensions={0}, use_global_device_ids=true | all-gather | bytes 737280 | tf_op jit(solution)/shard_map/gather_small/all_gather | solution.py:594
  233.5 20.9 %project.1 = (bf16[3072,2048]{1,0:T(8,128)(2,1)}, bf16[3072,256]{1,0:T(8,128)(2,1)}, bf16[3072,256]{1,0:T(8,128)(2,1)}, bf16[3072,256]{1,0:T(8,128)(2,1)}, f32[3072,256]{1,0:T(8,128)}, /*index=5*/f32[3072,256]{1,0:T(8,128)}) custom-call(bf16[3072,2048]{1,0:T(8,128)(2,1)} %bitcast.421, f32[1,2048]{1,0:T(1,128)} %bitcast.511, ...), custom_call_target="tpu_custom_call" | custom-call | flops 1000 | bytes 1000 | tf_op jit(solution)/shard_map/project/pallas_call | solution.py:186
  254.5 23.0 %attend.1 = bf16[2,1536,256]{2,1,0:T(8,128)(2,1)} custom-call(bf16[2,1536,256]{2,1,0:T(8,128)(2,1)} %bitcast.467, bf16[2,1536,256]{2,1,0:T(8,128)(2,1)} %bitcast.469, bf16[2,1536,256]{2,1,0:T(8,128)(2,1)} %bitcast.471, s32[2,1536,1]{2,1,0:T(8,128)} %convert_add_fusion.5.rd_ref, s32[2,1,1536]{2,1,0:T(1,128)} %fusion.61.cd_ref), custom_call_target="tpu_custom_call" | custom-call | flops 1000 | bytes 1000 | tf_op jit(solution)/shard_map/attend/pallas_call | solution.py:266
  345.9 17.5 %collective-permute-done.27 = bf16[384,2048]{1,0:T(8,128)(2,1)} collective-permute-done((bf16[384,2048]{1,0:T(8,128)(2,1)}, bf16[384,2048]{1,0:T(8,128)(2,1)}, u32[]{:S(2)}, u32[]{:S(2)}) %collective-permute-start.27) | collective-permute-done | bytes 1572896 | tf_op jit(solution)/shard_map/gather_xn/ppermute | solution.py:53
  415.2 16.2 %collective-permute-done.37 = bf16[384,2048]{1,0:T(8,128)(2,1)S(1)} collective-permute-done((bf16[384,2048]{1,0:T(8,128)(2,1)S(1)}, bf16[384,2048]{1,0:T(8,128)(2,1)S(1)}, u32[]{:S(2)}, u32[]{:S(2)}) %collective-permute-start.37) | collective-permute-done | bytes 1572896 | tf_op jit(solution)/shard_map/gather_dz/ppermute | solution.py:53
  465.5 86.0 %expert.2 = (bf16[2048,2048]{1,0:T(8,128)(2,1)}, bf16[2048,2048]{1,0:T(8,128)(2,1)}, bf16[2048,1024]{1,0:T(8,128)(2,1)}, bf16[2048,2048]{1,0:T(8,128)(2,1)}, bf1...) custom-call(s32[8,1,384]{2,1,0:T(1,128)} %get-tuple-element.271.rank_ref, ...), custom_call_target="tpu_custom_call" | custom-call | flops 1000 | bytes 1000 | tf_op jit(solution)/shard_map/expert0/expert/pallas_call | solution.py:458
  551.5 38.3 %expert_weight_grad.2 = bf16[2048,3072]{1,0:T(8,128)(2,1)} custom-call(bf16[2048,2048]{1,0:T(8,128)(2,1)} %get-tuple-element.61.xg_ref, bf16[2048,2048]{1,0:T(8,128)(2,1)} %get-tuple-element.62.dy_ref, bf16[2048,2048]{1,0:T(8,128)(2,1)} %get-tuple-element.63.dgu_ref, bf16[2048,1024]{1,0:T(8,128)(2,1)} %get-tuple-element.64.hm_ref), custom_call_target="tpu_custom_call" | custom-call | flops 1000 | bytes 1000 | tf_op jit(solution)/shard_map/expert0/expert_weight_grad/pallas_call | solution.py:490
  592.2 18.9 %all-gather.8.cloned.1.call-done = bf16[1,2048,3072]{2,1,0:T(8,128)(2,1)} async-done(((bf16[1,512,3072]{2,1,0:T(8,128)(2,1)}), bf16[1,2048,3072]{2,1,0:T(8,128)(2,1)}) %all-gather.8.cloned.1.call-update) | async-done | bytes 12582928 | tf_op jit(solution)/shard_map/gather_experts/all_gather | solution.py:624
  611.1 86.7 %expert.3 = (bf16[2048,2048]{1,0:T(8,128)(2,1)}, bf16[2048,2048]{1,0:T(8,128)(2,1)}, bf16[2048,1024]{1,0:T(8,128)(2,1)}, bf16[2048,2048]{1,0:T(8,128)(2,1)}, bf1...) custom-call(s32[8,1,384]{2,1,0:T(1,128)} %get-tuple-element.272.rank_ref, ...), custom_call_target="tpu_custom_call" | custom-call | flops 1000 | bytes 1000 | tf_op jit(solution)/shard_map/expert1/expert/pallas_call | solution.py:458
  719.1 38.8 %expert_weight_grad.3 = bf16[2048,3072]{1,0:T(8,128)(2,1)} custom-call(bf16[2048,2048]{1,0:T(8,128)(2,1)} %get-tuple-element.73.xg_ref, bf16[2048,2048]{1,0:T(8,128)(2,1)} %get-tuple-element.74.dy_ref, bf16[2048,2048]{1,0:T(8,128)(2,1)} %get-tuple-element.75.dgu_ref, bf16[2048,1024]{1,0:T(8,128)(2,1)} %get-tuple-element.76.hm_ref), custom_call_target="tpu_custom_call" | custom-call | flops 1000 | bytes 1000 | tf_op jit(solution)/shard_map/expert1/expert_weight_grad/pallas_call | solution.py:490
  788.9 31.7 %collective-permute-done.48 = f32[384,2]{0,1:T(2,128)S(1)} collective-permute-done((f32[384,2]{0,1:T(2,128)S(1)}, f32[384,2]{0,1:T(2,128)S(1)}, u32[]{:S(2)}, u32[]{:S(2)}) %collective-permute-start.48) | collective-permute-done | bytes 3104 | tf_op jit(solution)/shard_map/router_back/ppermute | solution.py:53
  836.9 15.9 %collective-permute-done.44 = bf16[192,2048]{1,0:T(8,128)(2,1)} collective-permute-done((bf16[192,2048]{1,0:T(8,128)(2,1)}, bf16[192,2048]{1,0:T(8,128)(2,1)}, u32[]{:S(2)}, u32[]{:S(2)}) %collective-permute-start.44) | collective-permute-done | bytes 786464 | tf_op jit(solution)/shard_map/scatter_dxn/ppermute | solution.py:53
  865.6 24.3 %all_to_all.40 = bf16[8,384,256]{2,1,0:T(8,128)(2,1)} all-to-all(bf16[8,384,256]{2,1,0:T(8,128)(2,1)S(1)} %bitcast.460), channel_id=1, replica_groups=mesh['seq'=4,'fsdp'=8] {'fsdp'}, dimensions={0} | all-to-all | bytes 3145728 | tf_op jit(solution)/shard_map/do_exchange/all_to_all | solution.py:702
  896.0 41.0 %attend_back.1 = (bf16[2,1536,256]{2,1,0:T(8,128)(2,1)}, bf16[2,1536,256]{2,1,0:T(8,128)(2,1)}, bf16[2,1536,256]{2,1,0:T(8,128)(2,1)}) custom-call(bf16[2,1536,256]{2,1,0:T(8,128)(2,1)} %bitcast.468, bf16[2,1536,256]{2,1,0:T(8,128)(2,1)} %bitcast.470, bf16[2,1536,256]{2,1,0:T(8,128)(2,1)} %bitcast.472, bf16[2,1536,256]{2,1,0:T(8,128)(2,1)} %bitcast.462, ...), custom_call_target="tpu_custom_call" | custom-call | flops 1000 | bytes 1000 | tf_op jit(solution)/shard_map/attend_back/pallas_call | solution.py:283
  936.9 28.6 %project_back.1 = (bf16[3072,768]{1,0:T(8,128)(2,1)}, bf16[2,4,8,48,2048]{4,3,2,1,0:T(8,128)(2,1)}, f32[8,128]{1,0:T(8,128)}) custom-call(bf16[3072,256]{1,0:T(8,128)(2,1)} %bitcast.492, bf16[3072,256]{1,0:T(8,128)(2,1)} %bitcast.493, bf16[3072,256]{1,0:T(8,128)(2,1)} %bitcast.494, f32[3072,256]{1,0:T(8,128)} %get-tuple-element.82.qp_ref, ...), custom_call_target="tpu_custom_call" | custom-call | flops 1000 | bytes 1000 | tf_op jit(solution)/shard_map/project_back/pallas_call | solution.py:337
  1093.3 15.5 %adam_expert.2 = (f32[2,512,3072]{2,1,0:T(8,128)}, f32[2,512,3072]{2,1,0:T(8,128)}, f32[2,512,3072]{2,1,0:T(8,128)}) custom-call(bf16[2,512,3072]{2,1,0:T(8,128)(2,1)} %w_ref.3, bf16[512,3072]{1,0:T(8,128)(2,1)} %reduce-scatter.4.cloned.1.call-done.g_ref, f32[2,512,3072]{2,1,0:T(8,128)} %m_ref.3, f32[2,512,3072]{2,1,0:T(8,128)} %v_ref.3), custom_call_target="tpu_custom_call" | custom-call | flops 1000 | bytes 1000 | tf_op jit(solution)/shard_map/adam_expert/pallas_call | solution.py:512
  1108.8 15.9 %adam_expert.3 = (f32[2,512,3072]{2,1,0:T(8,128)}, f32[2,512,3072]{2,1,0:T(8,128)}, f32[2,512,3072]{2,1,0:T(8,128)}) custom-call(bf16[2,512,3072]{2,1,0:T(8,128)(2,1)} %w_ref.3, bf16[512,3072]{1,0:T(8,128)(2,1)} %reduce-scatter.6.cloned.1.call-done.g_ref, f32[2,512,3072]{2,1,0:T(8,128)} %m_ref.3, ...), custom_call_target="tpu_custom_call", output_to_operand_aliasing={{0}: (4, {}), {1}: (5, {}), {2}: (6, {})} | custom-call | flops 1000 | bytes 1000 | tf_op jit(solution)/shard_map/adam_expert/pallas_call | solution.py:512
  1184.4 17.7 %collective-permute-done.59 = bf16[96,2048]{1,0:T(8,128)(2,1)} collective-permute-done((bf16[96,2048]{1,0:T(8,128)(2,1)}, bf16[96,2048]{1,0:T(8,128)(2,1)}, u32[]{:S(2)}, u32[]{:S(2)}) %collective-permute-start.59) | collective-permute-done | bytes 393248 | tf_op jit(solution)/shard_map/remap_out/ppermute | solution.py:53
  1206.4 22.9 %collective-permute-start.92 = (f32[1160]{0:T(1024)S(1)}, f32[1160]{0:T(1024)S(1)}, u32[]{:S(2)}, u32[]{:S(2)}) collective-permute-start(f32[1160]{0:T(1024)S(1)} %pad_maximum_fusion.15), channel_id=1, source_target_pairs={{0,8},{8,0},{16,24},{24,16},{1,9},{9,1},{17,25},{25,17},{2,10},{10... | collective-permute-start | bytes 13928 | tf_op jit(solution)/shard_map/small_sum/ppermute | solution.py:53
  1246.0 29.9 %collective-permute-done.93 = f32[1160]{0:T(1024)S(1)} collective-permute-done((f32[1160]{0:T(1024)S(1)}, f32[1160]{0:T(1024)S(1)}, u32[]{:S(2)}, u32[]{:S(2)}) %collective-permute-start.93) | collective-permute-done | bytes 4672 | tf_op jit(solution)/shard_map/small_sum/ppermute | solution.py:53
  1303.4 25.2 %collective-permute-done.66 = bf16[48,2048]{1,0:T(8,128)(2,1)S(1)} collective-permute-done((bf16[48,2048]{1,0:T(8,128)(2,1)S(1)}, bf16[48,2048]{1,0:T(8,128)(2,1)S(1)}, u32[]{:S(2)}, u32[]{:S(2)}) %collective-permute-start.66) | collective-permute-done | bytes 196640 | tf_op jit(solution)/shard_map/remap_out/ppermute | solution.py:53
  (647 shorter events, 687.2 us)
Async XLA Ops:
  7.2 223.7 %all-gather.6.cloned.1.call-start = ((), (), s32[]{:S(2)}) async-start(), calls=%async_computation.11 | async-start | bytes 3932160 | tf_op jit(solution)/shard_map/gather_wqkv/all_gather | solution.py:585
  29.6 435.9 %all-gather.10.cloned.1.call-start = ((), (), s32[]{:S(2)}) async-start(), calls=%async_computation.16 | async-start | bytes 15728640 | tf_op jit(solution)/shard_map/gather_experts/all_gather | solution.py:624
  80.5 66.9 %all-to-all-start.1 = ((bf16[4,96,2048]{2,1,0:T(8,128)(2,1)}), bf16[4,96,2048]{2,1,0:T(8,128)(2,1)S(1)}, u32[]{:S(2)}, u32[]{:S(2)}) async-start(bf16[4,96,2048]{2,1,0:T(8,128)(2,1)} %bitcast.1), calls=%async_computation.1 | async-start | bytes 3145728 | tf_op jit(solution)/shard_map/remap_x/all_to_all | solution.py:119
  101.4 509.7 %all-gather.8.cloned.1.call-start = ((), (), s32[]{:S(2)}) async-start(), calls=%async_computation.15 | async-start | bytes 15728640 | tf_op jit(solution)/shard_map/gather_experts/all_gather | solution.py:624
  151.3 47.8 %collective-permute-start.3 = (bf16[384,2048]{1,0:T(8,128)(2,1)S(1)}, bf16[384,2048]{1,0:T(8,128)(2,1)}, u32[]{:S(2)}, u32[]{:S(2)}) collective-permute-start(bf16[384,2048]{1,0:T(8,128)(2,1)S(1)} %bitcast.434), channel_id=1, source_target_pairs={{0,4},{1,5},{2,6},{3,7},{4,0},{5,1},{6,2},{7,3},{8,12},{9,13},{10,... | collective-permute-start | bytes 4718600 | tf_op jit(solution)/shard_map/gather_x/ppermute | solution.py:53
  152.1 68.0 %collective-permute-start = (bf16[384,2048]{1,0:T(8,128)(2,1)S(1)}, bf16[384,2048]{1,0:T(8,128)(2,1)}, u32[]{:S(2)}, u32[]{:S(2)}) collective-permute-start(bf16[384,2048]{1,0:T(8,128)(2,1)S(1)} %bitcast.435), channel_id=1, source_target_pairs={{0,1},{1,0},{2,3},{3,2},{4,5},{5,4},{6,7},{7,6},{8,9},{9,8},{10,11... | collective-permute-start | bytes 4718600 | tf_op jit(solution)/shard_map/gather_x/ppermute | solution.py:53
  216.7 67.5 %collective-permute-start.22 = (bf16[256,2048]{1,0:T(8,128)(2,1)}, bf16[256,2048]{1,0:T(8,128)(2,1)}, u32[]{:S(2)}, u32[]{:S(2)}) collective-permute-start(bf16[256,2048]{1,0:T(8,128)(2,1)} %collective-permute-done.21), channel_id=1, source_target_pairs={{0,1},{1,0},{2,3},{3,2},{4,5},{5,4},{6,7},{7,6},{8,9},{9,8},{10,11... | collective-permute-start | bytes 3145736 | tf_op jit(solution)/shard_map/gather_wo/ppermute | solution.py:53
  220.0 68.9 %collective-permute-start.25 = (bf16[256,2048]{1,0:T(8,128)(2,1)}, bf16[256,2048]{1,0:T(8,128)(2,1)}, u32[]{:S(2)}, u32[]{:S(2)}) collective-permute-start(bf16[256,2048]{1,0:T(8,128)(2,1)} %constant_dynamic-update-slice_fusion.18), channel_id=1, source_target_pairs={{0,1},{1,0},{2,3},{3,2},{4,5},{5,4},{6,7},{7,6},{8,9},{9,8},{10,11... | collective-permute-start | bytes 3145736 | tf_op jit(solution)/shard_map/gather_wo/ppermute | solution.py:53
  331.1 63.4 %all-to-all-start.4 = ((bf16[4,96,2048]{2,1,0:T(8,128)(2,1)}), bf16[4,96,2048]{2,1,0:T(8,128)(2,1)}, u32[]{:S(2)}, u32[]{:S(2)}) async-start(bf16[4,96,2048]{2,1,0:T(8,128)(2,1)} %bitcast.88), calls=%async_computation.4 | async-start | bytes 3145728 | tf_op jit(solution)/shard_map/remap_dz/all_to_all | solution.py:119
  335.4 560.6 %reduce-scatter.4.cloned.1.call-start = ((), (), s32[]{:S(2)}) async-start(), calls=%async_computation.12 | async-start | bytes 15728640 | tf_op jit(solution)/shard_map/expert0/reduce_scatter | solution.py:686
  336.3 47.0 %collective-permute-start.26 = (bf16[384,2048]{1,0:T(8,128)(2,1)}, bf16[384,2048]{1,0:T(8,128)(2,1)}, u32[]{:S(2)}, u32[]{:S(2)}) collective-permute-start(bf16[384,2048]{1,0:T(8,128)(2,1)} %multiply_convert_fusion), channel_id=1, source_target_pairs={{0,1},{1,0},{2,3},{3,2},{4,5},{5,4},{6,7},{7,6},{8,9},{9,8},{10,11... | collective-permute-start | bytes 4718600 | tf_op jit(solution)/shard_map/gather_xn/ppermute | solution.py:53
  404.9 52.0 %collective-permute-start.34 = (bf16[384,2048]{1,0:T(8,128)(2,1)S(1)}, bf16[384,2048]{1,0:T(8,128)(2,1)}, u32[]{:S(2)}, u32[]{:S(2)}) collective-permute-start(bf16[384,2048]{1,0:T(8,128)(2,1)S(1)} %bitcast.448), channel_id=1, source_target_pairs={{0,1},{1,0},{2,3},{3,2},{4,5},{5,4},{6,7},{7,6},{8,9},{9,8},{10,11... | collective-permute-start | bytes 4718600 | tf_op jit(solution)/shard_map/gather_dz/ppermute | solution.py:53
  589.8 519.0 %reduce-scatter.6.cloned.1.call-start = ((), (), s32[]{:S(2)}) async-start(), calls=%async_computation.13 | async-start | bytes 15728640 | tf_op jit(solution)/shard_map/expert1/reduce_scatter | solution.py:686
  757.9 609.0 %reduce-scatter.8.cloned.1.call-start = ((), (), s32[]{:S(2)}) async-start(), calls=%async_computation.14 | async-start | bytes 3932160 | tf_op jit(solution)/shard_map/scatter_wqkv/reduce_scatter | solution.py:723
  983.3 52.0 %collective-permute-start.54 = (bf16[4,384,2048]{2,1,0:T(8,128)(2,1)}, bf16[4,384,2048]{2,1,0:T(8,128)(2,1)}, u32[]{:S(2)}, u32[]{:S(2)}) collective-permute-start(bf16[4,384,2048]{2,1,0:T(8,128)(2,1)} %bitcast.126), channel_id=1, source_target_pairs={{0,1},{1,0},{2,3},{3,2},{4,5},{5,4},{6,7},{7,6},{8,9},{9,8},{10,11... | collective-permute-start | bytes 18874376 | tf_op jit(solution)/shard_map/scatter_out/ppermute | solution.py:53
  1054.2 70.6 %collective-permute-start.57 = (bf16[2,192,2048]{2,1,0:T(8,128)(2,1)}, bf16[2,192,2048]{2,1,0:T(8,128)(2,1)}, u32[]{:S(2)}, u32[]{:S(2)}) collective-permute-start(bf16[2,192,2048]{2,1,0:T(8,128)(2,1)} %pad_maximum_fusion.5), channel_id=1, source_target_pairs={{0,4},{1,5},{2,6},{3,7},{4,0},{5,1},{6,2},{7,3},{8,12},{9,13},{10,... | collective-permute-start | bytes 4718600 | tf_op jit(solution)/shard_map/scatter_out/ppermute | solution.py:53
  1057.0 69.5 %collective-permute-start.55 = (bf16[2,192,2048]{2,1,0:T(8,128)(2,1)}, bf16[2,192,2048]{2,1,0:T(8,128)(2,1)}, u32[]{:S(2)}, u32[]{:S(2)}) collective-permute-start(bf16[2,192,2048]{2,1,0:T(8,128)(2,1)} %pad_maximum_fusion.4), channel_id=1, source_target_pairs={{0,2},{1,3},{2,0},{3,1},{4,6},{5,7},{6,4},{7,5},{8,10},{9,11},{10,... | collective-permute-start | bytes 4718600 | tf_op jit(solution)/shard_map/scatter_out/ppermute | solution.py:53
  1080.0 53.8 %collective-permute-start.71 = (bf16[192,2048]{1,0:T(8,128)(2,1)}, bf16[192,2048]{1,0:T(8,128)(2,1)}, u32[]{:S(2)}, u32[]{:S(2)}) collective-permute-start(bf16[192,2048]{1,0:T(8,128)(2,1)} %get-tuple-element.181), channel_id=1, source_target_pairs={{0,4},{1,5},{2,6},{3,7},{4,0},{5,1},{6,2},{7,3},{8,12},{9,13},{10,... | collective-permute-start | bytes 2359304 | tf_op jit(solution)/shard_map/scatter_da/ppermute | solution.py:53
  1080.6 53.2 %collective-permute-start.73 = (bf16[192,2048]{1,0:T(8,128)(2,1)}, bf16[192,2048]{1,0:T(8,128)(2,1)}, u32[]{:S(2)}, u32[]{:S(2)}) collective-permute-start(bf16[192,2048]{1,0:T(8,128)(2,1)} %get-tuple-element.182), channel_id=1, source_target_pairs={{0,2},{1,3},{2,0},{3,1},{4,6},{5,7},{6,4},{7,5},{8,10},{9,11},{10,... | collective-permute-start | bytes 2359304 | tf_op jit(solution)/shard_map/scatter_da/ppermute | solution.py:53
  1146.9 140.3 %collective-permute-start.81 = (bf16[4,256,2048]{2,1,0:T(8,128)(2,1)}, bf16[4,256,2048]{2,1,0:T(8,128)(2,1)}, u32[]{:S(2)}, u32[]{:S(2)}) collective-permute-start(bf16[4,256,2048]{2,1,0:T(8,128)(2,1)} %slice_bitcast_fusion), channel_id=1, source_target_pairs={{0,1},{1,0},{2,3},{3,2},{4,5},{5,4},{6,7},{7,6},{8,9},{9,8},{10,11... | collective-permute-start | bytes 12582920 | tf_op jit(solution)/shard_map/scatter_wo/ppermute | solution.py:53
  1172.8 161.7 %all-to-all-start.6 = ((bf16[4,96,2048]{2,1,0:T(8,128)(2,1)}), bf16[4,96,2048]{2,1,0:T(8,128)(2,1)}, u32[]{:S(2)}, u32[]{:S(2)}) async-start(bf16[4,96,2048]{2,1,0:T(8,128)(2,1)} %bitcast.169), calls=%async_computation.7 | async-start | bytes 3145728 | tf_op jit(solution)/shard_map/remap_grad/all_to_all | solution.py:142
  1229.3 47.3 %collective-permute-start.94 = (f32[1160]{0:T(1024)S(1)}, f32[1160]{0:T(1024)S(1)}, u32[]{:S(2)}, u32[]{:S(2)}) collective-permute-start(f32[1160]{0:T(1024)S(1)} %pad_maximum_fusion.17), channel_id=1, source_target_pairs={{0,24},{8,16},{16,8},{24,0},{1,25},{9,17},{17,9},{25,1},{2,26},{10... | collective-permute-start | bytes 13928 | tf_op jit(solution)/shard_map/small_sum/ppermute | solution.py:53
  1232.7 106.0 %collective-permute-start.68 = (bf16[48,2048]{1,0:T(8,128)(2,1)S(1)}, bf16[48,2048]{1,0:T(8,128)(2,1)}, u32[]{:S(2)}, u32[]{:S(2)}) collective-permute-start(bf16[48,2048]{1,0:T(8,128)(2,1)S(1)} %get-tuple-element.225), channel_id=1, source_target_pairs={{0,7},{1,6},{2,5},{3,4},{4,3},{5,2},{6,1},{7,0},{8,15},{9,14},{10,... | collective-permute-start | bytes 589832 | tf_op jit(solution)/shard_map/remap_out/ppermute | solution.py:53
  1245.7 87.1 %collective-permute-start.67 = (bf16[48,2048]{1,0:T(8,128)(2,1)S(1)}, bf16[48,2048]{1,0:T(8,128)(2,1)}, u32[]{:S(2)}, u32[]{:S(2)}) collective-permute-start(bf16[48,2048]{1,0:T(8,128)(2,1)S(1)} %get-tuple-element.226), channel_id=1, source_target_pairs={{0,6},{1,7},{2,4},{3,5},{4,2},{5,3},{6,0},{7,1},{8,14},{9,15},{10,... | collective-permute-start | bytes 589832 | tf_op jit(solution)/shard_map/remap_out/ppermute | solution.py:53
  (153 other events, 3299.6 us)
Sparse Core Ops, SparseCore 0:
  29.8 107.6 all-gather.5
  139.0 254.4 all-gather.9
  395.0 216.0 all-gather.7
  613.3 210.0 reduce-scatter.3
  825.6 212.8 reduce-scatter.5
  1170.2 94.9 reduce-scatter.7

commit v2 on v1

--- a/solution.py
+++ b/solution.py
@@ -29,6 +29,11 @@
 
 BRIEF = pl.CostEstimate(flops=1000, bytes_accessed=1000, transcendentals=0)
 
+
+def lasting(us):
+    return pl.CostEstimate(flops=int(us * 1e9), bytes_accessed=1000, transcendentals=0)
+
+
 F32 = jnp.float32
 BF16 = jnp.bfloat16
 
@@ -77,72 +82,84 @@
     return [value, go(value, 1), by_x, go(by_x, 1), by_y, go(by_y, 1), far, go(far, 1)]
 
 
-def scatter_first(count, value):
-    return swap(value[1], 1, "fsdp", count) if count == 8 else None
-
-
-def scatter_rest(count, value, got):
-    if count != 8:
-        mine = lax.axis_index("fsdp")
-        stacked = value.transpose(1, 0, 2, 3).reshape(count, *value.shape[2:])
-        stacked = reorder(stacked, mine ^ jnp.arange(count))
-        return lax.psum_scatter(stacked, "fsdp", scatter_dimension=0).astype(F32)
-    go = functools.partial(swap, axis="fsdp", count=count)
-    total = value[0].astype(F32) + got.astype(F32)
-    half = total.shape[1] // 2
-    top, low = total[:, :half], total[:, half:]
-    by_x = go(jnp.stack([top[3], top[1]]).astype(BF16), 2).astype(F32)
-    by_y = go(jnp.stack([low[3], low[2]]).astype(BF16), 4).astype(F32)
-    y_last = go((top[2] + by_x[0]).astype(BF16), 4).astype(F32)
-    x_last = go((low[1] + by_y[0]).astype(BF16), 2).astype(F32)
-    return jnp.concatenate([top[0] + by_x[1] + y_last, low[0] + by_y[1] + x_last], axis=0)
-
-
-def plane_scatter(count, value):
-    return scatter_rest(count, value, scatter_first(count, value))
-
-
-def small_sum(value, shares, planes, seq_count, fsdp_count):
+class Scatter:
+    def __init__(self, count, near, far, hold=()):
+        self.count, self.near = count, near
+        if count != 8:
+            stacked = jnp.stack([near, far], axis=1).reshape(count, *near.shape[1:])
+            stacked = reorder(stacked, lax.axis_index("fsdp") ^ jnp.arange(count))
+            self.sum = lax.psum_scatter(stacked, "fsdp", scatter_dimension=0).astype(F32)
+            self.got, self.sends, self.lasts = self.sum, (self.sum,), (self.sum,)
+            return
+        self.half = near.shape[1] // 2
+        self.got = swap(far, 1, "fsdp", count)
+        sends = (self.total(slice(1, None, 2), 0).astype(BF16), self.total(slice(2, None), 1).astype(BF16))
+        if hold:
+            sends = lax.optimization_barrier((*sends, *hold))[:2]
+        self.sends = sends
+
+    def total(self, index, part):
+        rows = slice(self.half * part, self.half * (part + 1))
+        return self.near[index, rows].astype(F32) + self.got[index, rows].astype(F32)
+
+    def second(self, *beside):
+        if self.count == 8:
+            self.by_x = swap(self.sends[0], 2, "fsdp", self.count)
+            self.by_y = swap(self.sends[1], 4, "fsdp", self.count)
+            if beside:
+                self.by_x, self.by_y = lax.optimization_barrier((self.by_x, self.by_y, *beside))[:2]
+            self.lasts = (
+                (self.total(2, 0) + self.by_x[1].astype(F32)).astype(BF16),
+                (self.total(1, 1) + self.by_y[1].astype(F32)).astype(BF16),
+            )
+        return self
+
+    def third(self, *beside):
+        if self.count != 8:
+            return self.sum
+        y_last = swap(self.lasts[0], 4, "fsdp", self.count)
+        x_last = swap(self.lasts[1], 2, "fsdp", self.count)
+        if beside:
+            y_last, x_last = lax.optimization_barrier((y_last, x_last, *beside))[:2]
+        top = self.total(0, 0) + self.by_x[0].astype(F32) + y_last.astype(F32)
+        low = self.total(0, 1) + self.by_y[0].astype(F32) + x_last.astype(F32)
+        return jnp.concatenate([top, low], axis=0)
+
+
+def plane_sum(value, fsdp_count):
     step = 1
     while step < fsdp_count:
         value = value + swap(value, step, "fsdp", fsdp_count)
         step *= 2
-    return sum(exchange([shares(value, planes[m]) for m in range(seq_count)], "seq", seq_count))
-
-
-def to_plane(value, seq_count, fsdp_count):
-    rows, width = value.shape
-    members, chunk = fsdp_count // seq_count, rows // fsdp_count
-    value = value.reshape(fsdp_count, chunk, width)
-    value = lax.all_to_all(value, "fsdp", split_axis=0, concat_axis=0, tiled=True)
+    return value
+
+
+def to_plane_fsdp(value, fsdp_count):
+    value = value.reshape(fsdp_count, -1, value.shape[1])
+    return lax.all_to_all(value, "fsdp", split_axis=0, concat_axis=0, tiled=True)
+
+
+def to_plane_seq(value, seq_count, fsdp_count):
+    _, chunk, width = value.shape
+    members = fsdp_count // seq_count
     value = value.reshape(seq_count, members * chunk, width)
     value = lax.all_to_all(value, "seq", split_axis=0, concat_axis=0, tiled=True)
     value = value.reshape(seq_count, members, chunk, width).transpose(1, 0, 2, 3)
-    return value.reshape(rows, width)
-
-
-def from_plane(value, here, plane, seq_count, fsdp_count):
-    rows, width = value.shape
-    members, chunk = fsdp_count // seq_count, rows // fsdp_count
-    around, planes = here ^ jnp.arange(fsdp_count), plane ^ jnp.arange(seq_count)
-    value = value.reshape(members, seq_count, chunk, width).transpose(1, 0, 2, 3)
-    value = reorder(value.reshape(seq_count, members * chunk, width), planes)
-    value = jnp.stack(exchange(list(value), "seq", seq_count))
-    value = value.reshape(seq_count, members, chunk, width)
-    value = reorder(value, planes).reshape(fsdp_count, chunk, width)
-    value = jnp.stack(exchange(list(reorder(value, around)), "fsdp", fsdp_count))
-    return reorder(value, around).reshape(rows, width)
-
-
-def from_plane_whole(value, seq_count, fsdp_count):
+    return value.reshape(fsdp_count * chunk, width)
+
+
+def from_plane_seq(value, seq_count, fsdp_count):
     rows, width = value.shape
     members, chunk = fsdp_count // seq_count, rows // fsdp_count
     value = value.reshape(members, seq_count, chunk, width).transpose(1, 0, 2, 3)
     value = value.reshape(seq_count, members * chunk, width)
-    value = lax.all_to_all(value, "seq", split_axis=0, concat_axis=0, tiled=True)
-    value = value.reshape(fsdp_count, chunk, width)
-    value = lax.all_to_all(value, "fsdp", split_axis=0, concat_axis=0, tiled=True)
-    return value.reshape(rows, width)
+    return lax.all_to_all(value, "seq", split_axis=0, concat_axis=0, tiled=True).reshape(rows, width)
+
+
+def from_plane_fsdp(value, fsdp_count):
+    rows, width = value.shape
+    value = value.reshape(fsdp_count, rows // fsdp_count, width)
+    return lax.all_to_all(value, "fsdp", split_axis=0, concat_axis=0, tiled=True).reshape(rows, width)
 
 
 def head_norm(value):
@@ -288,13 +305,13 @@
         out_shape=[out, out, out],
         scratch_shapes=[pltpu.VMEM((length, HDIM), F32), pltpu.VMEM((length, HDIM), F32)],
         compiler_params=pltpu.CompilerParams(vmem_limit_bytes=VMEM_LIMIT),
-        cost_estimate=BRIEF,
+        cost_estimate=lasting(40),
         name="attend_back",
     )(q, k, v, do, row_doc, col_doc)
 
 
 def project_back_kernel(
-    heads, dq_ref, dk_ref, dv_ref, qp_ref, kp_ref, cos_ref, sin_ref, gq_ref, gk_ref, w_ref, dp_ref, da_ref, dg_ref
+    heads, dq_ref, dk_ref, dv_ref, qp_ref, kp_ref, cos_ref, sin_ref, gq_ref, gk_ref, w_ref, dp_ref, dg_ref, *da_refs
 ):
     cosine, sine = cos_ref[...], -sin_ref[...]
     width = heads * HDIM
@@ -318,7 +335,7 @@
             dp_ref[:, n * width + h * HDIM : n * width + (h + 1) * HDIM] = back.astype(BF16)
         dg_ref[n : n + 1, :] += total
     dp_ref[:, 2 * width :] = dv_ref[...]
-    split_chunks(da_ref, slice(None), dot(dp_ref[...], w_ref[...], 1, 1))
+    split_chunks(da_refs, slice(None), dot(dp_ref[...], w_ref[...], 1, 1))
 
 
 def project_back(dq, dk, dv, q_pre, k_pre, cosine, sine, gain_q, gain_k, w, block):
@@ -339,50 +356,53 @@
         grid=(rows // block,),
         in_specs=[row(width)] * 5
         + [row(HDIM), row(HDIM), whole((1, HDIM)), whole((1, HDIM)), whole(w.shape)],
-        out_specs=[row(3 * width), form, whole((8, HDIM))],
-        out_shape=[shape((rows, 3 * width), BF16), result, shape((8, HDIM), F32)],
+        out_specs=[row(3 * width), whole((8, HDIM)), *form],
+        out_shape=[shape((rows, 3 * width), BF16), shape((8, HDIM), F32), *result],
         compiler_params=pltpu.CompilerParams(vmem_limit_bytes=VMEM_LIMIT),
-        cost_estimate=BRIEF,
+        cost_estimate=lasting(28),
         name="project_back",
     )(dq, dk, dv, q_pre, k_pre, cosine, sine, gain_q, gain_k, w)
 
 
-def join_chunks(ref, cols):
-    if len(ref.shape) == 2:
-        return ref[:, cols]
-    two, half, _, chunk, _ = ref.shape
-    return jnp.concatenate([ref[k % 2, k // 2, 0, :, cols] for k in range(two * half)], axis=0)
-
-
-def split_chunks(ref, cols, value):
-    if len(ref.shape) == 2:
-        ref[:, cols] = value.astype(BF16)
+def join_chunks(refs, cols):
+    if len(refs) == 1:
+        return refs[0][:, cols]
+    half = refs[0].shape[0]
+    return jnp.concatenate([refs[k % 2][k // 2, 0, :, cols] for k in range(2 * half)], axis=0)
+
+
+def split_chunks(refs, cols, value):
+    if len(refs) == 1:
+        refs[0][:, cols] = value.astype(BF16)
         return
-    two, half, _, chunk, _ = ref.shape
-    for k in range(two * half):
-        ref[k % 2, k // 2, 0, :, cols] = value[k * chunk : (k + 1) * chunk].astype(BF16)
+    half, _, chunk, _ = refs[0].shape
+    for k in range(2 * half):
+        refs[k % 2][k // 2, 0, :, cols] = value[k * chunk : (k + 1) * chunk].astype(BF16)
 
 
 def chunk_form(blocks, rows, model):
     chunk = rows // blocks
     if chunk % 16:
-        return pl.BlockSpec((rows, model), lambda i: (i, 0)), jax.ShapeDtypeStruct((blocks * rows, model), BF16)
-    shape = (2, blocks // 2, blocks, chunk, model)
-    spec = pl.BlockSpec((2, blocks // 2, 1, chunk, model), lambda i: (0, 0, i, 0, 0))
-    return spec, jax.ShapeDtypeStruct(shape, BF16)
-
-
-def by_owner(value, blocks):
-    if value.ndim == 2:
+        return [pl.BlockSpec((rows, model), lambda i: (i, 0))], [jax.ShapeDtypeStruct((blocks * rows, model), BF16)]
+    spec = pl.BlockSpec((blocks // 2, 1, chunk, model), lambda i: (0, i, 0, 0))
+    return [spec] * 2, [jax.ShapeDtypeStruct((blocks // 2, blocks, chunk, model), BF16)] * 2
+
+
+def by_owner(parts, blocks):
+    if len(parts) == 1:
+        value = parts[0]
         rows, model = value.shape[0] // blocks, value.shape[1]
         value = value.reshape(blocks, blocks // 2, 2, rows // blocks, model).transpose(2, 1, 0, 3, 4)
-    return value.reshape(2, blocks // 2, -1, value.shape[-1])
-
-
-def expert_kernel(wide, narrow, more, rank_ref, rank_col_ref, gate_ref, x_ref, dz_ref, w_ref, *refs):
+        parts = list(value)
+    return [part.reshape(blocks // 2, -1, part.shape[-1]) for part in parts]
+
+
+def expert_kernel(wide, narrow, more, parts, rank_ref, rank_col_ref, gate_ref, x_ref, dz_ref, w_ref, *refs):
     if more:
-        old_out_ref, old_dx_ref, *refs = refs
-    xg_ref, dy_ref, hm_ref, dgu_ref, out_ref, dx_ref, dgate_ref, dzg_ref, yg_ref, dxe_ref, sum_ref = refs
+        old_out, old_dx, refs = refs[:parts], refs[parts : 2 * parts], refs[2 * parts :]
+    xg_ref, dy_ref, hm_ref, dgu_ref, *refs = refs
+    out_refs, dx_refs = refs[:parts], refs[parts : 2 * parts]
+    dgate_ref, dzg_ref, yg_ref, dxe_ref, sum_ref = refs[2 * parts :]
     rows, model = x_ref.shape
     capacity, feed = hm_ref.shape
     hit = rank_ref[0] == lax.broadcasted_iota(jnp.int32, (capacity, rows), 0)
@@ -437,10 +457,10 @@
         out = dot(sel_back, yg_ref[:, cols], 1, 0)
         dx = dot(sel_back, dxe_ref[:, cols], 1, 0)
         if more:
-            out += join_chunks(old_out_ref, cols).astype(F32)
-            dx += join_chunks(old_dx_ref, cols).astype(F32)
-        split_chunks(out_ref, cols, out)
-        split_chunks(dx_ref, cols, dx)
+            out += join_chunks(old_out, cols).astype(F32)
+            dx += join_chunks(old_dx, cols).astype(F32)
+        split_chunks(out_refs, cols, out)
+        split_chunks(dx_refs, cols, dx)
         return 0
 
     lax.fori_loop(0, model // wide, combine, 0)
@@ -453,21 +473,22 @@
     line = pl.BlockSpec((1, 1, rows), lambda i: (i, 0, 0))
     shape = jax.ShapeDtypeStruct
     slots = blocks * capacity
-    more = old is not None
+    more = bool(old)
     form, result = chunk_form(blocks, rows, model)
-    return pl.pallas_call(
-        functools.partial(expert_kernel, wide, narrow, more),
+    xg, dy, hm, dgu, *rest = pl.pallas_call(
+        functools.partial(expert_kernel, wide, narrow, more, len(form)),
         grid=(blocks,),
         in_specs=[line, pl.BlockSpec((1, rows, 1), lambda i: (i, 0, 0)), line, per_block(rows, model), per_block(rows, model),
-            pl.BlockSpec(w.shape, lambda i: (0, 0), pipeline_mode=pl.Buffered(1))] + [form] * (2 if more else 0),
-        out_specs=[per_block(capacity, model), per_block(capacity, model), per_block(capacity, feed), per_block(capacity, 2 * feed), form, form, line],
+            pl.BlockSpec(w.shape, lambda i: (0, 0), pipeline_mode=pl.Buffered(1))] + form * (2 if more else 0),
+        out_specs=[per_block(capacity, model), per_block(capacity, model), per_block(capacity, feed), per_block(capacity, 2 * feed), *form, *form, line],
         out_shape=[shape((slots, model), BF16), shape((slots, model), BF16), shape((slots, feed), BF16), shape((slots, 2 * feed), BF16),
-            result, result, shape((blocks, 1, rows), F32)],
+            *result, *result, shape((blocks, 1, rows), F32)],
         scratch_shapes=[pltpu.VMEM((capacity, model), BF16)] * 3 + [pltpu.VMEM((capacity, 128), F32)],
         compiler_params=pltpu.CompilerParams(vmem_limit_bytes=VMEM_LIMIT),
         cost_estimate=BRIEF,
         name="expert",
-    )(rank[:, None, :], rank[:, :, None], gate[:, None, :], x, dz, w, *(old or ()))
+    )(rank[:, None, :], rank[:, :, None], gate[:, None, :], x, dz, w, *old)
+    return xg, dy, hm, dgu, rest[: len(form)], rest[len(form) : -1], rest[-1][:, 0]
 
 
 def weight_kernel(narrow, xg_ref, dy_ref, dgu_ref, hm_ref, out_ref, flip_ref):
@@ -577,7 +598,7 @@
     with jax.named_scope("gather_wo"):
         out_part = gather_direct(attn_weight[:, 3 * model :], "seq", seq_count)
     with jax.named_scope("remap_x"):
-        x_low = to_plane(tokens[0], seq_count, fsdp_count)
+        x_low = to_plane_seq(to_plane_fsdp(tokens[0], fsdp_count), seq_count, fsdp_count)
     with jax.named_scope("gather_wqkv"):
         first_part = attn_weight[:, : 3 * model].reshape(shard, 3, fsdp_count, width).transpose(2, 0, 1, 3)
         first_part = reorder(first_part.reshape(fsdp_count, shard, 3 * width), around)
@@ -631,7 +652,7 @@
     with jax.named_scope("gather_x"):
         x_all = blocked(plane_gather(fsdp_count, x_low))
     with jax.named_scope("remap_dz"):
-        dz_low = to_plane(after(cotangent[0], x_all), seq_count, fsdp_count)
+        dz_low = to_plane_seq(to_plane_fsdp(after(cotangent[0], x_all), fsdp_count), seq_count, fsdp_count)
 
     own = here * EXP_DEV + jnp.arange(EXP_DEV, dtype=jnp.int32)
     named = jnp.any(routes_all[:, None, :, :] == own[None, :, None, None], axis=3)
@@ -668,100 +689,135 @@
         raised = jnp.where(chosen, jnp.exp(logits - top), 0.0)
         gates = raised / jnp.sum(raised, axis=2, keepdims=True)
         gates_mine = lax.dynamic_slice_in_dim(gates, here * EXP_DEV, EXP_DEV, axis=2)
-    sums, gate_back, expert_share, held = None, [], [], None
+    sums, gate_back, expert_share, held = (), [], [], None
     for e in range(EXP_DEV):
         with jax.named_scope(f"expert{e}"):
             w = expert_full[e] if held is None else after(expert_full[e], held)
             xg, dy, hm, dgu, mixed, dxn, dgate = run_expert(
                 rank[:, e], gates_mine[:, :, e], xn_all, dz_all, w, sums, capacity
             )
-            sums = (mixed, dxn)
-            gate_back.append(dgate[:, 0])
+            sums = (*mixed, *dxn)
+            gate_back.append(dgate)
             if e == EXP_DEV - 1:
-                dxn = by_owner(dxn, blocks)
-                dxn_first = scatter_first(fsdp_count, dxn)
-                if dxn_first is not None:
-                    xg = after(xg, dxn_first)
+                gate_parts = exchange(pieces(jnp.stack(gate_back, axis=2)), "fsdp", fsdp_count)
+                dxn = Scatter(fsdp_count, *by_owner(dxn, blocks), hold=gate_parts)
+                xg = after(xg, *dxn.sends)
             held = expert_weight_grad(xg, dy, dgu, hm)
             expert_share.append(lax.psum_scatter(held, "seq", scatter_dimension=0, tiled=True))
 
     with jax.named_scope("router_back"):
-        parts = exchange(pieces(jnp.stack(gate_back, axis=2)), "fsdp", fsdp_count)
-        gate_grad = reorder(jnp.stack(parts, axis=1), around, 1).reshape(rows, experts)
+        gate_grad = reorder(jnp.stack(gate_parts, axis=1), around, 1).reshape(rows, experts)
         gates_own, chosen_own = pieces(gates)[0], pieces(chosen)[0]
         gate_grad = jnp.where(chosen_own, gate_grad, 0.0)
         dlog = (gates_own * (gate_grad - jnp.sum(gates_own * gate_grad, axis=1, keepdims=True))).astype(BF16)
     with jax.named_scope("scatter_dxn"):
-        dxn_own = scatter_rest(fsdp_count, dxn, dxn_first)
+        dxn_own = dxn.second(held).third()
     dxn_own = dxn_own + dot(dlog, full_router, 1, 1)
     middle_back, ffn_gain_grad = norm_back(dxn_own, middle, ffn_gain)
     middle_grad = dz_low.astype(F32) + middle_back
     db = middle_grad.astype(BF16)
+
     with jax.named_scope("do_exchange"):
         do_own = dot(db, out_proj, 1, 1).astype(BF16).reshape(rows, fsdp_count, width).transpose(1, 0, 2)
         do_own = lax.all_to_all(do_own, "fsdp", split_axis=0, concat_axis=0, tiled=True)
         do_all = reorder(do_own, around).reshape(fsdp_count, blocks, chunk, width).transpose(1, 0, 2, 3)
         do_all = do_all.reshape(seq_shape)
-    do_all = after(do_all, held, expert_share[0])
+    with jax.named_scope("scatter_out"):
+        near, far = by_owner(mixed, blocks)
+        mixed = Scatter(fsdp_count, near, after(far, db), hold=(do_all,))
+    do_all = after(do_all, expert_share[0], *mixed.sends)
     dq, dk, dv = (
         t.reshape(-1, width) for t in attend_back(q_seq, k_seq, v_seq, do_all, row_doc, col_doc)
     )
     with jax.named_scope("scatter_out"):
-        mixture = plane_scatter(fsdp_count, by_owner(after(mixed, dq), blocks))
-        layer_low = (middle + mixture).astype(BF16)
-    d_proj, da_part, gain_qk = project_back(
-        dq, dk, dv, q_pre, k_pre, cosine_all, sine_all, gain_q, gain_k, in_proj, rows
+        mixed = mixed.second(dq)
+    d_proj, gain_qk, *da_part = project_back(
+        after(dq, *mixed.lasts), dk, dv, q_pre, k_pre, cosine_all, sine_all, gain_q, gain_k, in_proj, rows
     )
+    with jax.named_scope("scatter_out"):
+        layer_low = (middle + mixed.third(d_proj)).astype(BF16)
+    with jax.named_scope("scatter_da"):
+        near, far = by_owner(da_part, blocks)
+        da = Scatter(fsdp_count, near, after(far, layer_low))
     with jax.named_scope("remap_out"):
-        layer_out = from_plane(layer_low, here, plane, seq_count, fsdp_count)
+        layer_out = from_plane_seq(layer_low, seq_count, fsdp_count)
+    with jax.named_scope("weight_grads"):
+        in_grad = dot(after(a_all, *da.sends), d_proj, 0, 0).astype(BF16)
+        expert_new = adam_expert(
+            0, expert_weight, after(expert_share[0], *da.sends), expert_first, expert_second, None, RATE_EXPERT
+        )
     with jax.named_scope("scatter_da"):
-        da = plane_scatter(fsdp_count, by_owner(da_part, blocks))
-    input_back, attn_gain_grad = norm_back(da, inputs, attn_gain)
-    input_low = (middle_grad + input_back).astype(BF16)
-    with jax.named_scope("scatter_wqkv"):
-        in_grad = after(dot(a_all, d_proj, 0, 0).astype(BF16), expert_share[1], input_low)
-        in_share = lax.psum_scatter(in_grad, "seq", scatter_dimension=0, tiled=True)
-        in_share = reorder(in_share.reshape(fsdp_count, shard, 3 * width), around)
-        in_share = reorder(jnp.stack(exchange(list(in_share), "fsdp", fsdp_count)), around)
-        in_share = in_share.reshape(fsdp_count, shard, 3, width).transpose(1, 2, 0, 3).reshape(shard, 3 * model)
-    with jax.named_scope("remap_grad"):
-        input_grad = from_plane_whole(input_low, seq_count, fsdp_count).astype(F32)
-    with jax.named_scope("scatter_wo"):
-        out_grad = dot(o_own, db, 0, 0).astype(BF16).reshape(seq_count, fsdp_count, shard, model)
+        da = da.second(in_grad, expert_new[0])
+    with jax.named_scope("weight_grads"):
+        out_grad = dot(after(o_own, *da.lasts), db, 0, 0).astype(BF16)
+        out_grad = out_grad.reshape(seq_count, fsdp_count, shard, model)
         pairs = reorder(around, jnp.arange(fsdp_count).reshape(-1, 2).T.reshape(-1))
         out_grad = reorder(out_grad, pairs, 1).transpose(1, 0, 2, 3)
         out_grad = out_grad.reshape(2, fsdp_count // 2, seq_count * shard, model)
-        out_share = plane_scatter(fsdp_count, after(out_grad, da)).astype(BF16)
-        out_share = reorder(out_share.reshape(seq_count, shard, model), planes)
-        out_share = sum(p.astype(F32) for p in exchange(list(out_share), "seq", seq_count))
+    with jax.named_scope("scatter_da"):
+        da_own = da.third(out_grad, layer_out)
+    input_back, attn_gain_grad = norm_back(da_own, inputs, attn_gain)
+    input_low = (middle_grad + input_back).astype(BF16)
+    with jax.named_scope("remap_grad"):
+        input_grad = from_plane_seq(input_low, seq_count, fsdp_count)
+    with jax.named_scope("scatter_wqkv"):
+        in_grad = after(in_grad, input_low)
+        in_share = lax.psum_scatter(in_grad, "seq", scatter_dimension=0, tiled=True)
     with jax.named_scope("small_sum"):
         router_grad = dot(normed, dlog, 0, 0)
         small = jnp.concatenate(
             [router_grad.reshape(-1), attn_gain_grad, ffn_gain_grad, gain_qk[0], gain_qk[1]]
         )
+        small = plane_sum(small, fsdp_count)
         own_router, own_gain = shard * experts, gain_values.shape[0]
 
-        def shares(value, p):
+        def own_part(p):
             device = p * fsdp_count + here
             return jnp.concatenate(
                 [
-                    lax.dynamic_slice_in_dim(value, device * own_router, own_router),
-                    lax.dynamic_slice_in_dim(value, model * experts + device * own_gain, own_gain),
+                    lax.dynamic_slice_in_dim(small, device * own_router, own_router),
+                    lax.dynamic_slice_in_dim(small, model * experts + device * own_gain, own_gain),
                 ]
             )
 
-        small = small_sum(small, shares, planes, seq_count, fsdp_count)
-        router_share, gain_share = small[:own_router].reshape(shard, experts), small[own_router:]
+        small_parts = [own_part(planes[m]) for m in range(seq_count)]
+    with jax.named_scope("scatter_wo"):
+        out_grad = Scatter(fsdp_count, out_grad[0], after(out_grad[1], input_low), hold=small_parts)
+    with jax.named_scope("small_sum"):
+        small_parts = exchange(small_parts, "seq", seq_count)
+    for e in range(1, EXP_DEV):
+        expert_new = adam_expert(
+            e,
+            expert_weight,
+            after(expert_share[e], *out_grad.sends),
+            expert_first,
+            expert_second,
+            expert_new,
+            RATE_EXPERT,
+        )
+    with jax.named_scope("scatter_wo"):
+        out_grad = out_grad.second(expert_new[0])
+        out_share = out_grad.third().astype(BF16)
+    with jax.named_scope("scatter_wo"):
+        out_parts = reorder(out_share.reshape(seq_count, shard, model), planes)
+        out_parts = exchange(list(out_parts), "seq", seq_count)
+    with jax.named_scope("scatter_wqkv"):
+        in_share, *waiting = lax.optimization_barrier((in_share, *out_parts, *small_parts))
+        in_share = reorder(in_share.reshape(fsdp_count, shard, 3 * width), around)
+        in_share = reorder(jnp.stack(exchange(list(in_share), "fsdp", fsdp_count)), around)
+        in_share = in_share.reshape(fsdp_count, shard, 3, width).transpose(1, 2, 0, 3).reshape(shard, 3 * model)
+    with jax.named_scope("remap"):
+        both = jnp.concatenate([input_grad, layer_out], axis=1)
+        both = from_plane_fsdp(after(both, *out_grad.lasts), fsdp_count)
+        input_grad, layer_out = both[:, :model].astype(F32), both[:, model:]
+    out_share = sum(p.astype(F32) for p in waiting[:seq_count])
+    small_own = sum(waiting[seq_count:])
+    router_share, gain_share = small_own[:own_router].reshape(shard, experts), small_own[own_router:]
 
     attn_share = jnp.concatenate([in_share.astype(F32), out_share], axis=1)
     attn_new = adam_step(attn_weight, attn_share, attn_first, attn_second, RATE_ATTN)
     router_new = adam_step(router_weight, router_share, router_first, router_second, RATE_ROUTER)
     gain_new = adam_step(gain_values, gain_share, gain_first, gain_second, RATE_GAIN)
-    expert_new = None
-    for e in range(EXP_DEV):
-        expert_new = adam_expert(
-            e, expert_weight, expert_share[e], expert_first, expert_second, expert_new, RATE_EXPERT
-        )
     return (layer_out[None], input_grad[None], *attn_new, *router_new, *gain_new, *expert_new)
 
 

time: 1420 us -> 1240 us (0.87)
  waiting for transfers between devices: 354 us -> 278 us
  other arithmetic: 144 us -> 92.2 us
  local copies, waits for them, and re-layouts: 231 us -> 190 us
  blocking collectives: 64.7 us -> 40.5 us
  starting transfers between devices: 152 us -> 171 us
    ppermute x95 -> x85, waiting for transfers between devices: 280 us -> 177 us  [swap(): return lax.ppermute(value, axis, [(i, i ^ step) for i in range(count)])]
    add x13 -> x8, other arithmetic: 70.8 us -> 13.5 us  [the longest x3 11.4 us: third(): top = self.total(0, 0) + self.by_x[0].astype(F32) + y_last.astype(F32)]
    slice x10 -> x4, local copies, waits for them, and re-layouts: 36 us -> 7.23 us  [the longest x1 6.38 us: body(): out_grad[0]]
    all_to_all x1 -> x0, blocking collectives: 24.3 us -> none  [body(): lax.all_to_all(do_own, 'fsdp', split_axis=0, concat_axis=0, tiled=True)]
    all_to_all x6 -> x8, waiting for transfers between devices: 49.3 us -> 67.6 us  [the longest x2 33 us: to_plane_seq(): lax.all_to_all(value, 'seq', split_axis=0, concat_axis=0, tiled=True)]
    ppermute x95 -> x85, starting transfers between devices: 105 us -> 118 us  [swap(): return lax.ppermute(value, axis, [(i, i ^ step) for i in range(count)])]
    convert_element_type x14 -> x10, other arithmetic: 30.5 us -> 42.1 us  [the longest x4 23.2 us: __init__(): self.total(slice(2, None), 1).astype(BF16)]
    unnamed x200 -> x196, local copies, waits for them, and re-layouts: 73.9 us -> 62.5 us
  transfers between devices with their start and end apart: 108 -> 100, of which waited for: 35 -> 33; matrix products, arithmetic and copies ran while one was open for 28% -> 25% of each run, Pallas kernels for 28% -> 32%
where the time goes in v2:
time: 1240 us; the launch traced here: 1230 us
  Pallas kernels  396 us (32%)
  waiting for transfers between devices  278 us (22%)
  local copies, waits for them, and re-layouts  190 us (15%)
  starting transfers between devices  171 us (14%)
  other arithmetic  92.2 us (7%)
  matrix products  46.6 us (4%)
  blocking collectives  40.5 us (3%)
  between operations  18.6 us (2%)
    ppermute x85, waiting for transfers between devices, swap(): return lax.ppermute(value, axis, [(i, i ^ step) for i in range(count)])  177 us
    pallas_call x2, Pallas kernels, run_expert(): pl.pallas_call(functools.partial(expert_kernel, wide, narrow, more, len(f...  174 us
    ppermute x85, starting transfers between devices, swap(): return lax.ppermute(value, axis, [(i, i ^ step) for i in range(count)])  118 us
    pallas_call x2, Pallas kernels, expert_weight_grad(): pl.pallas_call(functools.partial(weight_kernel, narrow), grid=(model // b...  77.4 us
    unnamed x196, local copies, waits for them, and re-layouts  62.5 us
    dot_general x7, matrix products, dot(): lax.dot_general(a, b, (((ca,), (cb,)), ((), ())), preferred_element_type=...  46.6 us
    pallas_call x1, Pallas kernels, attend_back(): pl.pallas_call(functools.partial(attend_back_kernel, 256), grid=(seqs, wi...  41 us
    gather x13, local copies, waits for them, and re-layouts, reorder(): return jnp.take(stacked, index, axis=axis, mode='clip')  40.7 us
  transfers between devices with their start and end apart: 100, of which 33 were waited for; matrix products, arithmetic and copies ran while one was open for 25% of the time, Pallas kernels for 32%

profile of v2, /device:TPU:0, one launch (start us, length us, event | category | flops | bytes accessed | tf_op | source)
XLA Modules:
  0.0 1232.4 jit_solution(10254566890010492705)
XLA Ops:
  50.0 16.1 %collective-permute-done.16 = bf16[64,2048]{1,0:T(8,128)(2,1)S(1)} collective-permute-done((bf16[64,2048]{1,0:T(8,128)(2,1)S(1)}, bf16[64,2048]{1,0:T(8,128)(2,1)S(1)}, u32[]{:S(2)}, u32[]{:S(2)}) %collective-permute-start.16) | collective-permute-done | bytes 262176 | tf_op jit(solution)/shard_map/gather_wo/ppermute | solution.py:58
  82.1 19.6 %all-to-all-start.1 = ((bf16[4,96,2048]{2,1,0:T(8,128)(2,1)}), bf16[4,96,2048]{2,1,0:T(8,128)(2,1)S(1)}, u32[]{:S(2)}, u32[]{:S(2)}) async-start(bf16[4,96,2048]{2,1,0:T(8,128)(2,1)} %bitcast.2), calls=%async_computation.1 | async-start | bytes 3145728 | tf_op jit(solution)/shard_map/remap_x/all_to_all | solution.py:146
  122.8 25.3 %all-to-all-done.1 = bf16[4,96,2048]{2,1,0:T(8,128)(2,1)S(1)} async-done(((bf16[4,96,2048]{2,1,0:T(8,128)(2,1)}), bf16[4,96,2048]{2,1,0:T(8,128)(2,1)S(1)}, u32[]{:S(2)}, u32[]{:S(2)}) %all-to-all-start.1) | async-done | bytes 1572896 | tf_op jit(solution)/shard_map/remap_x/all_to_all | solution.py:146
  152.8 22.2 %all_gather.15 = f32[160,128]{1,0:T(8,128)S(1)} all-gather(f32[40,128]{1,0:T(8,128)S(1)} %pad_bitcast_fusion), channel_id=1, replica_groups=mesh['seq'=4,'fsdp'=8] {'seq'}, dimensions={0}, use_global_device_ids=true | all-gather | bytes 102400 | tf_op jit(solution)/shard_map/gather_small/all_gather | solution.py:614
  175.0 18.3 %all_gather.16 = f32[1280,128]{1,0:T(8,128)S(1)} all-gather(f32[160,128]{1,0:T(8,128)S(1)} %all_gather.15), channel_id=1, replica_groups=mesh['seq'=4,'fsdp'=8] {'fsdp'}, dimensions={0}, use_global_device_ids=true | all-gather | bytes 737280 | tf_op jit(solution)/shard_map/gather_small/all_gather | solution.py:615
  203.9 13.7 %collective-permute-done.5 = bf16[192,2048]{1,0:T(8,128)(2,1)} collective-permute-done((bf16[192,2048]{1,0:T(8,128)(2,1)}, bf16[192,2048]{1,0:T(8,128)(2,1)}, u32[]{:S(2)}, u32[]{:S(2)}) %collective-permute-start.5) | collective-permute-done | bytes 786464 | tf_op jit(solution)/shard_map/gather_x/ppermute | solution.py:58
  234.4 20.9 %project.1 = (bf16[3072,2048]{1,0:T(8,128)(2,1)}, bf16[3072,256]{1,0:T(8,128)(2,1)}, bf16[3072,256]{1,0:T(8,128)(2,1)}, bf16[3072,256]{1,0:T(8,128)(2,1)}, f32[3072,256]{1,0:T(8,128)}, /*index=5*/f32[3072,256]{1,0:T(8,128)}) custom-call(bf16[3072,2048]{1,0:T(8,128)(2,1)} %bitcast.362, f32[1,2048]{1,0:T(1,128)} %bitcast.450, ...), custom_call_target="tpu_custom_call" | custom-call | flops 1000 | bytes 1000 | tf_op jit(solution)/shard_map/project/pallas_call | solution.py:203
  255.3 23.0 %attend.1 = bf16[2,1536,256]{2,1,0:T(8,128)(2,1)} custom-call(bf16[2,1536,256]{2,1,0:T(8,128)(2,1)} %bitcast.438, bf16[2,1536,256]{2,1,0:T(8,128)(2,1)} %bitcast.440, bf16[2,1536,256]{2,1,0:T(8,128)(2,1)} %bitcast.442, s32[2,1536,1]{2,1,0:T(8,128)} %convert_add_fusion.1.rd_ref, s32[2,1,1536]{2,1,0:T(1,128)} %fusion.34.cd_ref), custom_call_target="tpu_custom_call" | custom-call | flops 1000 | bytes 1000 | tf_op jit(solution)/shard_map/attend/pallas_call | solution.py:283
  347.0 17.2 %collective-permute-done.27 = bf16[384,2048]{1,0:T(8,128)(2,1)} collective-permute-done((bf16[384,2048]{1,0:T(8,128)(2,1)}, bf16[384,2048]{1,0:T(8,128)(2,1)}, u32[]{:S(2)}, u32[]{:S(2)}) %collective-permute-start.27) | collective-permute-done | bytes 1572896 | tf_op jit(solution)/shard_map/gather_xn/ppermute | solution.py:58
  414.7 17.0 %collective-permute-done.35 = bf16[384,2048]{1,0:T(8,128)(2,1)S(1)} collective-permute-done((bf16[384,2048]{1,0:T(8,128)(2,1)S(1)}, bf16[384,2048]{1,0:T(8,128)(2,1)S(1)}, u32[]{:S(2)}, u32[]{:S(2)}) %collective-permute-start.35) | collective-permute-done | bytes 1572896 | tf_op jit(solution)/shard_map/gather_dz/ppermute | solution.py:58
  463.3 86.0 %expert.2 = (bf16[2048,2048]{1,0:T(8,128)(2,1)}, bf16[2048,2048]{1,0:T(8,128)(2,1)}, bf16[2048,1024]{1,0:T(8,128)(2,1)}, bf16[2048,2048]{1,0:T(8,128)(2,1)}, bf1...) custom-call(s32[8,1,384]{2,1,0:T(1,128)} %get-tuple-element.322.rank, ...), custom_call_target="tpu_custom_call" | custom-call | flops 1000 | bytes 1000 | tf_op jit(solution)/shard_map/expert0/expert/pallas_call | solution.py:478
  549.3 38.3 %expert_weight_grad.2 = bf16[2048,3072]{1,0:T(8,128)(2,1)} custom-call(bf16[2048,2048]{1,0:T(8,128)(2,1)} %get-tuple-element.100.xg_ref, bf16[2048,2048]{1,0:T(8,128)(2,1)} %get-tuple-element.101.dy_ref, bf16[2048,2048]{1,0:T(8,128)(2,1)} %get-tuple-element.102.dgu_ref, bf16[2048,1024]{1,0:T(8,128)(2,1)} %get-tuple-element.103.hm_ref), custom_call_target="tpu_custom_call" | custom-call | flops 1000 | bytes 1000 | tf_op jit(solution)/shard_map/expert0/expert_weight_grad/pallas_call | solution.py:511
  589.1 20.5 %all-gather.8.cloned.1.call-done = bf16[1,2048,3072]{2,1,0:T(8,128)(2,1)} async-done(((bf16[1,512,3072]{2,1,0:T(8,128)(2,1)}), bf16[1,2048,3072]{2,1,0:T(8,128)(2,1)}) %all-gather.8.cloned.1.call-update) | async-done | bytes 12582928 | tf_op jit(solution)/shard_map/gather_experts/all_gather | solution.py:645
  609.7 87.6 %expert.3 = (bf16[2048,2048]{1,0:T(8,128)(2,1)}, bf16[2048,2048]{1,0:T(8,128)(2,1)}, bf16[2048,1024]{1,0:T(8,128)(2,1)}, bf16[2048,2048]{1,0:T(8,128)(2,1)}, bf1...) custom-call(s32[8,1,384]{2,1,0:T(1,128)} %get-tuple-element.323.rank, ...), custom_call_target="tpu_custom_call" | custom-call | flops 1000 | bytes 1000 | tf_op jit(solution)/shard_map/expert1/expert/pallas_call | solution.py:478
  726.3 39.0 %expert_weight_grad.3 = bf16[2048,3072]{1,0:T(8,128)(2,1)} custom-call(bf16[2048,2048]{1,0:T(8,128)(2,1)} %get-tuple-element.116.xg_ref, bf16[2048,2048]{1,0:T(8,128)(2,1)} %get-tuple-element.117.dy_ref, bf16[2048,2048]{1,0:T(8,128)(2,1)} %get-tuple-element.118.dgu_ref, bf16[2048,1024]{1,0:T(8,128)(2,1)} %get-tuple-element.119.hm_ref), custom_call_target="tpu_custom_call" | custom-call | flops 1000 | bytes 1000 | tf_op jit(solution)/shard_map/expert1/expert_weight_grad/pallas_call | solution.py:511
  774.2 15.3 %collective-permute-done.52 = bf16[192,2048]{1,0:T(8,128)(2,1)} collective-permute-done((bf16[192,2048]{1,0:T(8,128)(2,1)}, bf16[192,2048]{1,0:T(8,128)(2,1)}, u32[]{:S(2)}, u32[]{:S(2)}) %collective-permute-start.52) | collective-permute-done | bytes 786464 | tf_op jit(solution)/shard_map/scatter_dxn/ppermute | solution.py:58
  810.9 20.4 %all-to-all-done.5 = bf16[8,384,256]{2,1,0:T(8,128)(2,1)} async-done(((bf16[8,384,256]{2,1,0:T(8,128)(2,1)}), bf16[8,384,256]{2,1,0:T(8,128)(2,1)}, u32[]{:S(2)}, u32[]{:S(2)}) %all-to-all-start.5) | async-done | bytes 1572896 | tf_op jit(solution)/shard_map/do_exchange/all_to_all | solution.py:722
  844.7 41.0 %attend_back.1 = (bf16[2,1536,256]{2,1,0:T(8,128)(2,1)}, bf16[2,1536,256]{2,1,0:T(8,128)(2,1)}, bf16[2,1536,256]{2,1,0:T(8,128)(2,1)}) custom-call(bf16[2,1536,256]{2,1,0:T(8,128)(2,1)} %bitcast.439, bf16[2,1536,256]{2,1,0:T(8,128)(2,1)} %bitcast.441, bf16[2,1536,256]{2,1,0:T(8,128)(2,1)} %bitcast.443, bf16[2,1536,256]{2,1,0:T(8,128)(2,1)} %bitcast.435, ...), custom_call_target="tpu_custom_call" | custom-call | flops 40000000000 | bytes 1000 | tf_op jit(solution)/shard_map/attend_back/pallas_call | solution.py:300
  892.3 28.3 %project_back.1 = (bf16[3072,768]{1,0:T(8,128)(2,1)}, f32[8,128]{1,0:T(8,128)}, bf16[4,8,48,2048]{3,2,1,0:T(8,128)(2,1)}, bf16[4,8,48,2048]{3,2,1,0:T(8,128)(2,1)}) custom-call(bf16[3072,256]{1,0:T(8,128)(2,1)} %bitcast.454, bf16[3072,256]{1,0:T(8,128)(2,1)} %bitcast.455, bf16[3072,256]{1,0:T(8,128)(2,1)} %bitcast.456, ...), custom_call_target="tpu_custom_call" | custom-call | flops 28000000000 | bytes 1000 | tf_op jit(solution)/shard_map/project_back/pallas_call | solution.py:354
  944.1 15.7 %convolution_convert_fusion.1 = bf16[2048,768]{1,0:T(8,128)(2,1)} fusion(bf16[3072,2048]{1,0:T(8,128)(2,1)} %get-tuple-element.143, bf16[3072,768]{1,0:T(8,128)(2,1)} %get-tuple-element.138), kind=kOutput, calls=%fused_computation.20 | convolution fusion | flops 9665249280 | bytes 20447232 | tf_op jit(solution)/shard_map/weight_grads/dot_general | solution.py:42
  959.7 15.6 %adam_expert.2 = (f32[2,512,3072]{2,1,0:T(8,128)}, f32[2,512,3072]{2,1,0:T(8,128)}, f32[2,512,3072]{2,1,0:T(8,128)}) custom-call(bf16[2,512,3072]{2,1,0:T(8,128)(2,1)} %w_ref.3, bf16[512,3072]{1,0:T(8,128)(2,1)} %reduce-scatter.4.cloned.1.call-done.g_ref, f32[2,512,3072]{2,1,0:T(8,128)} %m_ref.3, f32[2,512,3072]{2,1,0:T(8,128)} %v_ref.3), custom_call_target="tpu_custom_call" | custom-call | flops 1000 | bytes 1000 | tf_op jit(solution)/shard_map/weight_grads/adam_expert/pallas_call | solution.py:533
  1064.3 16.2 %adam_expert.3 = (f32[2,512,3072]{2,1,0:T(8,128)}, f32[2,512,3072]{2,1,0:T(8,128)}, f32[2,512,3072]{2,1,0:T(8,128)}) custom-call(bf16[2,512,3072]{2,1,0:T(8,128)(2,1)} %w_ref.3, bf16[512,3072]{1,0:T(8,128)(2,1)} %reduce-scatter.6.cloned.1.call-done.g_ref, f32[2,512,3072]{2,1,0:T(8,128)} %m_ref.3, ...), custom_call_target="tpu_custom_call", output_to_operand_aliasing={{0}: (4, {}), {1}: (5, {}), {2}: (6, {})} | custom-call | flops 1000 | bytes 1000 | tf_op jit(solution)/shard_map/adam_expert/pallas_call | solution.py:533
  1087.0 34.1 %collective-permute-start.75 = (f32[1160]{0:T(1024)S(1)}, f32[1160]{0:T(1024)S(1)}, u32[]{:S(2)}, u32[]{:S(2)}) collective-permute-start(f32[1160]{0:T(1024)S(1)} %pad_maximum_fusion.8), channel_id=1, source_target_pairs={{0,8},{8,0},{16,24},{24,16},{1,9},{9,1},{17,25},{25,17},{2,10},{10... | collective-permute-start | bytes 13928 | tf_op jit(solution)/shard_map/small_sum/ppermute | solution.py:58
  1148.8 33.4 %collective-permute-done.73 = bf16[64,2048]{1,0:T(8,128)(2,1)} collective-permute-done((bf16[64,2048]{1,0:T(8,128)(2,1)}, bf16[64,2048]{1,0:T(8,128)(2,1)}, u32[]{:S(2)}, u32[]{:S(2)}) %collective-permute-start.73) | collective-permute-done | bytes 262176 | tf_op jit(solution)/shard_map/scatter_wo/ppermute | solution.py:58
  (593 shorter events, 529.0 us)
Async XLA Ops:
  7.2 224.5 %all-gather.6.cloned.1.call-start = ((), (), s32[]{:S(2)}) async-start(), calls=%async_computation.12 | async-start | bytes 3932160 | tf_op jit(solution)/shard_map/gather_wqkv/all_gather | solution.py:606
  29.6 433.6 %all-gather.10.cloned.1.call-start = ((), (), s32[]{:S(2)}) async-start(), calls=%async_computation.17 | async-start | bytes 15728640 | tf_op jit(solution)/shard_map/gather_experts/all_gather | solution.py:645
  82.1 66.0 %all-to-all-start.1 = ((bf16[4,96,2048]{2,1,0:T(8,128)(2,1)}), bf16[4,96,2048]{2,1,0:T(8,128)(2,1)S(1)}, u32[]{:S(2)}, u32[]{:S(2)}) async-start(bf16[4,96,2048]{2,1,0:T(8,128)(2,1)} %bitcast.2), calls=%async_computation.1 | async-start | bytes 3145728 | tf_op jit(solution)/shard_map/remap_x/all_to_all | solution.py:146
  101.7 507.9 %all-gather.8.cloned.1.call-start = ((), (), s32[]{:S(2)}) async-start(), calls=%async_computation.16 | async-start | bytes 15728640 | tf_op jit(solution)/shard_map/gather_experts/all_gather | solution.py:645
  148.3 47.1 %collective-permute-start.1 = (bf16[384,2048]{1,0:T(8,128)(2,1)S(1)}, bf16[384,2048]{1,0:T(8,128)(2,1)}, u32[]{:S(2)}, u32[]{:S(2)}) collective-permute-start(bf16[384,2048]{1,0:T(8,128)(2,1)S(1)} %bitcast.370), channel_id=1, source_target_pairs={{0,2},{1,3},{2,0},{3,1},{4,6},{5,7},{6,4},{7,5},{8,10},{9,11},{10,... | collective-permute-start | bytes 4718600 | tf_op jit(solution)/shard_map/gather_x/ppermute | solution.py:58
  152.1 47.7 %collective-permute-start.3 = (bf16[384,2048]{1,0:T(8,128)(2,1)S(1)}, bf16[384,2048]{1,0:T(8,128)(2,1)}, u32[]{:S(2)}, u32[]{:S(2)}) collective-permute-start(bf16[384,2048]{1,0:T(8,128)(2,1)S(1)} %bitcast.371), channel_id=1, source_target_pairs={{0,4},{1,5},{2,6},{3,7},{4,0},{5,1},{6,2},{7,3},{8,12},{9,13},{10,... | collective-permute-start | bytes 4718600 | tf_op jit(solution)/shard_map/gather_x/ppermute | solution.py:58
  152.8 67.9 %collective-permute-start = (bf16[384,2048]{1,0:T(8,128)(2,1)S(1)}, bf16[384,2048]{1,0:T(8,128)(2,1)}, u32[]{:S(2)}, u32[]{:S(2)}) collective-permute-start(bf16[384,2048]{1,0:T(8,128)(2,1)S(1)} %bitcast.372), channel_id=1, source_target_pairs={{0,1},{1,0},{2,3},{3,2},{4,5},{5,4},{6,7},{7,6},{8,9},{9,8},{10,11... | collective-permute-start | bytes 4718600 | tf_op jit(solution)/shard_map/gather_x/ppermute | solution.py:58
  217.6 67.5 %collective-permute-start.22 = (bf16[256,2048]{1,0:T(8,128)(2,1)}, bf16[256,2048]{1,0:T(8,128)(2,1)}, u32[]{:S(2)}, u32[]{:S(2)}) collective-permute-start(bf16[256,2048]{1,0:T(8,128)(2,1)} %collective-permute-done.21), channel_id=1, source_target_pairs={{0,1},{1,0},{2,3},{3,2},{4,5},{5,4},{6,7},{7,6},{8,9},{9,8},{10,11... | collective-permute-start | bytes 3145736 | tf_op jit(solution)/shard_map/gather_wo/ppermute | solution.py:58
  220.7 69.1 %collective-permute-start.25 = (bf16[256,2048]{1,0:T(8,128)(2,1)}, bf16[256,2048]{1,0:T(8,128)(2,1)}, u32[]{:S(2)}, u32[]{:S(2)}) collective-permute-start(bf16[256,2048]{1,0:T(8,128)(2,1)} %constant_dynamic-update-slice_fusion.18), channel_id=1, source_target_pairs={{0,1},{1,0},{2,3},{3,2},{4,5},{5,4},{6,7},{7,6},{8,9},{9,8},{10,11... | collective-permute-start | bytes 3145736 | tf_op jit(solution)/shard_map/gather_wo/ppermute | solution.py:58
  321.5 42.7 %collective-permute-start.27 = (bf16[384,2048]{1,0:T(8,128)(2,1)}, bf16[384,2048]{1,0:T(8,128)(2,1)}, u32[]{:S(2)}, u32[]{:S(2)}) collective-permute-start(bf16[384,2048]{1,0:T(8,128)(2,1)} %multiply_convert_fusion), channel_id=1, source_target_pairs={{0,2},{1,3},{2,0},{3,1},{4,6},{5,7},{6,4},{7,5},{8,10},{9,11},{10,... | collective-permute-start | bytes 4718600 | tf_op jit(solution)/shard_map/gather_xn/ppermute | solution.py:58
  331.9 62.3 %all-to-all-start.3 = ((bf16[4,96,2048]{2,1,0:T(8,128)(2,1)}), bf16[4,96,2048]{2,1,0:T(8,128)(2,1)}, u32[]{:S(2)}, u32[]{:S(2)}) async-start(bf16[4,96,2048]{2,1,0:T(8,128)(2,1)} %bitcast.17), calls=%async_computation.3 | async-start | bytes 3145728 | tf_op jit(solution)/shard_map/remap_dz/all_to_all | solution.py:146
  336.3 508.4 %reduce-scatter.4.cloned.1.call-start = ((), (), s32[]{:S(2)}) async-start(), calls=%async_computation.13 | async-start | bytes 15728640 | tf_op jit(solution)/shard_map/expert0/reduce_scatter | solution.py:706
  337.4 46.4 %collective-permute-start.26 = (bf16[384,2048]{1,0:T(8,128)(2,1)}, bf16[384,2048]{1,0:T(8,128)(2,1)}, u32[]{:S(2)}, u32[]{:S(2)}) collective-permute-start(bf16[384,2048]{1,0:T(8,128)(2,1)} %multiply_convert_fusion), channel_id=1, source_target_pairs={{0,1},{1,0},{2,3},{3,2},{4,5},{5,4},{6,7},{7,6},{8,9},{9,8},{10,11... | collective-permute-start | bytes 4718600 | tf_op jit(solution)/shard_map/gather_xn/ppermute | solution.py:58
  404.6 50.0 %collective-permute-start.34 = (bf16[384,2048]{1,0:T(8,128)(2,1)S(1)}, bf16[384,2048]{1,0:T(8,128)(2,1)}, u32[]{:S(2)}, u32[]{:S(2)}) collective-permute-start(bf16[384,2048]{1,0:T(8,128)(2,1)S(1)} %bitcast.381), channel_id=1, source_target_pairs={{0,1},{1,0},{2,3},{3,2},{4,5},{5,4},{6,7},{7,6},{8,9},{9,8},{10,11... | collective-permute-start | bytes 4718600 | tf_op jit(solution)/shard_map/gather_dz/ppermute | solution.py:58
  717.6 47.7 %collective-permute-start.50 = (bf16[2,192,2048]{2,1,0:T(8,128)(2,1)}, bf16[2,192,2048]{2,1,0:T(8,128)(2,1)}, u32[]{:S(2)}, u32[]{:S(2)}) collective-permute-start(bf16[2,192,2048]{2,1,0:T(8,128)(2,1)} %get-tuple-element.113), channel_id=1, source_target_pairs={{0,2},{1,3},{2,0},{3,1},{4,6},{5,7},{6,4},{7,5},{8,10},{9,11},{10,... | collective-permute-start | bytes 4718600 | tf_op jit(solution)/shard_map/scatter_dxn/ppermute | solution.py:58
  719.2 46.1 %collective-permute-start.51 = (bf16[2,192,2048]{2,1,0:T(8,128)(2,1)}, bf16[2,192,2048]{2,1,0:T(8,128)(2,1)}, u32[]{:S(2)}, u32[]{:S(2)}) collective-permute-start(bf16[2,192,2048]{2,1,0:T(8,128)(2,1)} %get-tuple-element.114), channel_id=1, source_target_pairs={{0,4},{1,5},{2,6},{3,7},{4,0},{5,1},{6,2},{7,3},{8,12},{9,13},{10,... | collective-permute-start | bytes 4718600 | tf_op jit(solution)/shard_map/scatter_dxn/ppermute | solution.py:58
  810.3 254.0 %reduce-scatter.6.cloned.1.call-start = ((), (), s32[]{:S(2)}) async-start(), calls=%async_computation.14 | async-start | bytes 15728640 | tf_op jit(solution)/shard_map/expert1/reduce_scatter | solution.py:706
  843.9 41.8 %collective-permute-start.55 = (bf16[2,192,2048]{2,1,0:T(8,128)(2,1)}, bf16[2,192,2048]{2,1,0:T(8,128)(2,1)}, u32[]{:S(2)}, u32[]{:S(2)}) collective-permute-start(bf16[2,192,2048]{2,1,0:T(8,128)(2,1)} %get-tuple-element.125), channel_id=1, source_target_pairs={{0,2},{1,3},{2,0},{3,1},{4,6},{5,7},{6,4},{7,5},{8,10},{9,11},{10,... | collective-permute-start | bytes 4718600 | tf_op jit(solution)/shard_map/scatter_out/ppermute | solution.py:58
  930.1 82.6 %all-to-all-start.6 = ((bf16[4,96,2048]{2,1,0:T(8,128)(2,1)}), bf16[4,96,2048]{2,1,0:T(8,128)(2,1)S(1)}, u32[]{:S(2)}, u32[]{:S(2)}) async-start(bf16[4,96,2048]{2,1,0:T(8,128)(2,1)} %bitcast.140), calls=%async_computation.7 | async-start | bytes 3145728 | tf_op jit(solution)/shard_map/remap_out/all_to_all | solution.py:156
  933.7 248.5 %reduce-scatter.8.cloned.1.call-start = ((), (), s32[]{:S(2)}) async-start(), calls=%async_computation.15 | async-start | bytes 3932160 | tf_op jit(solution)/shard_map/scatter_wqkv/reduce_scatter | solution.py:765
  1053.6 88.2 %all-to-all-start.7 = ((bf16[4,96,2048]{2,1,0:T(8,128)(2,1)}), bf16[4,96,2048]{2,1,0:T(8,128)(2,1)S(1)}, u32[]{:S(2)}, u32[]{:S(2)}) async-start(bf16[4,96,2048]{2,1,0:T(8,128)(2,1)} %bitcast.146), calls=%async_computation.8 | async-start | bytes 3145728 | tf_op jit(solution)/shard_map/remap_grad/all_to_all | solution.py:156
  1087.0 54.8 %collective-permute-start.75 = (f32[1160]{0:T(1024)S(1)}, f32[1160]{0:T(1024)S(1)}, u32[]{:S(2)}, u32[]{:S(2)}) collective-permute-start(f32[1160]{0:T(1024)S(1)} %pad_maximum_fusion.8), channel_id=1, source_target_pairs={{0,8},{8,0},{16,24},{24,16},{1,9},{9,1},{17,25},{25,17},{2,10},{10... | collective-permute-start | bytes 13928 | tf_op jit(solution)/shard_map/small_sum/ppermute | solution.py:58
  1133.1 49.1 %collective-permute-start.73 = (bf16[64,2048]{1,0:T(8,128)(2,1)}, bf16[64,2048]{1,0:T(8,128)(2,1)}, u32[]{:S(2)}, u32[]{:S(2)}) collective-permute-start(bf16[64,2048]{1,0:T(8,128)(2,1)} %get-tuple-element.288), channel_id=1, source_target_pairs={{0,16},{8,24},{16,0},{24,8},{1,17},{9,25},{17,1},{25,9},{2,18},{10... | collective-permute-start | bytes 786440 | tf_op jit(solution)/shard_map/scatter_wo/ppermute | solution.py:58
  1143.7 79.0 %all-to-all-start.8 = ((bf16[8,48,4096]{2,1,0:T(8,128)(2,1)}), bf16[8,48,4096]{2,1,0:T(8,128)(2,1)S(1)}, u32[]{:S(2)}, u32[]{:S(2)}) async-start(bf16[8,48,4096]{2,1,0:T(8,128)(2,1)} %bitcast.159), calls=%async_computation.10 | async-start | bytes 6291456 | tf_op jit(solution)/shard_map/remap/all_to_all | solution.py:162
  (146 other events, 2753.8 us)
Sparse Core Ops, SparseCore 0:
  29.8 108.4 all-gather.5
  139.8 252.2 all-gather.9
  393.7 215.9 all-gather.7
  611.9 210.0 reduce-scatter.3
  824.1 240.1 reduce-scatter.5
  1066.5 110.2 reduce-scatter.7

commit v3 on v2

--- a/solution.py
+++ b/solution.py
@@ -491,29 +491,31 @@
     return xg, dy, hm, dgu, rest[: len(form)], rest[len(form) : -1], rest[-1][:, 0]
 
 
-def weight_kernel(narrow, xg_ref, dy_ref, dgu_ref, hm_ref, out_ref, flip_ref):
-    feed = hm_ref.shape[1]
-    for src, other, base, width in ((xg_ref, dgu_ref, 0, 2 * feed), (dy_ref, hm_ref, 2 * feed, feed)):
+def weight_kernel(narrow, xg_ref, dy_ref, dgu_ref, hm_ref, *refs):
+    *out_refs, flip_ref = refs
+    base = dgu_ref.shape[1] if len(out_refs) == 1 else 0
+    for src, other, out_ref, start in ((xg_ref, dgu_ref, out_refs[0], 0), (dy_ref, hm_ref, out_refs[-1], base)):
         flip_ref[...] = src[...].T
         def step(i, _):
             cols = pl.ds(pl.multiple_of(i * narrow, narrow), narrow)
-            to = pl.ds(pl.multiple_of(base + i * narrow, narrow), narrow)
+            to = pl.ds(pl.multiple_of(start + i * narrow, narrow), narrow)
             out_ref[:, to] = dot(flip_ref[...], other[:, cols], 1, 0).astype(BF16)
             return 0
-        lax.fori_loop(0, width // narrow, step, 0)
-
-
-def expert_weight_grad(xg, dy, dgu, hm, block=512, narrow=1024):
+        lax.fori_loop(0, other.shape[1] // narrow, step, 0)
+
+
+def expert_weight_grad(xg, dy, dgu, hm, parts, block=512, narrow=1024):
     slots, model = xg.shape
     feed = hm.shape[1]
+    widths = (3 * feed,) if parts == 1 else (2 * feed, feed)
     cut = pl.BlockSpec((slots, block), lambda i: (0, i))
     def whole(c): return pl.BlockSpec((slots, c), lambda i: (0, 0), pipeline_mode=pl.Buffered(1))
     return pl.pallas_call(
         functools.partial(weight_kernel, narrow),
         grid=(model // block,),
         in_specs=[cut, cut, whole(2 * feed), whole(feed)],
-        out_specs=pl.BlockSpec((block, 3 * feed), lambda i: (i, 0)),
-        out_shape=jax.ShapeDtypeStruct((model, 3 * feed), BF16),
+        out_specs=[pl.BlockSpec((block, c), lambda i: (i, 0)) for c in widths],
+        out_shape=[jax.ShapeDtypeStruct((model, c), BF16) for c in widths],
         scratch_shapes=[pltpu.VMEM((block, slots), BF16)],
         compiler_params=pltpu.CompilerParams(vmem_limit_bytes=VMEM_LIMIT),
         cost_estimate=BRIEF,
@@ -525,15 +527,16 @@
     new = adam_step(w_ref[0], g_ref[...], m_ref[0], v_ref[0], rate)
     m_out[0], v_out[0], w_out[0] = new
 
-def adam_expert(e, weight, grad, first, second, old, rate, block=64):
-    _, rows, cols = weight.shape
-    one = pl.BlockSpec((1, block, cols), lambda i: (e, i, 0))
+def adam_expert(e, base, weight, grad, first, second, old, rate, block=128, wide=1024):
+    rows, cols = grad.shape
+    one = pl.BlockSpec((1, block, wide), lambda i, j: (e, i, base // wide + j))
     out = jax.ShapeDtypeStruct(weight.shape, F32)
     old = tuple(old or ())
     return pl.pallas_call(
         functools.partial(adam_kernel, rate),
-        grid=(rows // block,),
-        in_specs=[one, pl.BlockSpec((block, cols), lambda i: (i, 0)), one, one] + [pl.BlockSpec(memory_space=pl.ANY)] * len(old),
+        grid=(rows // block, cols // wide),
+        in_specs=[one, pl.BlockSpec((block, wide), lambda i, j: (i, j)), one, one]
+        + [pl.BlockSpec(memory_space=pl.ANY)] * len(old),
         out_specs=[one] * 3,
         out_shape=[out] * 3,
         input_output_aliases={4 + i: i for i in range(len(old))},
@@ -692,7 +695,7 @@
     sums, gate_back, expert_share, held = (), [], [], None
     for e in range(EXP_DEV):
         with jax.named_scope(f"expert{e}"):
-            w = expert_full[e] if held is None else after(expert_full[e], held)
+            w = expert_full[e] if held is None else after(expert_full[e], *held)
             xg, dy, hm, dgu, mixed, dxn, dgate = run_expert(
                 rank[:, e], gates_mine[:, :, e], xn_all, dz_all, w, sums, capacity
             )
@@ -702,8 +705,10 @@
                 gate_parts = exchange(pieces(jnp.stack(gate_back, axis=2)), "fsdp", fsdp_count)
                 dxn = Scatter(fsdp_count, *by_owner(dxn, blocks), hold=gate_parts)
                 xg = after(xg, *dxn.sends)
-            held = expert_weight_grad(xg, dy, dgu, hm)
-            expert_share.append(lax.psum_scatter(held, "seq", scatter_dimension=0, tiled=True))
+            held = expert_weight_grad(xg, dy, dgu, hm, 1 if e < EXP_DEV - 1 else 2)
+            if e < EXP_DEV - 1:
+                expert_share.append(lax.psum_scatter(held[0], "seq", scatter_dimension=0, tiled=True))
+    last_up = lax.psum_scatter(held[0], "seq", scatter_dimension=0, tiled=True)
 
     with jax.named_scope("router_back"):
         gate_grad = reorder(jnp.stack(gate_parts, axis=1), around, 1).reshape(rows, experts)
@@ -711,7 +716,7 @@
         gate_grad = jnp.where(chosen_own, gate_grad, 0.0)
         dlog = (gates_own * (gate_grad - jnp.sum(gates_own * gate_grad, axis=1, keepdims=True))).astype(BF16)
     with jax.named_scope("scatter_dxn"):
-        dxn_own = dxn.second(held).third()
+        dxn_own = dxn.second(*held).third()
     dxn_own = dxn_own + dot(dlog, full_router, 1, 1)
     middle_back, ffn_gain_grad = norm_back(dxn_own, middle, ffn_gain)
     middle_grad = dz_low.astype(F32) + middle_back
@@ -743,11 +748,15 @@
         layer_out = from_plane_seq(layer_low, seq_count, fsdp_count)
     with jax.named_scope("weight_grads"):
         in_grad = dot(after(a_all, *da.sends), d_proj, 0, 0).astype(BF16)
-        expert_new = adam_expert(
-            0, expert_weight, after(expert_share[0], *da.sends), expert_first, expert_second, None, RATE_EXPERT
-        )
+        in_share = lax.psum_scatter(in_grad, "seq", scatter_dimension=0, tiled=True)
+        moments = (expert_first, expert_second)
+        expert_new = None
+        for e in range(EXP_DEV - 1):
+            share = after(expert_share[e], *da.sends)
+            expert_new = adam_expert(e, 0, expert_weight, share, *moments, expert_new, RATE_EXPERT)
     with jax.named_scope("scatter_da"):
         da = da.second(in_grad, expert_new[0])
+    last_down = lax.psum_scatter(after(held[1], *da.lasts), "seq", scatter_dimension=0, tiled=True)
     with jax.named_scope("weight_grads"):
         out_grad = dot(after(o_own, *da.lasts), db, 0, 0).astype(BF16)
         out_grad = out_grad.reshape(seq_count, fsdp_count, shard, model)
@@ -760,9 +769,6 @@
     input_low = (middle_grad + input_back).astype(BF16)
     with jax.named_scope("remap_grad"):
         input_grad = from_plane_seq(input_low, seq_count, fsdp_count)
-    with jax.named_scope("scatter_wqkv"):
-        in_grad = after(in_grad, input_low)
-        in_share = lax.psum_scatter(in_grad, "seq", scatter_dimension=0, tiled=True)
     with jax.named_scope("small_sum"):
         router_grad = dot(normed, dlog, 0, 0)
         small = jnp.concatenate(
@@ -783,40 +789,35 @@
         small_parts = [own_part(planes[m]) for m in range(seq_count)]
     with jax.named_scope("scatter_wo"):
         out_grad = Scatter(fsdp_count, out_grad[0], after(out_grad[1], input_low), hold=small_parts)
-    with jax.named_scope("small_sum"):
-        small_parts = exchange(small_parts, "seq", seq_count)
-    for e in range(1, EXP_DEV):
-        expert_new = adam_expert(
-            e,
-            expert_weight,
-            after(expert_share[e], *out_grad.sends),
-            expert_first,
-            expert_second,
-            expert_new,
-            RATE_EXPERT,
-        )
+    last = EXP_DEV - 1
+    expert_new = adam_expert(
+        last, 0, expert_weight, after(last_up, *out_grad.sends), *moments, expert_new, RATE_EXPERT
+    )
     with jax.named_scope("scatter_wo"):
         out_grad = out_grad.second(expert_new[0])
         out_share = out_grad.third().astype(BF16)
     with jax.named_scope("scatter_wo"):
-        out_parts = reorder(out_share.reshape(seq_count, shard, model), planes)
-        out_parts = exchange(list(out_parts), "seq", seq_count)
+        out_sent = reorder(out_share.reshape(seq_count, shard, model), planes)
+        out_parts = exchange(list(out_sent), "seq", seq_count)
     with jax.named_scope("scatter_wqkv"):
-        in_share, *waiting = lax.optimization_barrier((in_share, *out_parts, *small_parts))
-        in_share = reorder(in_share.reshape(fsdp_count, shard, 3 * width), around)
+        in_share = after(in_share, out_sent)
+        in_share = sent = reorder(in_share.reshape(fsdp_count, shard, 3 * width), around)
         in_share = reorder(jnp.stack(exchange(list(in_share), "fsdp", fsdp_count)), around)
         in_share = in_share.reshape(fsdp_count, shard, 3, width).transpose(1, 2, 0, 3).reshape(shard, 3 * model)
     with jax.named_scope("remap"):
         both = jnp.concatenate([input_grad, layer_out], axis=1)
-        both = from_plane_fsdp(after(both, *out_grad.lasts), fsdp_count)
+        both = from_plane_fsdp(after(both, sent), fsdp_count)
         input_grad, layer_out = both[:, :model].astype(F32), both[:, model:]
-    out_share = sum(p.astype(F32) for p in waiting[:seq_count])
-    small_own = sum(waiting[seq_count:])
+    out_share = sum(p.astype(F32) for p in out_parts)
+    small_own = sum(exchange(list(lax.optimization_barrier((*small_parts, in_share))[:-1]), "seq", seq_count))
     router_share, gain_share = small_own[:own_router].reshape(shard, experts), small_own[own_router:]
 
     attn_share = jnp.concatenate([in_share.astype(F32), out_share], axis=1)
     attn_new = adam_step(attn_weight, attn_share, attn_first, attn_second, RATE_ATTN)
     router_new = adam_step(router_weight, router_share, router_first, router_second, RATE_ROUTER)
+    expert_new = adam_expert(
+        last, 2 * FFE, expert_weight, after(last_down, attn_new[0]), *moments, expert_new, RATE_EXPERT
+    )
     gain_new = adam_step(gain_values, gain_share, gain_first, gain_second, RATE_GAIN)
     return (layer_out[None], input_grad[None], *attn_new, *router_new, *gain_new, *expert_new)
 

time: 1240 us -> 1220 us (0.984)
  starting transfers between devices: 171 us -> 129 us
  waiting for transfers between devices: 278 us -> 291 us
    ppermute x85, starting transfers between devices: 118 us -> 76.4 us  [swap(): return lax.ppermute(value, axis, [(i, i ^ step) for i in range(count)])]
    all_to_all x2, waiting for transfers between devices: 5.57 us -> 26.8 us  [from_plane_seq(): lax.all_to_all(value, 'seq', split_axis=0, concat_axis=0, tiled=True)]
    pallas_call x2 -> x3, Pallas kernels: 31.8 us -> 35.9 us  [adam_expert(): pl.pallas_call(functools.partial(adam_kernel, rate), grid=(rows // block,...]
    unnamed x196 -> x200, local copies, waits for them, and re-layouts: 62.5 us -> 62.6 us
  transfers between devices with their start and end apart: 100 -> 101, of which waited for: 33 -> 36; matrix products, arithmetic and copies ran while one was open for 25% -> 26% of each run, Pallas kernels for 32% -> 33%
where the time goes in v3:
time: 1220 us; the launch traced here: 1200 us
  Pallas kernels  399 us (33%)
  waiting for transfers between devices  291 us (24%)
  local copies, waits for them, and re-layouts  181 us (15%)
  starting transfers between devices  129 us (11%)
  other arithmetic  96.9 us (8%)
  matrix products  46.8 us (4%)
  blocking collectives  40.5 us (3%)
  between operations  18.9 us (2%)
    ppermute x85, waiting for transfers between devices, swap(): return lax.ppermute(value, axis, [(i, i ^ step) for i in range(count)])  175 us
    pallas_call x2, Pallas kernels, run_expert(): pl.pallas_call(functools.partial(expert_kernel, wide, narrow, more, len(f...  174 us
    pallas_call x2, Pallas kernels, expert_weight_grad(): pl.pallas_call(functools.partial(weight_kernel, narrow), grid=(model // b...  76.6 us
    ppermute x85, starting transfers between devices, swap(): return lax.ppermute(value, axis, [(i, i ^ step) for i in range(count)])  76.4 us
    unnamed x200, local copies, waits for them, and re-layouts  62.6 us
    dot_general x7, matrix products, dot(): lax.dot_general(a, b, (((ca,), (cb,)), ((), ())), preferred_element_type=...  46.8 us
    pallas_call x1, Pallas kernels, attend_back(): pl.pallas_call(functools.partial(attend_back_kernel, 256), grid=(seqs, wi...  41 us
    gather x13, local copies, waits for them, and re-layouts, reorder(): return jnp.take(stacked, index, axis=axis, mode='clip')  38.6 us
  transfers between devices with their start and end apart: 101, of which 36 were waited for; matrix products, arithmetic and copies ran while one was open for 26% of the time, Pallas kernels for 33%

profile of v3, /device:TPU:0, one launch (start us, length us, event | category | flops | bytes accessed | tf_op | source)
XLA Modules:
  0.0 1203.2 jit_solution(15600736530289131472)
XLA Ops:
  50.0 16.1 %collective-permute-done.16 = bf16[64,2048]{1,0:T(8,128)(2,1)S(1)} collective-permute-done((bf16[64,2048]{1,0:T(8,128)(2,1)S(1)}, bf16[64,2048]{1,0:T(8,128)(2,1)S(1)}, u32[]{:S(2)}, u32[]{:S(2)}) %collective-permute-start.16) | collective-permute-done | bytes 262176 | tf_op jit(solution)/shard_map/gather_wo/ppermute | solution.py:58
  82.1 19.7 %all-to-all-start.1 = ((bf16[4,96,2048]{2,1,0:T(8,128)(2,1)}), bf16[4,96,2048]{2,1,0:T(8,128)(2,1)S(1)}, u32[]{:S(2)}, u32[]{:S(2)}) async-start(bf16[4,96,2048]{2,1,0:T(8,128)(2,1)} %bitcast.2), calls=%async_computation.1 | async-start | bytes 3145728 | tf_op jit(solution)/shard_map/remap_x/all_to_all | solution.py:146
  122.9 25.2 %all-to-all-done.1 = bf16[4,96,2048]{2,1,0:T(8,128)(2,1)S(1)} async-done(((bf16[4,96,2048]{2,1,0:T(8,128)(2,1)}), bf16[4,96,2048]{2,1,0:T(8,128)(2,1)S(1)}, u32[]{:S(2)}, u32[]{:S(2)}) %all-to-all-start.1) | async-done | bytes 1572896 | tf_op jit(solution)/shard_map/remap_x/all_to_all | solution.py:146
  152.8 22.3 %all_gather.15 = f32[160,128]{1,0:T(8,128)S(1)} all-gather(f32[40,128]{1,0:T(8,128)S(1)} %pad_bitcast_fusion), channel_id=1, replica_groups=mesh['seq'=4,'fsdp'=8] {'seq'}, dimensions={0}, use_global_device_ids=true | all-gather | bytes 102400 | tf_op jit(solution)/shard_map/gather_small/all_gather | solution.py:617
  175.1 18.2 %all_gather.16 = f32[1280,128]{1,0:T(8,128)S(1)} all-gather(f32[160,128]{1,0:T(8,128)S(1)} %all_gather.15), channel_id=1, replica_groups=mesh['seq'=4,'fsdp'=8] {'fsdp'}, dimensions={0}, use_global_device_ids=true | all-gather | bytes 737280 | tf_op jit(solution)/shard_map/gather_small/all_gather | solution.py:618
  203.9 13.7 %collective-permute-done.5 = bf16[192,2048]{1,0:T(8,128)(2,1)} collective-permute-done((bf16[192,2048]{1,0:T(8,128)(2,1)}, bf16[192,2048]{1,0:T(8,128)(2,1)}, u32[]{:S(2)}, u32[]{:S(2)}) %collective-permute-start.5) | collective-permute-done | bytes 786464 | tf_op jit(solution)/shard_map/gather_x/ppermute | solution.py:58
  234.4 20.9 %project.1 = (bf16[3072,2048]{1,0:T(8,128)(2,1)}, bf16[3072,256]{1,0:T(8,128)(2,1)}, bf16[3072,256]{1,0:T(8,128)(2,1)}, bf16[3072,256]{1,0:T(8,128)(2,1)}, f32[3072,256]{1,0:T(8,128)}, /*index=5*/f32[3072,256]{1,0:T(8,128)}) custom-call(bf16[3072,2048]{1,0:T(8,128)(2,1)} %bitcast.365, f32[1,2048]{1,0:T(1,128)} %bitcast.453, ...), custom_call_target="tpu_custom_call" | custom-call | flops 1000 | bytes 1000 | tf_op jit(solution)/shard_map/project/pallas_call | solution.py:203
  255.3 23.0 %attend.1 = bf16[2,1536,256]{2,1,0:T(8,128)(2,1)} custom-call(bf16[2,1536,256]{2,1,0:T(8,128)(2,1)} %bitcast.441, bf16[2,1536,256]{2,1,0:T(8,128)(2,1)} %bitcast.443, bf16[2,1536,256]{2,1,0:T(8,128)(2,1)} %bitcast.445, s32[2,1536,1]{2,1,0:T(8,128)} %convert_add_fusion.1.rd_ref, s32[2,1,1536]{2,1,0:T(1,128)} %fusion.36.cd_ref), custom_call_target="tpu_custom_call" | custom-call | flops 1000 | bytes 1000 | tf_op jit(solution)/shard_map/attend/pallas_call | solution.py:283
  346.9 17.3 %collective-permute-done.27 = bf16[384,2048]{1,0:T(8,128)(2,1)} collective-permute-done((bf16[384,2048]{1,0:T(8,128)(2,1)}, bf16[384,2048]{1,0:T(8,128)(2,1)}, u32[]{:S(2)}, u32[]{:S(2)}) %collective-permute-start.27) | collective-permute-done | bytes 1572896 | tf_op jit(solution)/shard_map/gather_xn/ppermute | solution.py:58
  414.7 17.0 %collective-permute-done.35 = bf16[384,2048]{1,0:T(8,128)(2,1)S(1)} collective-permute-done((bf16[384,2048]{1,0:T(8,128)(2,1)S(1)}, bf16[384,2048]{1,0:T(8,128)(2,1)S(1)}, u32[]{:S(2)}, u32[]{:S(2)}) %collective-permute-start.35) | collective-permute-done | bytes 1572896 | tf_op jit(solution)/shard_map/gather_dz/ppermute | solution.py:58
  463.3 85.9 %expert.2 = (bf16[2048,2048]{1,0:T(8,128)(2,1)}, bf16[2048,2048]{1,0:T(8,128)(2,1)}, bf16[2048,1024]{1,0:T(8,128)(2,1)}, bf16[2048,2048]{1,0:T(8,128)(2,1)}, bf1...) custom-call(s32[8,1,384]{2,1,0:T(1,128)} %get-tuple-element.325.rank, ...), custom_call_target="tpu_custom_call" | custom-call | flops 1000 | bytes 1000 | tf_op jit(solution)/shard_map/expert0/expert/pallas_call | solution.py:478
  549.2 38.3 %expert_weight_grad.2 = bf16[2048,3072]{1,0:T(8,128)(2,1)} custom-call(bf16[2048,2048]{1,0:T(8,128)(2,1)} %get-tuple-element.102.xg_ref, bf16[2048,2048]{1,0:T(8,128)(2,1)} %get-tuple-element.103.dy_ref, bf16[2048,2048]{1,0:T(8,128)(2,1)} %get-tuple-element.104.dgu_ref, bf16[2048,1024]{1,0:T(8,128)(2,1)} %get-tuple-element.105.hm_ref), custom_call_target="tpu_custom_call" | custom-call | flops 1000 | bytes 1000 | tf_op jit(solution)/shard_map/expert0/expert_weight_grad/pallas_call | solution.py:513
  589.0 20.7 %all-gather.8.cloned.1.call-done = bf16[1,2048,3072]{2,1,0:T(8,128)(2,1)} async-done(((bf16[1,512,3072]{2,1,0:T(8,128)(2,1)}), bf16[1,2048,3072]{2,1,0:T(8,128)(2,1)}) %all-gather.8.cloned.1.call-update) | async-done | bytes 12582928 | tf_op jit(solution)/shard_map/gather_experts/all_gather | solution.py:648
  609.7 87.7 %expert.3 = (bf16[2048,2048]{1,0:T(8,128)(2,1)}, bf16[2048,2048]{1,0:T(8,128)(2,1)}, bf16[2048,1024]{1,0:T(8,128)(2,1)}, bf16[2048,2048]{1,0:T(8,128)(2,1)}, bf1...) custom-call(s32[8,1,384]{2,1,0:T(1,128)} %get-tuple-element.326.rank, ...), custom_call_target="tpu_custom_call" | custom-call | flops 1000 | bytes 1000 | tf_op jit(solution)/shard_map/expert1/expert/pallas_call | solution.py:478
  726.3 38.2 %expert_weight_grad.3 = (bf16[2048,2048]{1,0:T(8,128)(2,1)}, bf16[2048,1024]{1,0:T(8,128)(2,1)}) custom-call(bf16[2048,2048]{1,0:T(8,128)(2,1)} %get-tuple-element.118.xg_ref, bf16[2048,2048]{1,0:T(8,128)(2,1)} %get-tuple-element.119.dy_ref, bf16[2048,2048]{1,0:T(8,128)(2,1)} %get-tuple-element.120.dgu_ref, bf16[2048,1024]{1,0:T(8,128)(2,1)} %get-tuple-element.121.hm_ref), custom_call_target="tpu_custom_call" | custom-call | flops 1000 | bytes 1000 | tf_op jit(solution)/shard_map/expert1/expert_weight_grad/pallas_call | solution.py:513
  773.4 15.3 %collective-permute-done.52 = bf16[192,2048]{1,0:T(8,128)(2,1)} collective-permute-done((bf16[192,2048]{1,0:T(8,128)(2,1)}, bf16[192,2048]{1,0:T(8,128)(2,1)}, u32[]{:S(2)}, u32[]{:S(2)}) %collective-permute-start.52) | collective-permute-done | bytes 786464 | tf_op jit(solution)/shard_map/scatter_dxn/ppermute | solution.py:58
  810.2 20.4 %all-to-all-done.5 = bf16[8,384,256]{2,1,0:T(8,128)(2,1)} async-done(((bf16[8,384,256]{2,1,0:T(8,128)(2,1)}), bf16[8,384,256]{2,1,0:T(8,128)(2,1)}, u32[]{:S(2)}, u32[]{:S(2)}) %all-to-all-start.5) | async-done | bytes 1572896 | tf_op jit(solution)/shard_map/do_exchange/all_to_all | solution.py:727
  843.9 41.0 %attend_back.1 = (bf16[2,1536,256]{2,1,0:T(8,128)(2,1)}, bf16[2,1536,256]{2,1,0:T(8,128)(2,1)}, bf16[2,1536,256]{2,1,0:T(8,128)(2,1)}) custom-call(bf16[2,1536,256]{2,1,0:T(8,128)(2,1)} %bitcast.442, bf16[2,1536,256]{2,1,0:T(8,128)(2,1)} %bitcast.444, bf16[2,1536,256]{2,1,0:T(8,128)(2,1)} %bitcast.446, bf16[2,1536,256]{2,1,0:T(8,128)(2,1)} %bitcast.438, ...), custom_call_target="tpu_custom_call" | custom-call | flops 40000000000 | bytes 1000 | tf_op jit(solution)/shard_map/attend_back/pallas_call | solution.py:300
  891.6 28.3 %project_back.1 = (bf16[3072,768]{1,0:T(8,128)(2,1)}, f32[8,128]{1,0:T(8,128)}, bf16[4,8,48,2048]{3,2,1,0:T(8,128)(2,1)}, bf16[4,8,48,2048]{3,2,1,0:T(8,128)(2,1)}) custom-call(bf16[3072,256]{1,0:T(8,128)(2,1)} %bitcast.457, bf16[3072,256]{1,0:T(8,128)(2,1)} %bitcast.458, bf16[3072,256]{1,0:T(8,128)(2,1)} %bitcast.459, ...), custom_call_target="tpu_custom_call" | custom-call | flops 28000000000 | bytes 1000 | tf_op jit(solution)/shard_map/project_back/pallas_call | solution.py:354
  943.0 15.8 %convolution_convert_fusion.1 = bf16[2048,768]{1,0:T(8,128)(2,1)} fusion(bf16[3072,2048]{1,0:T(8,128)(2,1)} %get-tuple-element.147, bf16[3072,768]{1,0:T(8,128)(2,1)} %get-tuple-element.142), kind=kOutput, calls=%fused_computation.20 | convolution fusion | flops 9665249280 | bytes 20447232 | tf_op jit(solution)/shard_map/weight_grads/dot_general | solution.py:42
  959.1 17.3 %adam_expert.3 = (f32[2,512,3072]{2,1,0:T(8,128)}, f32[2,512,3072]{2,1,0:T(8,128)}, f32[2,512,3072]{2,1,0:T(8,128)}) custom-call(bf16[2,512,3072]{2,1,0:T(8,128)(2,1)} %w_ref.5, bf16[512,3072]{1,0:T(8,128)(2,1)} %reduce-scatter.5.cloned.1.call-done.g_ref, f32[2,512,3072]{2,1,0:T(8,128)} %m_ref.5, f32[2,512,3072]{2,1,0:T(8,128)} %v_ref.5), custom_call_target="tpu_custom_call" | custom-call | flops 1000 | bytes 1000 | tf_op jit(solution)/shard_map/weight_grads/adam_expert/pallas_call | solution.py:535
  1051.8 12.3 %adam_expert.4 = (f32[2,512,3072]{2,1,0:T(8,128)}, f32[2,512,3072]{2,1,0:T(8,128)}, f32[2,512,3072]{2,1,0:T(8,128)}) custom-call(bf16[2,512,3072]{2,1,0:T(8,128)(2,1)} %w_ref.5, bf16[512,2048]{1,0:T(8,128)(2,1)} %reduce-scatter.9.cloned.1.call-done.g_ref, f32[2,512,3072]{2,1,0:T(8,128)} %m_ref.5, ...), custom_call_target="tpu_custom_call", output_to_operand_aliasing={{0}: (4, {}), {1}: (5, {}), {2}: (6, {})} | custom-call | flops 1000 | bytes 1000 | tf_op jit(solution)/shard_map/adam_expert/pallas_call | solution.py:535
  1092.3 26.8 %all-to-all-done.7 = bf16[4,96,2048]{2,1,0:T(8,128)(2,1)S(1)} async-done(((bf16[4,96,2048]{2,1,0:T(8,128)(2,1)}), bf16[4,96,2048]{2,1,0:T(8,128)(2,1)S(1)}, u32[]{:S(2)}, u32[]{:S(2)}) %all-to-all-start.7) | async-done | bytes 1572896 | tf_op jit(solution)/shard_map/remap_grad/all_to_all | solution.py:156
  1160.3 19.1 %collective-permute-done.79 = bf16[64,2048]{1,0:T(8,128)(2,1)} collective-permute-done((bf16[64,2048]{1,0:T(8,128)(2,1)}, bf16[64,2048]{1,0:T(8,128)(2,1)}, u32[]{:S(2)}, u32[]{:S(2)}) %collective-permute-start.79) | collective-permute-done | bytes 262176 | tf_op jit(solution)/shard_map/scatter_wo/ppermute | solution.py:58
  (602 shorter events, 523.6 us)
Async XLA Ops:
  7.2 224.5 %all-gather.6.cloned.1.call-start = ((), (), s32[]{:S(2)}) async-start(), calls=%async_computation.13 | async-start | bytes 3932160 | tf_op jit(solution)/shard_map/gather_wqkv/all_gather | solution.py:609
  29.7 433.6 %all-gather.10.cloned.1.call-start = ((), (), s32[]{:S(2)}) async-start(), calls=%async_computation.19 | async-start | bytes 15728640 | tf_op jit(solution)/shard_map/gather_experts/all_gather | solution.py:648
  82.1 66.1 %all-to-all-start.1 = ((bf16[4,96,2048]{2,1,0:T(8,128)(2,1)}), bf16[4,96,2048]{2,1,0:T(8,128)(2,1)S(1)}, u32[]{:S(2)}, u32[]{:S(2)}) async-start(bf16[4,96,2048]{2,1,0:T(8,128)(2,1)} %bitcast.2), calls=%async_computation.1 | async-start | bytes 3145728 | tf_op jit(solution)/shard_map/remap_x/all_to_all | solution.py:146
  101.8 508.0 %all-gather.8.cloned.1.call-start = ((), (), s32[]{:S(2)}) async-start(), calls=%async_computation.18 | async-start | bytes 15728640 | tf_op jit(solution)/shard_map/gather_experts/all_gather | solution.py:648
  148.3 47.1 %collective-permute-start.1 = (bf16[384,2048]{1,0:T(8,128)(2,1)S(1)}, bf16[384,2048]{1,0:T(8,128)(2,1)}, u32[]{:S(2)}, u32[]{:S(2)}) collective-permute-start(bf16[384,2048]{1,0:T(8,128)(2,1)S(1)} %bitcast.373), channel_id=1, source_target_pairs={{0,2},{1,3},{2,0},{3,1},{4,6},{5,7},{6,4},{7,5},{8,10},{9,11},{10,... | collective-permute-start | bytes 4718600 | tf_op jit(solution)/shard_map/gather_x/ppermute | solution.py:58
  152.0 47.7 %collective-permute-start.3 = (bf16[384,2048]{1,0:T(8,128)(2,1)S(1)}, bf16[384,2048]{1,0:T(8,128)(2,1)}, u32[]{:S(2)}, u32[]{:S(2)}) collective-permute-start(bf16[384,2048]{1,0:T(8,128)(2,1)S(1)} %bitcast.374), channel_id=1, source_target_pairs={{0,4},{1,5},{2,6},{3,7},{4,0},{5,1},{6,2},{7,3},{8,12},{9,13},{10,... | collective-permute-start | bytes 4718600 | tf_op jit(solution)/shard_map/gather_x/ppermute | solution.py:58
  152.8 67.9 %collective-permute-start = (bf16[384,2048]{1,0:T(8,128)(2,1)S(1)}, bf16[384,2048]{1,0:T(8,128)(2,1)}, u32[]{:S(2)}, u32[]{:S(2)}) collective-permute-start(bf16[384,2048]{1,0:T(8,128)(2,1)S(1)} %bitcast.375), channel_id=1, source_target_pairs={{0,1},{1,0},{2,3},{3,2},{4,5},{5,4},{6,7},{7,6},{8,9},{9,8},{10,11... | collective-permute-start | bytes 4718600 | tf_op jit(solution)/shard_map/gather_x/ppermute | solution.py:58
  217.6 67.5 %collective-permute-start.22 = (bf16[256,2048]{1,0:T(8,128)(2,1)}, bf16[256,2048]{1,0:T(8,128)(2,1)}, u32[]{:S(2)}, u32[]{:S(2)}) collective-permute-start(bf16[256,2048]{1,0:T(8,128)(2,1)} %collective-permute-done.21), channel_id=1, source_target_pairs={{0,1},{1,0},{2,3},{3,2},{4,5},{5,4},{6,7},{7,6},{8,9},{9,8},{10,11... | collective-permute-start | bytes 3145736 | tf_op jit(solution)/shard_map/gather_wo/ppermute | solution.py:58
  220.7 69.1 %collective-permute-start.25 = (bf16[256,2048]{1,0:T(8,128)(2,1)}, bf16[256,2048]{1,0:T(8,128)(2,1)}, u32[]{:S(2)}, u32[]{:S(2)}) collective-permute-start(bf16[256,2048]{1,0:T(8,128)(2,1)} %constant_dynamic-update-slice_fusion.18), channel_id=1, source_target_pairs={{0,1},{1,0},{2,3},{3,2},{4,5},{5,4},{6,7},{7,6},{8,9},{9,8},{10,11... | collective-permute-start | bytes 3145736 | tf_op jit(solution)/shard_map/gather_wo/ppermute | solution.py:58
  321.5 42.7 %collective-permute-start.27 = (bf16[384,2048]{1,0:T(8,128)(2,1)}, bf16[384,2048]{1,0:T(8,128)(2,1)}, u32[]{:S(2)}, u32[]{:S(2)}) collective-permute-start(bf16[384,2048]{1,0:T(8,128)(2,1)} %multiply_convert_fusion), channel_id=1, source_target_pairs={{0,2},{1,3},{2,0},{3,1},{4,6},{5,7},{6,4},{7,5},{8,10},{9,11},{10,... | collective-permute-start | bytes 4718600 | tf_op jit(solution)/shard_map/gather_xn/ppermute | solution.py:58
  331.9 62.4 %all-to-all-start.3 = ((bf16[4,96,2048]{2,1,0:T(8,128)(2,1)}), bf16[4,96,2048]{2,1,0:T(8,128)(2,1)}, u32[]{:S(2)}, u32[]{:S(2)}) async-start(bf16[4,96,2048]{2,1,0:T(8,128)(2,1)} %bitcast.17), calls=%async_computation.3 | async-start | bytes 3145728 | tf_op jit(solution)/shard_map/remap_dz/all_to_all | solution.py:146
  336.2 507.7 %reduce-scatter.5.cloned.1.call-start = ((), (), s32[]{:S(2)}) async-start(), calls=%async_computation.14 | async-start | bytes 15728640 | tf_op jit(solution)/shard_map/expert0/reduce_scatter | solution.py:710
  337.3 46.4 %collective-permute-start.26 = (bf16[384,2048]{1,0:T(8,128)(2,1)}, bf16[384,2048]{1,0:T(8,128)(2,1)}, u32[]{:S(2)}, u32[]{:S(2)}) collective-permute-start(bf16[384,2048]{1,0:T(8,128)(2,1)} %multiply_convert_fusion), channel_id=1, source_target_pairs={{0,1},{1,0},{2,3},{3,2},{4,5},{5,4},{6,7},{7,6},{8,9},{9,8},{10,11... | collective-permute-start | bytes 4718600 | tf_op jit(solution)/shard_map/gather_xn/ppermute | solution.py:58
  404.6 50.0 %collective-permute-start.34 = (bf16[384,2048]{1,0:T(8,128)(2,1)S(1)}, bf16[384,2048]{1,0:T(8,128)(2,1)}, u32[]{:S(2)}, u32[]{:S(2)}) collective-permute-start(bf16[384,2048]{1,0:T(8,128)(2,1)S(1)} %bitcast.384), channel_id=1, source_target_pairs={{0,1},{1,0},{2,3},{3,2},{4,5},{5,4},{6,7},{7,6},{8,9},{9,8},{10,11... | collective-permute-start | bytes 4718600 | tf_op jit(solution)/shard_map/gather_dz/ppermute | solution.py:58
  717.6 46.9 %collective-permute-start.50 = (bf16[2,192,2048]{2,1,0:T(8,128)(2,1)}, bf16[2,192,2048]{2,1,0:T(8,128)(2,1)}, u32[]{:S(2)}, u32[]{:S(2)}) collective-permute-start(bf16[2,192,2048]{2,1,0:T(8,128)(2,1)} %get-tuple-element.115), channel_id=1, source_target_pairs={{0,2},{1,3},{2,0},{3,1},{4,6},{5,7},{6,4},{7,5},{8,10},{9,11},{10,... | collective-permute-start | bytes 4718600 | tf_op jit(solution)/shard_map/scatter_dxn/ppermute | solution.py:58
  719.1 45.4 %collective-permute-start.51 = (bf16[2,192,2048]{2,1,0:T(8,128)(2,1)}, bf16[2,192,2048]{2,1,0:T(8,128)(2,1)}, u32[]{:S(2)}, u32[]{:S(2)}) collective-permute-start(bf16[2,192,2048]{2,1,0:T(8,128)(2,1)} %get-tuple-element.116), channel_id=1, source_target_pairs={{0,4},{1,5},{2,6},{3,7},{4,0},{5,1},{6,2},{7,3},{8,12},{9,13},{10,... | collective-permute-start | bytes 4718600 | tf_op jit(solution)/shard_map/scatter_dxn/ppermute | solution.py:58
  809.6 242.2 %reduce-scatter.9.cloned.1.call-start = ((), (), s32[]{:S(2)}) async-start(), calls=%async_computation.16 | async-start | bytes 10485760 | tf_op jit(solution)/shard_map/reduce_scatter | solution.py:711
  843.1 41.8 %collective-permute-start.55 = (bf16[2,192,2048]{2,1,0:T(8,128)(2,1)}, bf16[2,192,2048]{2,1,0:T(8,128)(2,1)}, u32[]{:S(2)}, u32[]{:S(2)}) collective-permute-start(bf16[2,192,2048]{2,1,0:T(8,128)(2,1)} %get-tuple-element.129), channel_id=1, source_target_pairs={{0,2},{1,3},{2,0},{3,1},{4,6},{5,7},{6,4},{7,5},{8,10},{9,11},{10,... | collective-permute-start | bytes 4718600 | tf_op jit(solution)/shard_map/scatter_out/ppermute | solution.py:58
  843.2 41.7 %collective-permute-start.56 = (bf16[2,192,2048]{2,1,0:T(8,128)(2,1)}, bf16[2,192,2048]{2,1,0:T(8,128)(2,1)}, u32[]{:S(2)}, u32[]{:S(2)}) collective-permute-start(bf16[2,192,2048]{2,1,0:T(8,128)(2,1)} %get-tuple-element.130), channel_id=1, source_target_pairs={{0,4},{1,5},{2,6},{3,7},{4,0},{5,1},{6,2},{7,3},{8,12},{9,13},{10,... | collective-permute-start | bytes 4718600 | tf_op jit(solution)/shard_map/scatter_out/ppermute | solution.py:58
  929.2 76.8 %all-to-all-start.6 = ((bf16[4,96,2048]{2,1,0:T(8,128)(2,1)}), bf16[4,96,2048]{2,1,0:T(8,128)(2,1)S(1)}, u32[]{:S(2)}, u32[]{:S(2)}) async-start(bf16[4,96,2048]{2,1,0:T(8,128)(2,1)} %bitcast.140), calls=%async_computation.7 | async-start | bytes 3145728 | tf_op jit(solution)/shard_map/remap_out/all_to_all | solution.py:156
  932.8 154.7 %reduce-scatter.7.cloned.1.call-start = ((), (), s32[]{:S(2)}) async-start(), calls=%async_computation.15 | async-start | bytes 3932160 | tf_op jit(solution)/shard_map/weight_grads/reduce_scatter | solution.py:751
  958.8 228.3 %reduce-scatter.11.cloned.1.call-start = ((), (), s32[]{:S(2)}) async-start(), calls=%async_computation.17 | async-start | bytes 5242880 | tf_op jit(solution)/shard_map/reduce_scatter | solution.py:759
  1047.9 71.1 %all-to-all-start.7 = ((bf16[4,96,2048]{2,1,0:T(8,128)(2,1)}), bf16[4,96,2048]{2,1,0:T(8,128)(2,1)S(1)}, u32[]{:S(2)}, u32[]{:S(2)}) async-start(bf16[4,96,2048]{2,1,0:T(8,128)(2,1)} %bitcast.146), calls=%async_computation.8 | async-start | bytes 3145728 | tf_op jit(solution)/shard_map/remap_grad/all_to_all | solution.py:156
  1148.3 45.0 %all-to-all-start.8 = ((bf16[8,48,4096]{2,1,0:T(8,128)(2,1)}), bf16[8,48,4096]{2,1,0:T(8,128)(2,1)S(1)}, u32[]{:S(2)}, u32[]{:S(2)}) async-start(bf16[8,48,4096]{2,1,0:T(8,128)(2,1)} %bitcast.164), calls=%async_computation.11 | async-start | bytes 6291456 | tf_op jit(solution)/shard_map/remap/all_to_all | solution.py:162
  (149 other events, 2590.0 us)
Sparse Core Ops, SparseCore 0:
  29.8 108.3 all-gather.5
  139.8 252.4 all-gather.9
  393.8 215.8 all-gather.7
  611.9 209.9 reduce-scatter.4
  824.2 170.6 reduce-scatter.8
  997.6 79.9 reduce-scatter.6
  1079.9 101.1 reduce-scatter.10

commit v4 on v3

--- a/solution.py
+++ b/solution.py
@@ -527,8 +527,9 @@
     new = adam_step(w_ref[0], g_ref[...], m_ref[0], v_ref[0], rate)
     m_out[0], v_out[0], w_out[0] = new
 
-def adam_expert(e, base, weight, grad, first, second, old, rate, block=128, wide=1024):
+def adam_part(e, base, weight, grad, first, second, old, rate, block=128, wide=1024):
     rows, cols = grad.shape
+    block = min(block, rows)
     one = pl.BlockSpec((1, block, wide), lambda i, j: (e, i, base // wide + j))
     out = jax.ShapeDtypeStruct(weight.shape, F32)
     old = tuple(old or ())
@@ -542,7 +543,7 @@
         input_output_aliases={4 + i: i for i in range(len(old))},
         compiler_params=pltpu.CompilerParams(vmem_limit_bytes=VMEM_LIMIT),
         cost_estimate=BRIEF,
-        name="adam_expert",
+        name="adam_part",
     )(weight, grad, first, second, *old)
 
 
@@ -601,7 +602,9 @@
     with jax.named_scope("gather_wo"):
         out_part = gather_direct(attn_weight[:, 3 * model :], "seq", seq_count)
     with jax.named_scope("remap_x"):
-        x_low = to_plane_seq(to_plane_fsdp(tokens[0], fsdp_count), seq_count, fsdp_count)
+        x_parts = reorder(tokens[0].reshape(fsdp_count, chunk, model), around)
+        x_parts = reorder(jnp.stack(exchange(list(x_parts), "fsdp", fsdp_count)), around)
+        x_low = to_plane_seq(x_parts, seq_count, fsdp_count)
     with jax.named_scope("gather_wqkv"):
         first_part = attn_weight[:, : 3 * model].reshape(shard, 3, fsdp_count, width).transpose(2, 0, 1, 3)
         first_part = reorder(first_part.reshape(fsdp_count, shard, 3 * width), around)
@@ -753,7 +756,7 @@
         expert_new = None
         for e in range(EXP_DEV - 1):
             share = after(expert_share[e], *da.sends)
-            expert_new = adam_expert(e, 0, expert_weight, share, *moments, expert_new, RATE_EXPERT)
+            expert_new = adam_part(e, 0, expert_weight, share, *moments, expert_new, RATE_EXPERT)
     with jax.named_scope("scatter_da"):
         da = da.second(in_grad, expert_new[0])
     last_down = lax.psum_scatter(after(held[1], *da.lasts), "seq", scatter_dimension=0, tiled=True)
@@ -790,7 +793,7 @@
     with jax.named_scope("scatter_wo"):
         out_grad = Scatter(fsdp_count, out_grad[0], after(out_grad[1], input_low), hold=small_parts)
     last = EXP_DEV - 1
-    expert_new = adam_expert(
+    expert_new = adam_part(
         last, 0, expert_weight, after(last_up, *out_grad.sends), *moments, expert_new, RATE_EXPERT
     )
     with jax.named_scope("scatter_wo"):
@@ -808,16 +811,31 @@
         both = jnp.concatenate([input_grad, layer_out], axis=1)
         both = from_plane_fsdp(after(both, sent), fsdp_count)
         input_grad, layer_out = both[:, :model].astype(F32), both[:, model:]
-    out_share = sum(p.astype(F32) for p in out_parts)
     small_own = sum(exchange(list(lax.optimization_barrier((*small_parts, in_share))[:-1]), "seq", seq_count))
     router_share, gain_share = small_own[:own_router].reshape(shard, experts), small_own[own_router:]
 
-    attn_share = jnp.concatenate([in_share.astype(F32), out_share], axis=1)
-    attn_new = adam_step(attn_weight, attn_share, attn_first, attn_second, RATE_ATTN)
+    attn_states = [v[None] for v in (attn_weight, attn_first, attn_second)]
+    attn_new = adam_part(0, 0, attn_states[0], in_share, *attn_states[1:], None, RATE_ATTN, wide=2048)
     router_new = adam_step(router_weight, router_share, router_first, router_second, RATE_ROUTER)
-    expert_new = adam_expert(
-        last, 2 * FFE, expert_weight, after(last_down, attn_new[0]), *moments, expert_new, RATE_EXPERT
-    )
+    last_down, input_grad, layer_out, _ = lax.optimization_barrier(
+        (last_down, input_grad, layer_out, attn_new[0])
+    )
+    expert_new = adam_part(
+        last,
+        2 * FFE,
+        expert_weight,
+        last_down,
+        *moments,
+        expert_new,
+        RATE_EXPERT,
+        block=256,
+    )
+    out_parts = lax.optimization_barrier((*out_parts, expert_new[0]))[:-1]
+    out_share = sum(p.astype(F32) for p in out_parts)
+    attn_new = adam_part(
+        0, 3 * model, attn_states[0], out_share, *attn_states[1:], attn_new, RATE_ATTN
+    )
+    attn_new = [v[0] for v in attn_new]
     gain_new = adam_step(gain_values, gain_share, gain_first, gain_second, RATE_GAIN)
     return (layer_out[None], input_grad[None], *attn_new, *router_new, *gain_new, *expert_new)
 

time: 1220 us -> 1210 us (level)
    ppermute x85 -> x92, waiting for transfers between devices: 175 us -> 204 us  [swap(): return lax.ppermute(value, axis, [(i, i ^ step) for i in range(count)])]
    all_to_all x2, waiting for transfers between devices: 26.8 us -> 12.6 us  [from_plane_seq(): lax.all_to_all(value, 'seq', split_axis=0, concat_axis=0, tiled=True)]
    ppermute x85 -> x92, starting transfers between devices: 76.4 us -> 85.1 us  [swap(): return lax.ppermute(value, axis, [(i, i ^ step) for i in range(count)])]
    pallas_call x3 -> x5, Pallas kernels: 35.9 us -> 43 us  [adam_part(): pl.pallas_call(functools.partial(adam_kernel, rate), grid=(rows // block,...]
    unnamed x200 -> x190, local copies, waits for them, and re-layouts: 62.6 us -> 55.8 us
    gather x13 -> x15, local copies, waits for them, and re-layouts: 38.6 us -> 37.9 us  [reorder(): return jnp.take(stacked, index, axis=axis, mode='clip')]
  transfers between devices with their start and end apart: 101 -> 107, of which waited for: 36 -> 41; matrix products, arithmetic and copies ran while one was open for 26% -> 24% of each run, Pallas kernels for 33% -> 34%
where the time goes in v4:
time: 1210 us; the launch traced here: 1200 us
  Pallas kernels  406 us (34%)
  waiting for transfers between devices  303 us (25%)
  local copies, waits for them, and re-layouts  171 us (14%)
  starting transfers between devices  127 us (10%)
  other arithmetic  88.3 us (7%)
  matrix products  45.5 us (4%)
  blocking collectives  40.5 us (3%)
  between operations  18.9 us (2%)
    ppermute x92, waiting for transfers between devices, swap(): return lax.ppermute(value, axis, [(i, i ^ step) for i in range(count)])  204 us
    pallas_call x2, Pallas kernels, run_expert(): pl.pallas_call(functools.partial(expert_kernel, wide, narrow, more, len(f...  174 us
    ppermute x92, starting transfers between devices, swap(): return lax.ppermute(value, axis, [(i, i ^ step) for i in range(count)])  85.1 us
    pallas_call x2, Pallas kernels, expert_weight_grad(): pl.pallas_call(functools.partial(weight_kernel, narrow), grid=(model // b...  76.6 us
    unnamed x190, local copies, waits for them, and re-layouts  55.8 us
    dot_general x7, matrix products, dot(): lax.dot_general(a, b, (((ca,), (cb,)), ((), ())), preferred_element_type=...  45.5 us
    pallas_call x5, Pallas kernels, adam_part(): pl.pallas_call(functools.partial(adam_kernel, rate), grid=(rows // block,...  43 us
    pallas_call x1, Pallas kernels, attend_back(): pl.pallas_call(functools.partial(attend_back_kernel, 256), grid=(seqs, wi...  41 us
  transfers between devices with their start and end apart: 107, of which 41 were waited for; matrix products, arithmetic and copies ran while one was open for 24% of the time, Pallas kernels for 34%

profile of v4, /device:TPU:0, one launch (start us, length us, event | category | flops | bytes accessed | tf_op | source)
XLA Modules:
  0.0 1200.4 jit_solution(9790832021618239510)
XLA Ops:
  92.2 12.5 %all-to-all-start = ((bf16[4,96,2048]{2,1,0:T(8,128)(2,1)}), bf16[4,96,2048]{2,1,0:T(8,128)(2,1)S(1)}, u32[]{:S(2)}, u32[]{:S(2)}) async-start(bf16[4,96,2048]{2,1,0:T(8,128)(2,1)} %bitcast.17), calls=%async_computation | async-start | bytes 3145728 | tf_op jit(solution)/shard_map/remap_x/all_to_all | solution.py:146
  129.3 19.6 %all-to-all-done = bf16[4,96,2048]{2,1,0:T(8,128)(2,1)S(1)} async-done(((bf16[4,96,2048]{2,1,0:T(8,128)(2,1)}), bf16[4,96,2048]{2,1,0:T(8,128)(2,1)S(1)}, u32[]{:S(2)}, u32[]{:S(2)}) %all-to-all-start) | async-done | bytes 1572896 | tf_op jit(solution)/shard_map/remap_x/all_to_all | solution.py:146
  153.6 20.4 %all_gather.15 = f32[160,128]{1,0:T(8,128)S(1)} all-gather(f32[40,128]{1,0:T(8,128)S(1)} %pad_bitcast_fusion), channel_id=1, replica_groups=mesh['seq'=4,'fsdp'=8] {'seq'}, dimensions={0}, use_global_device_ids=true | all-gather | bytes 102400 | tf_op jit(solution)/shard_map/gather_small/all_gather | solution.py:620
  174.0 20.0 %all_gather.16 = f32[1280,128]{1,0:T(8,128)S(1)} all-gather(f32[160,128]{1,0:T(8,128)S(1)} %all_gather.15), channel_id=1, replica_groups=mesh['seq'=4,'fsdp'=8] {'fsdp'}, dimensions={0}, use_global_device_ids=true | all-gather | bytes 737280 | tf_op jit(solution)/shard_map/gather_small/all_gather | solution.py:621
  204.6 13.7 %collective-permute-done.12 = bf16[192,2048]{1,0:T(8,128)(2,1)} collective-permute-done((bf16[192,2048]{1,0:T(8,128)(2,1)}, bf16[192,2048]{1,0:T(8,128)(2,1)}, u32[]{:S(2)}, u32[]{:S(2)}) %collective-permute-start.12) | collective-permute-done | bytes 786464 | tf_op jit(solution)/shard_map/gather_x/ppermute | solution.py:58
  234.9 20.9 %project.1 = (bf16[3072,2048]{1,0:T(8,128)(2,1)}, bf16[3072,256]{1,0:T(8,128)(2,1)}, bf16[3072,256]{1,0:T(8,128)(2,1)}, bf16[3072,256]{1,0:T(8,128)(2,1)}, f32[3072,256]{1,0:T(8,128)}, /*index=5*/f32[3072,256]{1,0:T(8,128)}) custom-call(bf16[3072,2048]{1,0:T(8,128)(2,1)} %bitcast.392, f32[1,2048]{1,0:T(1,128)} %bitcast.491, ...), custom_call_target="tpu_custom_call" | custom-call | flops 1000 | bytes 1000 | tf_op jit(solution)/shard_map/project/pallas_call | solution.py:203
  255.8 23.0 %attend.1 = bf16[2,1536,256]{2,1,0:T(8,128)(2,1)} custom-call(bf16[2,1536,256]{2,1,0:T(8,128)(2,1)} %bitcast.481, bf16[2,1536,256]{2,1,0:T(8,128)(2,1)} %bitcast.483, bf16[2,1536,256]{2,1,0:T(8,128)(2,1)} %bitcast.485, s32[2,1536,1]{2,1,0:T(8,128)} %convert_add_fusion.1.rd_ref, s32[2,1,1536]{2,1,0:T(1,128)} %fusion.32.cd_ref), custom_call_target="tpu_custom_call" | custom-call | flops 1000 | bytes 1000 | tf_op jit(solution)/shard_map/attend/pallas_call | solution.py:283
  346.8 17.9 %collective-permute-done.34 = bf16[384,2048]{1,0:T(8,128)(2,1)} collective-permute-done((bf16[384,2048]{1,0:T(8,128)(2,1)S(1)}, bf16[384,2048]{1,0:T(8,128)(2,1)}, u32[]{:S(2)}, u32[]{:S(2)}) %collective-permute-start.34) | collective-permute-done | bytes 1572896 | tf_op jit(solution)/shard_map/gather_xn/ppermute | solution.py:58
  413.7 16.5 %collective-permute-done.44 = bf16[384,2048]{1,0:T(8,128)(2,1)S(1)} collective-permute-done((bf16[384,2048]{1,0:T(8,128)(2,1)S(1)}, bf16[384,2048]{1,0:T(8,128)(2,1)S(1)}, u32[]{:S(2)}, u32[]{:S(2)}) %collective-permute-start.44) | collective-permute-done | bytes 1572896 | tf_op jit(solution)/shard_map/gather_dz/ppermute | solution.py:58
  462.7 86.0 %expert.2 = (bf16[2048,2048]{1,0:T(8,128)(2,1)}, bf16[2048,2048]{1,0:T(8,128)(2,1)}, bf16[2048,1024]{1,0:T(8,128)(2,1)}, bf16[2048,2048]{1,0:T(8,128)(2,1)}, bf1...) custom-call(s32[8,1,384]{2,1,0:T(1,128)} %get-tuple-element.355.rank, ...), custom_call_target="tpu_custom_call" | custom-call | flops 1000 | bytes 1000 | tf_op jit(solution)/shard_map/expert0/expert/pallas_call | solution.py:478
  548.7 38.3 %expert_weight_grad.2 = bf16[2048,3072]{1,0:T(8,128)(2,1)} custom-call(bf16[2048,2048]{1,0:T(8,128)(2,1)} %get-tuple-element.114.xg_ref, bf16[2048,2048]{1,0:T(8,128)(2,1)} %get-tuple-element.115.dy_ref, bf16[2048,2048]{1,0:T(8,128)(2,1)} %get-tuple-element.116.dgu_ref, bf16[2048,1024]{1,0:T(8,128)(2,1)} %get-tuple-element.117.hm_ref), custom_call_target="tpu_custom_call" | custom-call | flops 1000 | bytes 1000 | tf_op jit(solution)/shard_map/expert0/expert_weight_grad/pallas_call | solution.py:513
  588.5 17.5 %all-gather.8.cloned.1.call-done = bf16[1,2048,3072]{2,1,0:T(8,128)(2,1)} async-done(((bf16[1,512,3072]{2,1,0:T(8,128)(2,1)}), bf16[1,2048,3072]{2,1,0:T(8,128)(2,1)}) %all-gather.8.cloned.1.call-update) | async-done | bytes 12582928 | tf_op jit(solution)/shard_map/gather_experts/all_gather | solution.py:651
  606.1 87.6 %expert.3 = (bf16[2048,2048]{1,0:T(8,128)(2,1)}, bf16[2048,2048]{1,0:T(8,128)(2,1)}, bf16[2048,1024]{1,0:T(8,128)(2,1)}, bf16[2048,2048]{1,0:T(8,128)(2,1)}, bf1...) custom-call(s32[8,1,384]{2,1,0:T(1,128)} %get-tuple-element.356.rank, ...), custom_call_target="tpu_custom_call" | custom-call | flops 1000 | bytes 1000 | tf_op jit(solution)/shard_map/expert1/expert/pallas_call | solution.py:478
  716.5 38.3 %expert_weight_grad.3 = (bf16[2048,2048]{1,0:T(8,128)(2,1)}, bf16[2048,1024]{1,0:T(8,128)(2,1)}) custom-call(bf16[2048,2048]{1,0:T(8,128)(2,1)} %get-tuple-element.130.xg_ref, bf16[2048,2048]{1,0:T(8,128)(2,1)} %get-tuple-element.131.dy_ref, bf16[2048,2048]{1,0:T(8,128)(2,1)} %get-tuple-element.132.dgu_ref, bf16[2048,1024]{1,0:T(8,128)(2,1)} %get-tuple-element.133.hm_ref), custom_call_target="tpu_custom_call" | custom-call | flops 1000 | bytes 1000 | tf_op jit(solution)/shard_map/expert1/expert_weight_grad/pallas_call | solution.py:513
  763.8 15.0 %collective-permute-done.59 = bf16[192,2048]{1,0:T(8,128)(2,1)S(1)} collective-permute-done((bf16[192,2048]{1,0:T(8,128)(2,1)}, bf16[192,2048]{1,0:T(8,128)(2,1)S(1)}, u32[]{:S(2)}, u32[]{:S(2)}) %collective-permute-start.59) | collective-permute-done | bytes 786464 | tf_op jit(solution)/shard_map/scatter_dxn/ppermute | solution.py:58
  800.9 20.4 %all-to-all-done.4 = bf16[8,384,256]{2,1,0:T(8,128)(2,1)S(1)} async-done(((bf16[8,384,256]{2,1,0:T(8,128)(2,1)}), bf16[8,384,256]{2,1,0:T(8,128)(2,1)S(1)}, u32[]{:S(2)}, u32[]{:S(2)}) %all-to-all-start.4) | async-done | bytes 1572896 | tf_op jit(solution)/shard_map/do_exchange/all_to_all | solution.py:730
  830.5 41.0 %attend_back.1 = (bf16[2,1536,256]{2,1,0:T(8,128)(2,1)}, bf16[2,1536,256]{2,1,0:T(8,128)(2,1)}, bf16[2,1536,256]{2,1,0:T(8,128)(2,1)}) custom-call(bf16[2,1536,256]{2,1,0:T(8,128)(2,1)} %bitcast.482, bf16[2,1536,256]{2,1,0:T(8,128)(2,1)} %bitcast.484, bf16[2,1536,256]{2,1,0:T(8,128)(2,1)} %bitcast.486, bf16[2,1536,256]{2,1,0:T(8,128)(2,1)} %bitcast.478, ...), custom_call_target="tpu_custom_call" | custom-call | flops 40000000000 | bytes 1000 | tf_op jit(solution)/shard_map/attend_back/pallas_call | solution.py:300
  877.2 28.3 %project_back.1 = (bf16[3072,768]{1,0:T(8,128)(2,1)}, f32[8,128]{1,0:T(8,128)}, bf16[4,8,48,2048]{3,2,1,0:T(8,128)(2,1)}, bf16[4,8,48,2048]{3,2,1,0:T(8,128)(2,1)}) custom-call(bf16[3072,256]{1,0:T(8,128)(2,1)} %bitcast.495, bf16[3072,256]{1,0:T(8,128)(2,1)} %bitcast.496, bf16[3072,256]{1,0:T(8,128)(2,1)} %bitcast.497, ...), custom_call_target="tpu_custom_call" | custom-call | flops 28000000000 | bytes 1000 | tf_op jit(solution)/shard_map/project_back/pallas_call | solution.py:354
  927.2 15.7 %convolution_convert_fusion.1 = bf16[2048,768]{1,0:T(8,128)(2,1)} fusion(bf16[3072,2048]{1,0:T(8,128)(2,1)} %get-tuple-element.159, bf16[3072,768]{1,0:T(8,128)(2,1)} %get-tuple-element.154), kind=kOutput, calls=%fused_computation.22 | convolution fusion | flops 9665249280 | bytes 20447232 | tf_op jit(solution)/shard_map/weight_grads/dot_general | solution.py:42
  943.2 17.4 %adam_part.5 = (f32[2,512,3072]{2,1,0:T(8,128)}, f32[2,512,3072]{2,1,0:T(8,128)}, f32[2,512,3072]{2,1,0:T(8,128)}) custom-call(bf16[2,512,3072]{2,1,0:T(8,128)(2,1)} %w_ref.5, bf16[512,3072]{1,0:T(8,128)(2,1)} %reduce-scatter.5.cloned.1.call-done.g_ref, f32[2,512,3072]{2,1,0:T(8,128)} %m_ref.5, f32[2,512,3072]{2,1,0:T(8,128)} %v_ref.5), custom_call_target="tpu_custom_call" | custom-call | flops 1000 | bytes 1000 | tf_op jit(solution)/shard_map/weight_grads/adam_part/pallas_call | solution.py:536
  1038.8 12.3 %adam_part.6 = (f32[2,512,3072]{2,1,0:T(8,128)}, f32[2,512,3072]{2,1,0:T(8,128)}, f32[2,512,3072]{2,1,0:T(8,128)}) custom-call(bf16[2,512,3072]{2,1,0:T(8,128)(2,1)} %w_ref.5, bf16[512,2048]{1,0:T(8,128)(2,1)} %reduce-scatter.11.cloned.1.call-done.g_ref, f32[2,512,3072]{2,1,0:T(8,128)} %m_ref.5, ...), custom_call_target="tpu_custom_call", output_to_operand_aliasing={{0}: (4, {}), {1}: (5, {}), {2}: (6, {})} | custom-call | flops 1000 | bytes 1000 | tf_op jit(solution)/shard_map/adam_part/pallas_call | solution.py:536
  1084.0 10.5 all-to-all-done.6
  1108.4 36.0 %collective-permute-done.80 = bf16[64,768]{1,0:T(8,128)(2,1)S(1)} collective-permute-done((bf16[64,768]{1,0:T(8,128)(2,1)S(1)}, bf16[64,768]{1,0:T(8,128)(2,1)S(1)}, u32[]{:S(2)}, u32[]{:S(2)}) %collective-permute-start.80) | collective-permute-done | bytes 98336 | tf_op jit(solution)/shard_map/scatter_wqkv/ppermute | solution.py:58
  1178.4 11.2 collective-permute-done.87
  (608 shorter events, 541.5 us)
Async XLA Ops:
  7.2 225.1 %all-gather.6.cloned.1.call-start = ((), (), s32[]{:S(2)}) async-start(), calls=%async_computation.12 | async-start | bytes 3932160 | tf_op jit(solution)/shard_map/gather_wqkv/all_gather | solution.py:612
  30.1 432.6 %all-gather.10.cloned.1.call-start = ((), (), s32[]{:S(2)}) async-start(), calls=%async_computation.18 | async-start | bytes 15728640 | tf_op jit(solution)/shard_map/gather_experts/all_gather | solution.py:651
  92.2 56.6 %all-to-all-start = ((bf16[4,96,2048]{2,1,0:T(8,128)(2,1)}), bf16[4,96,2048]{2,1,0:T(8,128)(2,1)S(1)}, u32[]{:S(2)}, u32[]{:S(2)}) async-start(bf16[4,96,2048]{2,1,0:T(8,128)(2,1)} %bitcast.17), calls=%async_computation | async-start | bytes 3145728 | tf_op jit(solution)/shard_map/remap_x/all_to_all | solution.py:146
  104.7 501.4 %all-gather.8.cloned.1.call-start = ((), (), s32[]{:S(2)}) async-start(), calls=%async_computation.17 | async-start | bytes 15728640 | tf_op jit(solution)/shard_map/gather_experts/all_gather | solution.py:651
  149.0 47.2 %collective-permute-start.8 = (bf16[384,2048]{1,0:T(8,128)(2,1)S(1)}, bf16[384,2048]{1,0:T(8,128)(2,1)}, u32[]{:S(2)}, u32[]{:S(2)}) collective-permute-start(bf16[384,2048]{1,0:T(8,128)(2,1)S(1)} %bitcast.400), channel_id=1, source_target_pairs={{0,2},{1,3},{2,0},{3,1},{4,6},{5,7},{6,4},{7,5},{8,10},{9,11},{10,... | collective-permute-start | bytes 4718600 | tf_op jit(solution)/shard_map/gather_x/ppermute | solution.py:58
  152.7 47.7 %collective-permute-start.10 = (bf16[384,2048]{1,0:T(8,128)(2,1)S(1)}, bf16[384,2048]{1,0:T(8,128)(2,1)}, u32[]{:S(2)}, u32[]{:S(2)}) collective-permute-start(bf16[384,2048]{1,0:T(8,128)(2,1)S(1)} %bitcast.401), channel_id=1, source_target_pairs={{0,4},{1,5},{2,6},{3,7},{4,0},{5,1},{6,2},{7,3},{8,12},{9,13},{10,... | collective-permute-start | bytes 4718600 | tf_op jit(solution)/shard_map/gather_x/ppermute | solution.py:58
  153.6 67.8 %collective-permute-start.7 = (bf16[384,2048]{1,0:T(8,128)(2,1)S(1)}, bf16[384,2048]{1,0:T(8,128)(2,1)}, u32[]{:S(2)}, u32[]{:S(2)}) collective-permute-start(bf16[384,2048]{1,0:T(8,128)(2,1)S(1)} %bitcast.402), channel_id=1, source_target_pairs={{0,1},{1,0},{2,3},{3,2},{4,5},{5,4},{6,7},{7,6},{8,9},{9,8},{10,11... | collective-permute-start | bytes 4718600 | tf_op jit(solution)/shard_map/gather_x/ppermute | solution.py:58
  218.3 67.3 %collective-permute-start.29 = (bf16[256,2048]{1,0:T(8,128)(2,1)}, bf16[256,2048]{1,0:T(8,128)(2,1)}, u32[]{:S(2)}, u32[]{:S(2)}) collective-permute-start(bf16[256,2048]{1,0:T(8,128)(2,1)} %collective-permute-done.28), channel_id=1, source_target_pairs={{0,1},{1,0},{2,3},{3,2},{4,5},{5,4},{6,7},{7,6},{8,9},{9,8},{10,11... | collective-permute-start | bytes 3145736 | tf_op jit(solution)/shard_map/gather_wo/ppermute | solution.py:58
  221.3 68.9 %collective-permute-start.32 = (bf16[256,2048]{1,0:T(8,128)(2,1)}, bf16[256,2048]{1,0:T(8,128)(2,1)}, u32[]{:S(2)}, u32[]{:S(2)}) collective-permute-start(bf16[256,2048]{1,0:T(8,128)(2,1)} %constant_dynamic-update-slice_fusion.18), channel_id=1, source_target_pairs={{0,1},{1,0},{2,3},{3,2},{4,5},{5,4},{6,7},{7,6},{8,9},{9,8},{10,11... | collective-permute-start | bytes 3145736 | tf_op jit(solution)/shard_map/gather_wo/ppermute | solution.py:58
  321.0 43.7 %collective-permute-start.34 = (bf16[384,2048]{1,0:T(8,128)(2,1)S(1)}, bf16[384,2048]{1,0:T(8,128)(2,1)}, u32[]{:S(2)}, u32[]{:S(2)}) collective-permute-start(bf16[384,2048]{1,0:T(8,128)(2,1)S(1)} %multiply_convert_fusion), channel_id=1, source_target_pairs={{0,2},{1,3},{2,0},{3,1},{4,6},{5,7},{6,4},{7,5},{8,10},{9,11},{10,... | collective-permute-start | bytes 4718600 | tf_op jit(solution)/shard_map/gather_xn/ppermute | solution.py:58
  332.4 59.8 %all-to-all-start.3 = ((bf16[4,96,2048]{2,1,0:T(8,128)(2,1)}), bf16[4,96,2048]{2,1,0:T(8,128)(2,1)S(1)}, u32[]{:S(2)}, u32[]{:S(2)}) async-start(bf16[4,96,2048]{2,1,0:T(8,128)(2,1)} %bitcast.102), calls=%async_computation.3 | async-start | bytes 3145728 | tf_op jit(solution)/shard_map/remap_dz/all_to_all | solution.py:146
  336.2 494.3 %reduce-scatter.5.cloned.1.call-start = ((), (), s32[]{:S(2)}) async-start(), calls=%async_computation.13 | async-start | bytes 15728640 | tf_op jit(solution)/shard_map/expert0/reduce_scatter | solution.py:713
  337.2 44.9 %collective-permute-start.33 = (bf16[384,2048]{1,0:T(8,128)(2,1)S(1)}, bf16[384,2048]{1,0:T(8,128)(2,1)}, u32[]{:S(2)}, u32[]{:S(2)}) collective-permute-start(bf16[384,2048]{1,0:T(8,128)(2,1)S(1)} %multiply_convert_fusion), channel_id=1, source_target_pairs={{0,1},{1,0},{2,3},{3,2},{4,5},{5,4},{6,7},{7,6},{8,9},{9,8},{10,11... | collective-permute-start | bytes 4718600 | tf_op jit(solution)/shard_map/gather_xn/ppermute | solution.py:58
  403.7 50.4 %collective-permute-start.41 = (bf16[384,2048]{1,0:T(8,128)(2,1)S(1)}, bf16[384,2048]{1,0:T(8,128)(2,1)}, u32[]{:S(2)}, u32[]{:S(2)}) collective-permute-start(bf16[384,2048]{1,0:T(8,128)(2,1)S(1)} %bitcast.412), channel_id=1, source_target_pairs={{0,1},{1,0},{2,3},{3,2},{4,5},{5,4},{6,7},{7,6},{8,9},{9,8},{10,11... | collective-permute-start | bytes 4718600 | tf_op jit(solution)/shard_map/gather_dz/ppermute | solution.py:58
  800.3 238.5 %reduce-scatter.11.cloned.1.call-start = ((), (), s32[]{:S(2)}) async-start(), calls=%async_computation.16 | async-start | bytes 10485760 | tf_op jit(solution)/shard_map/reduce_scatter | solution.py:714
  912.0 81.0 %all-to-all-start.5 = ((bf16[4,96,2048]{2,1,0:T(8,128)(2,1)}), bf16[4,96,2048]{2,1,0:T(8,128)(2,1)S(1)}, u32[]{:S(2)}, u32[]{:S(2)}) async-start(bf16[4,96,2048]{2,1,0:T(8,128)(2,1)} %bitcast.154), calls=%async_computation.7 | async-start | bytes 3145728 | tf_op jit(solution)/shard_map/remap_out/all_to_all | solution.py:156
  915.5 163.7 %reduce-scatter.9.cloned.1.call-start = ((), (), s32[]{:S(2)}) async-start(), calls=%async_computation.15 | async-start | bytes 3932160 | tf_op jit(solution)/shard_map/weight_grads/reduce_scatter | solution.py:754
  942.9 230.3 %reduce-scatter.7.cloned.1.call-start = ((), (), s32[]{:S(2)}) async-start(), calls=%async_computation.14 | async-start | bytes 5242880 | tf_op jit(solution)/shard_map/reduce_scatter | solution.py:762
  1033.9 60.6 %all-to-all-start.6 = ((bf16[4,96,2048]{2,1,0:T(8,128)(2,1)}), bf16[4,96,2048]{2,1,0:T(8,128)(2,1)S(1)}, u32[]{:S(2)}, u32[]{:S(2)}) async-start(bf16[4,96,2048]{2,1,0:T(8,128)(2,1)} %bitcast.160), calls=%async_computation.8 | async-start | bytes 3145728 | tf_op jit(solution)/shard_map/remap_grad/all_to_all | solution.py:156
  1096.6 72.1 %all-to-all-start.7 = ((bf16[8,48,4096]{2,1,0:T(8,128)(2,1)}), bf16[8,48,4096]{2,1,0:T(8,128)(2,1)}, u32[]{:S(2)}, u32[]{:S(2)}) async-start(bf16[8,48,4096]{2,1,0:T(8,128)(2,1)} %bitcast.414), calls=%async_computation.11 | async-start | bytes 6291456 | tf_op jit(solution)/shard_map/remap/all_to_all | solution.py:162
  1101.2 48.3 %collective-permute-start.85 = (bf16[64,768]{1,0:T(8,128)(2,1)S(1)}, bf16[64,768]{1,0:T(8,128)(2,1)S(1)}, u32[]{:S(2)}, u32[]{:S(2)}) collective-permute-start(bf16[64,768]{1,0:T(8,128)(2,1)S(1)} %get-tuple-element.326), channel_id=1, source_target_pairs={{0,7},{1,6},{2,5},{3,4},{4,3},{5,2},{6,1},{7,0},{8,15},{9,14},{10,... | collective-permute-start | bytes 294920 | tf_op jit(solution)/shard_map/scatter_wqkv/ppermute | solution.py:58
  1103.7 45.7 %collective-permute-start.84 = (bf16[64,768]{1,0:T(8,128)(2,1)S(1)}, bf16[64,768]{1,0:T(8,128)(2,1)S(1)}, u32[]{:S(2)}, u32[]{:S(2)}) collective-permute-start(bf16[64,768]{1,0:T(8,128)(2,1)S(1)} %get-tuple-element.327), channel_id=1, source_target_pairs={{0,6},{1,7},{2,4},{3,5},{4,2},{5,3},{6,0},{7,1},{8,14},{9,15},{10,... | collective-permute-start | bytes 294920 | tf_op jit(solution)/shard_map/scatter_wqkv/ppermute | solution.py:58
  1104.1 45.4 %collective-permute-start.83 = (bf16[64,768]{1,0:T(8,128)(2,1)S(1)}, bf16[64,768]{1,0:T(8,128)(2,1)S(1)}, u32[]{:S(2)}, u32[]{:S(2)}) collective-permute-start(bf16[64,768]{1,0:T(8,128)(2,1)S(1)} %get-tuple-element.328), channel_id=1, source_target_pairs={{0,5},{1,4},{2,7},{3,6},{4,1},{5,0},{6,3},{7,2},{8,13},{9,12},{10,... | collective-permute-start | bytes 294920 | tf_op jit(solution)/shard_map/scatter_wqkv/ppermute | solution.py:58
  1105.4 44.0 %collective-permute-start.82 = (bf16[64,768]{1,0:T(8,128)(2,1)S(1)}, bf16[64,768]{1,0:T(8,128)(2,1)S(1)}, u32[]{:S(2)}, u32[]{:S(2)}) collective-permute-start(bf16[64,768]{1,0:T(8,128)(2,1)S(1)} %get-tuple-element.329), channel_id=1, source_target_pairs={{0,4},{1,5},{2,6},{3,7},{4,0},{5,1},{6,2},{7,3},{8,12},{9,13},{10,... | collective-permute-start | bytes 294920 | tf_op jit(solution)/shard_map/scatter_wqkv/ppermute | solution.py:58
  (147 other events, 3306.9 us)
Sparse Core Ops, SparseCore 0:
  30.2 108.2 all-gather.5
  140.1 248.4 all-gather.9
  390.1 215.8 all-gather.7
  608.3 210.0 reduce-scatter.4
  820.6 170.5 reduce-scatter.10
  993.9 85.3 reduce-scatter.8
  1081.5 91.1 reduce-scatter.6
